TPU v7x, 32 devices: a whole 2x2x4 slice. The times are simulated.
32 devices in a mesh: dp: 2 (over y), ctx: 16 (over z, x, core).
Axes of the slice: x: 2, y: 2, z: 4, core: 2. Of those that a mesh axis runs over, the one named last changes fastest.
Arguments:
- tokens: bfloat16 [8192, 1024], P(('dp', 'ctx')), may hold values from -6 to 6
- seq_lengths: int32 [2, 4], P('dp'), may hold values from 1 to 2048, 4096 in all within a row
- dealing: int32 [2, 64], P('dp'), may hold values from 0 to 63, as said below
- ln1_gain: bfloat16 [1024], P(('dp', 'ctx')), may hold values from 0.5 to 1.5
- ln1_bias: bfloat16 [1024], P(('dp', 'ctx')), may hold values from -1 to 1
- ln2_gain: bfloat16 [1024], P(('dp', 'ctx')), may hold values from 0.5 to 1.5
- ln2_bias: bfloat16 [1024], P(('dp', 'ctx')), may hold values from -1 to 1
- w_qkv: bfloat16 [1024, 3072], P(('dp', 'ctx')), may hold values from -0.25 to 0.25
- b_qkv: bfloat16 [3072], P(('dp', 'ctx')), may hold values from -1 to 1
- w_out: bfloat16 [1024, 1024], P(('dp', 'ctx')), may hold values from -0.75 to 0.75
- w_in: bfloat16 [1024, 4096], P(('dp', 'ctx')), may hold values from -0.1875 to 0.1875
- b_in: bfloat16 [4096], P(('dp', 'ctx')), may hold values from -2.5 to 2.5
- w_fc2: bfloat16 [4096, 1024], P(('dp', 'ctx')), may hold values from -0.09375 to 0.09375
- b_out: bfloat16 [1024], P(('dp', 'ctx')), may hold values from -1 to 1
- cotangent: bfloat16 [8192, 1024], P(('dp', 'ctx')), may hold values from -6 to 6
Outputs:
- mixed: bfloat16 [8192, 1024], P(('dp', 'ctx'))
- grad_tokens: float32 [8192, 1024], P(('dp', 'ctx'))
- grad_ln1_gain: float32 [1024], P(('dp', 'ctx'))
- grad_ln1_bias: float32 [1024], P(('dp', 'ctx'))
- grad_ln2_gain: float32 [1024], P(('dp', 'ctx'))
- grad_ln2_bias: float32 [1024], P(('dp', 'ctx'))
- grad_w_qkv: float32 [1024, 3072], P(('dp', 'ctx'))
- grad_b_qkv: float32 [3072], P(('dp', 'ctx'))
- grad_w_out: float32 [1024, 1024], P(('dp', 'ctx'))
- grad_w_in: float32 [1024, 4096], P(('dp', 'ctx'))
- grad_b_in: float32 [4096], P(('dp', 'ctx'))
- grad_w_fc2: float32 [4096, 1024], P(('dp', 'ctx'))
- grad_b_out: float32 [1024], P(('dp', 'ctx'))
Inputs may be any that keep to these rules, and one draw needn't show every extreme that they name: `seq_lengths`: each row gives, in order, the lengths of the sequences packed into the 4096 places of one group; a row sums to 4096; its largest is exactly 2048. `dealing`: each row names every packed block of 64 places once. Slots are ordered by ctx index and then by local block; the slots at one local place b of all ctx indices hold, in some order, one run of consecutive packed blocks that starts at b times the number of ctx devices.
All inputs are finite; a program needn't handle non-finite values.
Results may differ from a plain program's by a relative error of at most 0.012.
The roundings to bfloat16 on the way count: a program that leaves them out, or rounds other values in their place, can miss the bound.
Values may be sent and summed in bfloat16 or wider, within the bound.
No kernel may reach another device: no remote copies, remote signals or barrier semaphores. Data moves between devices by JAX's collectives and lax.ppermute only.
A program may use at most 320 MiB of HBM per device.

v0:
```python
import functools

import jax
import jax.numpy as jnp
from jax import lax
from jax.experimental import pallas as pl
from jax.experimental.pallas import tpu as pltpu
from jax.sharding import Mesh
from jax.sharding import PartitionSpec as P

HEAD = 64
ROT = 16
LONGEST = 2048
GROUP_IN = 4
TILE = 256
EPS = 1e-05
NEG = -1e30
F32 = jnp.float32
BF16 = jnp.bfloat16
G_AXES = ("dp", "out")
ALL_AXES = ("dp", "in", "out")


def dot(a, b):
    return jnp.dot(a, b, preferred_element_type=F32)


def dot_nt(a, b):
    return lax.dot_general(a, b, (((1,), (1,)), ((), ())), preferred_element_type=F32)


def dot_tn(a, b):
    return lax.dot_general(a, b, (((0,), (0,)), ((), ())), preferred_element_type=F32)


def xor_swap(value, axis, size, step):
    return lax.ppermute(value, axis, [(i, i ^ step) for i in range(size)])


def rotary(x, cos, sin_l, sin_r, sign):
    left = pltpu.roll(x, 128 - ROT // 2, 1)
    right = pltpu.roll(x, ROT // 2, 1)
    return x * cos - sign * (left * sin_l) + sign * (right * sin_r)


def pair_up(x, block):
    blocks = [x[i : i + block] for i in range(0, x.shape[0], block)]
    return jnp.concatenate([jnp.concatenate(blocks[i : i + 2], axis=1) for i in range(0, len(blocks), 2)], axis=0)


def unpair(x, block):
    parts = []
    for i in range(0, x.shape[0], block):
        parts += [x[i : i + block, :HEAD], x[i : i + block, HEAD:]]
    return jnp.concatenate(parts, axis=0)


def params(flops, size, exps=0):
    return dict(
        compiler_params=pltpu.CompilerParams(vmem_limit_bytes=40 * 2**20),
        cost_estimate=pl.CostEstimate(flops=flops, bytes_accessed=size, transcendentals=exps),
    )


def row_at(i, z):
    return (i, 0)


def whole_at(i, z):
    return (0, 0)


def slab_at(i, z):
    return (0, i, 0)


def normalized(x_ref):
    x = x_ref[...].astype(F32)
    centred = x - jnp.mean(x, axis=-1, keepdims=True)
    return centred * lax.rsqrt(jnp.mean(centred * centred, axis=-1, keepdims=True) + EPS)


def prep_kernel(heads, block, z_ref, x_ref, norm_ref, w_ref, b_ref, cos_ref, sl_ref, sr_ref, qk_ref, v_ref, n1_ref, n2_ref):
    z = z_ref[0]
    xhat = normalized(x_ref)
    n1 = (xhat * norm_ref[0:1] + norm_ref[1:2]).astype(BF16)
    n1_ref[...] = n1
    n2_ref[...] = (xhat * norm_ref[2:3] + norm_ref[3:4]).astype(BF16)
    joined = dot(n1, w_ref[...]) + b_ref[...]
    cos, sl, sr = cos_ref[...], sl_ref[...], sr_ref[...]
    cols = heads * HEAD
    for h in range(heads):
        at = h * HEAD
        part = jnp.concatenate([joined[:, at : at + HEAD], joined[:, cols + at : cols + at + HEAD]], axis=1)
        qk_ref[z ^ h] = rotary(part, cos, sl, sr, 1.0).astype(BF16)
        v_ref[z ^ h] = pair_up(joined[:, 2 * cols + at : 2 * cols + at + HEAD], block).astype(BF16)


def prep(z, x, norms, w, bias, cos, sl, sr, block):
    rows, width = x.shape
    heads = w.shape[1] // (3 * HEAD)
    table = pl.BlockSpec((TILE, 2 * HEAD), row_at)
    tile = pl.BlockSpec((TILE, width), row_at)
    norm = jax.ShapeDtypeStruct((rows, width), BF16)
    return pl.pallas_call(
        functools.partial(prep_kernel, heads, block),
        grid_spec=pltpu.PrefetchScalarGridSpec(
            num_scalar_prefetch=1,
            grid=(rows // TILE,),
            in_specs=[
                tile,
                pl.BlockSpec(norms.shape, whole_at),
                pl.BlockSpec(w.shape, whole_at),
                pl.BlockSpec(bias.shape, whole_at),
                table,
                table,
                table,
            ],
            out_specs=[
                pl.BlockSpec((heads, TILE, 2 * HEAD), slab_at),
                pl.BlockSpec((heads, TILE // 2, 2 * HEAD), slab_at),
                tile,
                tile,
            ],
        ),
        out_shape=[
            jax.ShapeDtypeStruct((heads, rows, 2 * HEAD), BF16),
            jax.ShapeDtypeStruct((heads, rows // 2, 2 * HEAD), BF16),
            norm,
            norm,
        ],
        **params(2 * rows * width * w.shape[1], 12 * 2**20),
    )(z, x, norms, w, bias, cos, sl, sr)


def feed_kernel(x_ref, n2_ref, dy_ref, norm_ref, w_in_ref, w_fc2_ref, b_ref, h_ref, du_ref, y_ref, dx_ref, sums_ref, db_ref):
    up = dot(n2_ref[...], w_in_ref[...]) + b_ref[...]
    cdf = 0.5 + 0.5 * lax.erf(up * (0.5**0.5))
    hidden = (up * cdf).astype(BF16)
    slope = cdf + up * (jnp.exp(-0.5 * up * up) * 0.3989422804014327)
    grad_up = (dot_nt(dy_ref[...], w_fc2_ref[...]) * slope).astype(BF16)
    h_ref[...] = hidden
    du_ref[...] = grad_up
    y_ref[...] = dot(hidden, w_fc2_ref[...])
    grad_norm = dot_nt(grad_up, w_in_ref[...])
    dx_ref[...] = grad_norm * norm_ref[2:3]
    gain = jnp.sum(grad_norm * normalized(x_ref), axis=0, keepdims=True)
    shift = jnp.sum(grad_norm, axis=0, keepdims=True)
    bias = jnp.sum(grad_up.astype(F32), axis=0, keepdims=True)

    @pl.when(pl.program_id(0) == 0)
    def _():
        sums_ref[...] = jnp.zeros_like(sums_ref)
        db_ref[...] = jnp.zeros_like(db_ref)

    sums_ref[0:1] += gain
    sums_ref[1:2] += shift
    db_ref[0:1] += bias


def feed(x, n2, dy, norms, w_in, w_fc2, bias):
    rows, width = x.shape
    units = w_in.shape[1]
    row, whole = lambda i: (i, 0), lambda i: (0, 0)
    tile, tile_ff = pl.BlockSpec((TILE, width), row), pl.BlockSpec((TILE, units), row)
    return pl.pallas_call(
        feed_kernel,
        grid=(rows // TILE,),
        in_specs=[
            tile,
            tile,
            tile,
            pl.BlockSpec(norms.shape, whole),
            pl.BlockSpec(w_in.shape, whole),
            pl.BlockSpec(w_fc2.shape, whole),
            pl.BlockSpec(bias.shape, whole),
        ],
        out_specs=[
            tile_ff,
            tile_ff,
            tile,
            tile,
            pl.BlockSpec((8, width), whole),
            pl.BlockSpec((8, units), whole),
        ],
        out_shape=[
            jax.ShapeDtypeStruct((rows, units), BF16),
            jax.ShapeDtypeStruct((rows, units), BF16),
            jax.ShapeDtypeStruct((rows, width), F32),
            jax.ShapeDtypeStruct((rows, width), F32),
            jax.ShapeDtypeStruct((8, width), F32),
            jax.ShapeDtypeStruct((8, units), F32),
        ],
        **params(8 * rows * width * units, 24 * 2**20, 2 * rows * units),
    )(x, n2, dy, norms, w_in, w_fc2, bias)


def grad_att_kernel(heads, block, z_ref, dy_ref, wo_ref, do_ref):
    z = z_ref[0]
    grad = dot_nt(dy_ref[...], wo_ref[...])
    for h in range(heads):
        do_ref[z ^ h] = pair_up(grad[:, h * HEAD : (h + 1) * HEAD], block).astype(BF16)


def grad_att(z, dy, wo, block):
    rows, width = dy.shape
    heads = wo.shape[0] // HEAD
    return pl.pallas_call(
        functools.partial(grad_att_kernel, heads, block),
        grid_spec=pltpu.PrefetchScalarGridSpec(
            num_scalar_prefetch=1,
            grid=(rows // TILE,),
            in_specs=[pl.BlockSpec((TILE, width), row_at), pl.BlockSpec(wo.shape, whole_at)],
            out_specs=pl.BlockSpec((heads, TILE // 2, 2 * HEAD), slab_at),
        ),
        out_shape=jax.ShapeDtypeStruct((heads, rows // 2, 2 * HEAD), BF16),
        **params(2 * rows * width * wo.shape[0], 4 * 2**20),
    )(z, dy, wo)


def merge_heads_kernel(heads, block, z_ref, part_ref, o_ref):
    z = z_ref[0]
    for h in range(0, heads, 2):
        one, two = unpair(part_ref[z ^ h].astype(F32), block), unpair(part_ref[z ^ (h + 1)].astype(F32), block)
        o_ref[:, h * HEAD : (h + 2) * HEAD] = jnp.concatenate([one, two], axis=1).astype(BF16)


def merge_heads(z, parts, block):
    heads, half_rows, _ = parts.shape
    return pl.pallas_call(
        functools.partial(merge_heads_kernel, heads, block),
        grid_spec=pltpu.PrefetchScalarGridSpec(
            num_scalar_prefetch=1,
            grid=(2 * half_rows // TILE,),
            in_specs=[pl.BlockSpec((heads, TILE // 2, 2 * HEAD), slab_at)],
            out_specs=pl.BlockSpec((TILE, heads * HEAD), row_at),
        ),
        out_shape=jax.ShapeDtypeStruct((2 * half_rows, heads * HEAD), BF16),
        **params(half_rows * 1024, 2**20),
    )(z, parts)


def post_kernel(
    heads, block, z_ref, dqk_ref, dv_ref, x_ref, dx_ref, norm_ref, w_ref, cos_ref, sl_ref, sr_ref, da_ref, sum_ref, sums_ref, db_ref
):
    z = z_ref[0]
    cos, sl, sr = cos_ref[...], sl_ref[...], sr_ref[...]
    cols = heads * HEAD
    for h in range(0, heads, 2):
        at = h * HEAD
        one = rotary(dqk_ref[z ^ h].astype(F32), cos, sl, sr, -1.0)
        two = rotary(dqk_ref[z ^ (h + 1)].astype(F32), cos, sl, sr, -1.0)
        da_ref[:, at : at + 2 * HEAD] = jnp.concatenate([one[:, :HEAD], two[:, :HEAD]], axis=1).astype(BF16)
        da_ref[:, cols + at : cols + at + 2 * HEAD] = jnp.concatenate([one[:, HEAD:], two[:, HEAD:]], axis=1).astype(BF16)
        one, two = unpair(dv_ref[z ^ h].astype(F32), block), unpair(dv_ref[z ^ (h + 1)].astype(F32), block)
        da_ref[:, 2 * cols + at : 2 * cols + at + 2 * HEAD] = jnp.concatenate([one, two], axis=1).astype(BF16)
    grad = da_ref[...]
    grad_norm = dot_nt(grad, w_ref[...])
    sum_ref[...] = (dx_ref[...] + grad_norm * norm_ref[0:1]).astype(BF16)
    gain = jnp.sum(grad_norm * normalized(x_ref), axis=0, keepdims=True)
    shift = jnp.sum(grad_norm, axis=0, keepdims=True)
    bias = jnp.sum(grad.astype(F32), axis=0, keepdims=True)

    @pl.when(pl.program_id(0) == 0)
    def _():
        sums_ref[...] = jnp.zeros_like(sums_ref)
        db_ref[...] = jnp.zeros_like(db_ref)

    sums_ref[0:1] += gain
    sums_ref[1:2] += shift
    db_ref[0:1] += bias


def post(z, dqk, dv, x, dx, norms, w, cos, sl, sr, block):
    heads, rows, _ = dqk.shape
    width = x.shape[1]
    three = heads * 3 * HEAD
    table = pl.BlockSpec((TILE, 2 * HEAD), row_at)
    tile = pl.BlockSpec((TILE, width), row_at)
    return pl.pallas_call(
        functools.partial(post_kernel, heads, block),
        grid_spec=pltpu.PrefetchScalarGridSpec(
            num_scalar_prefetch=1,
            grid=(rows // TILE,),
            in_specs=[
                pl.BlockSpec((heads, TILE, 2 * HEAD), slab_at),
                pl.BlockSpec((heads, TILE // 2, 2 * HEAD), slab_at),
                tile,
                tile,
                pl.BlockSpec(norms.shape, whole_at),
                pl.BlockSpec(w.shape, whole_at),
                table,
                table,
                table,
            ],
            out_specs=[
                pl.BlockSpec((TILE, three), row_at),
                tile,
                pl.BlockSpec((8, width), whole_at),
                pl.BlockSpec((8, three), whole_at),
            ],
        ),
        out_shape=[
            jax.ShapeDtypeStruct((rows, three), BF16),
            jax.ShapeDtypeStruct((rows, width), BF16),
            jax.ShapeDtypeStruct((8, width), F32),
            jax.ShapeDtypeStruct((8, three), F32),
        ],
        **params(2 * rows * width * three, 14 * 2**20),
    )(z, dqk, dv, x, dx, norms, w, cos, sl, sr)


def doc_start(packed, ends_ref, count):
    start = packed * 0
    for d in range(count):
        start = jnp.where(packed >= ends_ref[d], ends_ref[d], start)
    return start


def doc_end(packed, ends_ref, count):
    end = ends_ref[count - 1]
    for d in range(count - 2, -1, -1):
        end = jnp.where(packed < ends_ref[d], ends_ref[d], end)
    return end


def tile_at(i):
    return pl.ds(pl.multiple_of(i * TILE, TILE), TILE)


def load_half(ref, source, block):
    both = ref[pl.ds(pl.multiple_of((source // 2) * block, block), block), :].astype(F32)
    return jnp.where(source % 2 == 0, both[:, :HEAD], both[:, HEAD:])


def masked_scores(k_s, q_t, ends_ref, count, i, j):
    s = dot(k_s[tile_at(j), :], q_t[:HEAD, tile_at(i)])
    key_at = lax.broadcasted_iota(jnp.int32, (TILE, TILE), 0)
    query_at = lax.broadcasted_iota(jnp.int32, (TILE, TILE), 1)
    query_row = i * TILE + lax.broadcasted_iota(jnp.int32, (1, TILE), 1)
    first = doc_start(query_row, ends_ref, count) - j * TILE
    last = (i - j) * TILE + query_at
    return jnp.where((key_at >= first) & (key_at <= last), s, NEG)


def forward_kernel(block, count, source_ref, packed_ref, ends_ref, qk_ref, v_ref, o_ref, o_t, lse_ref, k_s, q_t, v_t, o_s):
    rows = qk_ref.shape[0]
    tiles = rows // TILE
    per = TILE // block
    scale = HEAD ** (-0.5)

    def gather(i, carry):
        qk, v = [], []
        for b in range(per):
            src = source_ref[i * per + b]
            qk.append(qk_ref[pl.ds(pl.multiple_of(src * block, block), block), :].astype(F32))
            v.append(load_half(v_ref, src, block))
        qk, v = jnp.concatenate(qk, axis=0), jnp.concatenate(v, axis=0)
        k_s[tile_at(i), :] = qk[:, HEAD:].astype(BF16)
        q_t[:, tile_at(i)] = (qk.T[:HEAD] * scale).astype(BF16)
        v_t[:, tile_at(i)] = v.T.astype(BF16)
        return carry

    lax.fori_loop(0, tiles, gather, 0)

    def forward(i, carry):
        def step(j, state):
            top, total, acc = state
            s = masked_scores(k_s, q_t, ends_ref, count, i, j)
            new_top = jnp.maximum(top, jnp.max(s, axis=0, keepdims=True))
            p = jnp.exp(s - new_top)
            fade = jnp.exp(top - new_top)
            total = total * fade + jnp.sum(p, axis=0, keepdims=True)
            acc = acc * fade + dot(v_t[:, tile_at(j)], p.astype(BF16))
            return new_top, total, acc

        low = doc_start(i * TILE, ends_ref, count) // TILE
        top, total, acc = lax.fori_loop(
            low, i + 1, step, (jnp.full((1, TILE), NEG, F32), jnp.zeros((1, TILE), F32), jnp.zeros((HEAD, TILE), F32))
        )
        out = acc / total
        lse_ref[:, tile_at(i)] = top + jnp.log(total)
        o_t[:, tile_at(i)] = out
        o_s[tile_at(i), :] = out.T
        return carry

    lax.fori_loop(0, tiles, forward, 0)

    def scatter(i, carry):
        both = [o_s[pl.ds(pl.multiple_of(packed_ref[2 * i + b] * block, block), block), :] for b in range(2)]
        o_ref[pl.ds(pl.multiple_of(i * block, block), block), :] = jnp.concatenate(both, axis=1).astype(BF16)
        return carry

    lax.fori_loop(0, rows // (2 * block), scatter, 0)


def backward_kernel(
    block, count, source_ref, packed_ref, ends_ref, qk_ref, v_ref, do_ref, o_t, lse_ref, dqk_ref, dv_ref, q_s, k_s, v_s, do_s, qk_t, do_t, dq_t, delta_s, dk_s, dv_s
):
    rows = qk_ref.shape[0]
    tiles = rows // TILE
    per = TILE // block
    scale = HEAD ** (-0.5)

    def gather(i, carry):
        qk, v, do = [], [], []
        for b in range(per):
            src = source_ref[i * per + b]
            qk.append(qk_ref[pl.ds(pl.multiple_of(src * block, block), block), :].astype(F32))
            v.append(load_half(v_ref, src, block))
            do.append(load_half(do_ref, src, block))
        qk, v, do = jnp.concatenate(qk, axis=0), jnp.concatenate(v, axis=0), jnp.concatenate(do, axis=0)
        here = tile_at(i)
        q_s[here, :] = (qk[:, :HEAD] * scale).astype(BF16)
        k_s[here, :] = qk[:, HEAD:].astype(BF16)
        turned = qk.T
        qk_t[:HEAD, here] = (turned[:HEAD] * scale).astype(BF16)
        qk_t[HEAD:, here] = turned[HEAD:].astype(BF16)
        v_s[here, :] = v.astype(BF16)
        do_s[here, :] = do.astype(BF16)
        do_turned = do.T
        do_t[:, here] = do_turned.astype(BF16)
        dq_t[:, here] = jnp.zeros((HEAD, TILE), F32)
        delta_s[:, here] = jnp.sum(o_t[:, here] * do_turned, axis=0, keepdims=True)
        return carry

    lax.fori_loop(0, tiles, gather, 0)

    def backward(j, carry):
        keys = tile_at(j)

        def step(i, state):
            dk, dv = state
            here = tile_at(i)
            p = jnp.exp(masked_scores(k_s, qk_t, ends_ref, count, i, j) - lse_ref[:, here])
            dp = dot(v_s[keys, :], do_t[:, here])
            ds = (p * (dp - delta_s[:, here])).astype(BF16)
            dv = dv + dot(p.astype(BF16), do_s[here, :])
            dk = dk + dot(ds, q_s[here, :])
            dq_t[:, here] += dot(qk_t[HEAD:, keys], ds)
            return dk, dv

        high = (doc_end(j * TILE + TILE - 1, ends_ref, count) - 1) // TILE
        zero = jnp.zeros((TILE, HEAD), F32)
        dk, dv = lax.fori_loop(j, high + 1, step, (zero, zero))
        dk_s[keys, :] = dk
        dv_s[keys, :] = dv
        return carry

    lax.fori_loop(0, tiles, backward, 0)

    def scatter(i, carry):
        here = tile_at(i)
        dq = (dq_t[:, here] * scale).T
        dqk = jnp.concatenate([dq, dk_s[here, :]], axis=1).astype(BF16)
        for b in range(per):
            dst = pl.ds(pl.multiple_of(source_ref[i * per + b] * block, block), block)
            dqk_ref[dst, :] = dqk[b * block : (b + 1) * block, :]
        return carry

    lax.fori_loop(0, tiles, scatter, 0)

    def scatter_v(i, carry):
        both = [dv_s[pl.ds(pl.multiple_of(packed_ref[2 * i + b] * block, block), block), :] for b in range(2)]
        dv_ref[pl.ds(pl.multiple_of(i * block, block), block), :] = jnp.concatenate(both, axis=1).astype(BF16)
        return carry

    lax.fori_loop(0, rows // (2 * block), scatter_v, 0)


IN_VMEM = pl.BlockSpec(memory_space=pltpu.VMEM)
IN_SMEM = pl.BlockSpec(memory_space=pltpu.SMEM)


def attend_forward(source, packed, ends, qk, v, block):
    rows = qk.shape[0]
    turned = pltpu.VMEM((HEAD, rows), BF16)
    return pl.pallas_call(
        functools.partial(forward_kernel, block, ends.shape[0]),
        in_specs=[IN_SMEM] * 3 + [IN_VMEM] * 2,
        out_specs=[IN_VMEM] * 3,
        out_shape=[
            jax.ShapeDtypeStruct((rows // 2, 2 * HEAD), BF16),
            jax.ShapeDtypeStruct((HEAD, rows), F32),
            jax.ShapeDtypeStruct((1, rows), F32),
        ],
        scratch_shapes=[pltpu.VMEM((rows, HEAD), BF16), turned, turned, pltpu.VMEM((rows, HEAD), F32)],
        **params(rows * rows * HEAD * 4, 6 * rows * HEAD * 2, rows * rows),
    )(source, packed, ends, qk, v)


def attend_backward(source, packed, ends, qk, v, do, o_t, lse, block):
    rows = qk.shape[0]
    half = pltpu.VMEM((rows, HEAD), BF16)
    wide = pltpu.VMEM((rows, HEAD), F32)
    return pl.pallas_call(
        functools.partial(backward_kernel, block, ends.shape[0]),
        in_specs=[IN_SMEM] * 3 + [IN_VMEM] * 5,
        out_specs=[IN_VMEM] * 2,
        out_shape=[
            jax.ShapeDtypeStruct((rows, 2 * HEAD), BF16),
            jax.ShapeDtypeStruct((rows // 2, 2 * HEAD), BF16),
        ],
        scratch_shapes=[
            half,
            half,
            half,
            half,
            pltpu.VMEM((2 * HEAD, rows), BF16),
            pltpu.VMEM((HEAD, rows), BF16),
            pltpu.VMEM((HEAD, rows), F32),
            pltpu.VMEM((1, rows), F32),
            wide,
            wide,
        ],
        **params(rows * rows * HEAD * 10, 12 * rows * HEAD * 2, rows * rows),
    )(source, packed, ends, qk, v, do, o_t, lse)


def join_in(value, far):
    far = jnp.stack([value, far])
    near = xor_swap(far, "in", GROUP_IN, 1)
    return jnp.stack([far[0], near[0], far[1], near[1]])


def scatter_in(parts):
    half = parts.shape[-1] // 2
    sums = []
    for at in (0, half):
        cut = slice(at, at + half)
        near = xor_swap(jnp.stack([parts[1, :, cut], parts[3, :, cut]]), "in", GROUP_IN, 1)
        far = (parts[2, :, cut].astype(F32) + near[1].astype(F32)).astype(BF16)
        far = xor_swap(far, "in", GROUP_IN, 2)
        sums.append(parts[0, :, cut].astype(F32) + near[0].astype(F32) + far.astype(F32))
    return jnp.concatenate(sums, axis=1)


def exchange_in(parts, t):
    here = [lax.dynamic_index_in_dim(parts, t ^ s, 0, keepdims=False) for s in range(GROUP_IN)]
    there = [here[0]] + [xor_swap(here[s], "in", GROUP_IN, s) for s in range(1, GROUP_IN)]
    stacked = jnp.stack(there)
    return jnp.stack([lax.dynamic_index_in_dim(stacked, t ^ u, 0, keepdims=False) for u in range(GROUP_IN)])


def exchange_out(parts, size):
    return jnp.stack([parts[0]] + [xor_swap(parts[s], "out", size, s) for s in range(1, size)])


def body(
    tokens,
    seq_lengths,
    dealing,
    ln1_gain,
    ln1_bias,
    ln2_gain,
    ln2_bias,
    w_qkv,
    b_qkv,
    w_out,
    w_in,
    b_in,
    w_fc2,
    b_out,
    cotangent,
):
    n_dp, n_out, n_in = lax.axis_size("dp"), lax.axis_size("out"), lax.axis_size("in")
    n_g = n_dp * n_out
    n_all = n_g * n_in
    rows_dev, width = tokens.shape
    ff = w_in.shape[1]
    ff_in = ff // n_in
    r_w = w_in.shape[0]
    r_ff = w_fc2.shape[0]
    block = LONGEST // (2 * n_out * n_in)
    slots_dev = rows_dev // block
    heads = width // HEAD
    h_in = heads // n_in
    cols = h_in * HEAD
    rows = rows_dev * n_in
    z, t = lax.axis_index("out"), lax.axis_index("in")
    z_arr = z[None].astype(jnp.int32)
    lengths, order = seq_lengths[0], dealing[0]
    ends = jnp.cumsum(lengths)

    slots = order.shape[0]
    ids = jnp.arange(slots, dtype=jnp.int32)
    slot_of = jnp.sum(jnp.where(order[None, :] == ids[:, None], ids[None, :], 0), axis=1)
    chunk = slot_of // slots_dev
    source = (((chunk % n_out) ^ z) * n_in + ((chunk // n_out) ^ t)) * slots_dev + slot_of % slots_dev
    source = source.astype(jnp.int32)
    lies = ids // slots_dev
    slot_here = (((lies % n_in) ^ t) * n_out + ((lies // n_in) ^ z)) * slots_dev + ids % slots_dev
    packed_of = jnp.sum(jnp.where(slot_here[:, None] == ids[None, :], order[None, :], 0), axis=1).astype(jnp.int32)

    part = jnp.arange(rows, dtype=jnp.int32)
    packed = packed_of[: rows // block].reshape(-1, 1) * block + jnp.arange(block, dtype=jnp.int32)[None, :]
    packed = packed.reshape(rows)
    starts = jnp.max(jnp.where(packed[:, None] >= ends[None, :], ends[None, :], 0), axis=1)
    position = (packed - starts).astype(F32)
    lane = jnp.arange(2 * HEAD, dtype=jnp.int32) % HEAD
    half = ROT // 2
    freq = 10000.0 ** (-2.0 * (lane % half).astype(F32) / ROT)
    phase = position[:, None] * freq[None, :]
    cos = jnp.where(lane < ROT, jnp.cos(phase), 1.0)
    sine = jnp.sin(phase)
    sin_l = jnp.where(lane < half, sine, 0.0)
    sin_r = jnp.where((lane >= half) & (lane < ROT), sine, 0.0)

    vectors = [ln1_gain, ln1_bias, ln2_gain, ln2_bias, b_qkv, b_out, b_in]
    sizes = [v.shape[0] for v in vectors]
    n_vec = sum(sizes)
    vec_cols = n_vec // r_w
    x_far = xor_swap(tokens, "in", n_in, 2)
    qkv_cols = jnp.transpose(w_qkv.reshape(r_w, 3, n_in, cols), (2, 0, 1, 3)).reshape(n_in, r_w, 3 * cols)
    in_cols = jnp.transpose(w_in.reshape(r_w, n_dp, n_in, n_out, r_ff), (2, 0, 1, 3, 4)).reshape(n_in, r_w, ff_in)
    vec = jnp.pad(jnp.concatenate(vectors).reshape(r_w, vec_cols), ((0, 0), (0, 128 - vec_cols)))
    vec = jnp.broadcast_to(vec[None], (n_in, r_w, 128))
    joined_cols = exchange_in(jnp.concatenate([qkv_cols, vec, in_cols], axis=2), t).reshape(n_in * r_w, -1)
    home = []
    for b in range(n_all):
        t_to, g_to = b // n_g, b % n_g
        home.append((b, ((g_to // n_out) * n_in + t_to) * n_out + g_to % n_out))
    out_rows = lax.ppermute(w_out, ALL_AXES, home).reshape(n_in * r_w, cols)
    first = jnp.concatenate([joined_cols[:, : 3 * cols + 128], out_rows], axis=1)
    first, x_far, cotangent = lax.optimization_barrier((first, x_far, cotangent))
    dy_far = xor_swap(cotangent, "in", n_in, 2)
    first = lax.all_gather(first, G_AXES, axis=0, tiled=False)
    second = jnp.concatenate([joined_cols[:, 3 * cols + 128 :], w_fc2], axis=1)
    second = lax.all_gather(second, G_AXES, axis=0, tiled=False)

    def natural(value):
        value = value.reshape(n_dp, n_out, n_in, r_w, -1)
        return jnp.transpose(value, (0, 2, 1, 3, 4)).reshape(n_all * r_w, -1)

    def by_owner(value):
        value = value.reshape(n_dp, n_in, n_out, r_w, -1)
        return jnp.transpose(value, (0, 2, 1, 3, 4)).reshape(n_g, n_in * r_w, -1)

    weight_qkv = natural(first[:, :, : 3 * cols])
    weight_out = first[:, :, 3 * cols + 128 :].reshape(cols, width)
    weight_in = natural(second[:, :, :ff_in])
    weight_fc2 = second[:, :, ff_in:].reshape(ff_in, width)
    vec_all = first[:, :, 3 * cols : 3 * cols + vec_cols].reshape(n_dp, n_out, n_in, n_vec).astype(F32)
    vec_all = jnp.transpose(vec_all, (0, 2, 1, 3))
    spans, at = [], 0
    for size in sizes:
        spans.append(vec_all[..., at : at + size])
        at += size
    gain_one, shift_one, gain_two, shift_two = [s.reshape(width) for s in spans[:4]]
    bias_out = spans[5].reshape(width)
    bias_in = lax.dynamic_index_in_dim(spans[6], t, 1, keepdims=False).reshape(ff_in)
    bias_qkv = lax.dynamic_index_in_dim(spans[4].reshape(3, n_in, cols), t, 1, keepdims=False).reshape(-1)
    norms = jnp.concatenate([jnp.stack([gain_one, shift_one, gain_two, shift_two]), jnp.zeros((4, width), F32)])

    x_all = join_in(tokens, x_far).reshape(rows, width)
    dy_all = join_in(cotangent, dy_far).reshape(rows, width)

    qk, v, n1, n2 = prep(z_arr, x_all, norms, weight_qkv, bias_qkv[None], cos, sin_l, sin_r, block)
    qk = exchange_out(qk, n_out).reshape(n_out * rows, 2 * HEAD)
    v = exchange_out(v, n_out).reshape(n_out * rows // 2, 2 * HEAD)
    do = grad_att(z_arr, dy_all, weight_out, block)
    do = exchange_out(do, n_out).reshape(n_out * rows // 2, 2 * HEAD)
    o, o_t, lse = attend_forward(source, packed_of, ends, qk, v, block)
    o = exchange_out(o.reshape(n_out, rows // 2, 2 * HEAD), n_out)

    hidden, grad_up, y_ff, dx_ff, sums_two, grad_b_in = feed(x_all, n2, dy_all, norms, weight_in, weight_fc2, bias_in[None])
    grad_fc2 = dot_tn(hidden, dy_all)
    grad_in = dot_tn(n2, grad_up)
    second_grads = jnp.concatenate(
        [by_owner(grad_in.astype(BF16)), grad_fc2.astype(BF16).reshape(n_g, r_ff, width)], axis=2
    )

    o = merge_heads(z_arr, o, block)
    y_part = (y_ff + dot(o, weight_out)).astype(BF16)

    do, second_grads, y_part = lax.optimization_barrier((do, second_grads, y_part))
    second_grads = lax.psum_scatter(second_grads, G_AXES, scatter_dimension=0, tiled=False)
    own = tokens.astype(F32)
    mixed = (own + scatter_in(y_part.reshape(n_in, rows_dev, width)) + bias_out).astype(BF16)
    dqk, dv = attend_backward(source, packed_of, ends, qk, v, do, o_t, lse, block)
    dqk = exchange_out(dqk.reshape(n_out, rows, 2 * HEAD), n_out)
    dv = exchange_out(dv.reshape(n_out, rows // 2, 2 * HEAD), n_out)
    dqk, dv, mixed, second_grads = lax.optimization_barrier((dqk, dv, mixed, second_grads))
    da, w_parts, sums_one, grad_b_qkv = post(
        z_arr, dqk, dv, x_all, dx_ff, norms, weight_qkv, cos, sin_l, sin_r, block
    )

    grad_qkv = dot_tn(n1, da)
    grad_out = dot_tn(o, dy_all)

    def placed(vector, axis):
        spread = jnp.expand_dims(vector, axis)
        mask = (jnp.arange(n_in) == t).reshape([-1 if a == axis else 1 for a in range(spread.ndim)])
        return jnp.where(mask, spread, 0.0).reshape(-1)

    grad_own = cotangent.astype(F32)
    vec_grads = [
        sums_one[0],
        sums_one[1],
        sums_two[0],
        sums_two[1],
        placed(grad_b_qkv[0].reshape(3, cols), 1),
        jnp.sum(grad_own, axis=0),
        placed(grad_b_in[0].reshape(n_dp, n_out, r_ff), 1),
    ]
    vec_grads = jnp.concatenate([v.reshape(n_dp, n_in, n_out, -1) for v in vec_grads], axis=3)
    vec_grads = jnp.transpose(vec_grads, (0, 2, 1, 3)).reshape(n_g, n_in * r_w, vec_cols)
    vec_grads = jnp.pad(vec_grads, ((0, 0), (0, 0), (0, 128 - vec_cols)))
    first_grads = jnp.concatenate(
        [
            by_owner(grad_qkv.astype(BF16)),
            vec_grads.astype(BF16),
            grad_out.astype(BF16).reshape(n_g, n_in * r_w, cols),
        ],
        axis=2,
    )
    first_grads = lax.psum_scatter(first_grads, G_AXES, scatter_dimension=0, tiled=False)

    in_part = exchange_in(second_grads[:, :ff_in].reshape(n_in, r_w, ff_in), t)
    in_part = in_part.reshape(n_in, r_w, n_dp, n_out, r_ff)
    grad_w_in = jnp.transpose(in_part, (1, 2, 0, 3, 4)).reshape(r_w, ff).astype(F32)
    grad_w_fc2 = second_grads[:, ff_in:].astype(F32)
    back_home = [(b, a) for a, b in home]
    out_part = first_grads[:, 3 * cols + 128 :].reshape(r_w, width)
    grad_w_out = lax.ppermute(out_part, ALL_AXES, back_home).astype(F32)
    qkv_part = exchange_in(first_grads[:, : 3 * cols + 128].reshape(n_in, r_w, 3 * cols + 128), t)
    qkv_grad = jnp.transpose(qkv_part[:, :, : 3 * cols].reshape(n_in, r_w, 3, cols), (1, 2, 0, 3))
    grad_w_qkv = qkv_grad.reshape(r_w, 3 * width).astype(F32)
    vec_part = qkv_part[:, :, 3 * cols : 3 * cols + vec_cols].reshape(n_in, n_vec).astype(F32)
    vec_part = jnp.sum(vec_part, axis=0)
    vec_out, at = [], 0
    for size in sizes:
        vec_out.append(vec_part[at : at + size])
        at += size

    w_sum = scatter_in(w_parts.reshape(n_in, rows_dev, width))
    centred = own - jnp.mean(own, axis=-1, keepdims=True)
    own_rstd = lax.rsqrt(jnp.mean(centred * centred, axis=-1, keepdims=True) + EPS)
    own_hat = centred * own_rstd
    mean_w = jnp.mean(w_sum, axis=-1, keepdims=True)
    mean_wx = jnp.mean(w_sum * own_hat, axis=-1, keepdims=True)
    grad_tokens = grad_own + own_rstd * (w_sum - mean_w - own_hat * mean_wx)
    return (
        mixed,
        grad_tokens,
        vec_out[0],
        vec_out[1],
        vec_out[2],
        vec_out[3],
        grad_w_qkv,
        vec_out[4],
        grad_w_out,
        grad_w_in,
        vec_out[6],
        grad_w_fc2,
        vec_out[5],
    )


def solution(mesh):
    n_dp, n_ctx = mesh.shape["dp"], mesh.shape["ctx"]
    split = Mesh(mesh.devices.reshape(n_dp, GROUP_IN, n_ctx // GROUP_IN), ALL_AXES)
    mat, vec, group = P(ALL_AXES, None), P(ALL_AXES), P("dp", None)
    return jax.shard_map(
        body,
        mesh=split,
        in_specs=(mat, group, group, vec, vec, vec, vec, mat, vec, mat, mat, vec, mat, vec, mat),
        out_specs=(mat, mat, vec, vec, vec, vec, mat, vec, mat, mat, vec, mat, vec),
        check_vma=False,
    )
```

profile of v0, /device:TPU:0, one launch (start us, length us, event | category | flops | bytes accessed | tf_op | source)
XLA Modules:
  0.0 437.9 jit_solution(3371645000363410661)
XLA Ops:
  8.7 4.8 %concatenate.31 = bf16[384]{0:T(512)(128)(2,1)S(1)} concatenate(bf16[32]{0:T(256)(128)(2,1)} %param.18, bf16[32]{0:T(256)(128)(2,1)} %param.19, bf16[32]{0:T(256)(128)(2,1)} %param.20, bf16[32]{0:T(256)(128)(2,1)} %param.21, bf16[96]{0:T(256)(128)(2,1)} %param.23, bf16[32]{0:T(256)(128)(2,1)} %param.28, bf16[128]{0:T(256)(128)(2,1)} %param.26), dimensions={0} | concatenate | bytes 1536 | tf_op jit(solution)/shard_map/concatenate | solution.py:616
  15.1 5.1 %collective-permute-start.2 = (bf16[32,1920]{1,0:T(8,128)(2,1)S(1)}, bf16[32,1920]{1,0:T(8,128)(2,1)S(1)}, u32[]{:S(2)}, u32[]{:S(2)}) collective-permute-start(bf16[32,1920]{1,0:T(8,128)(2,1)S(1)} %get-tuple-element.136), channel_id=1, source_target_pairs={{0,12},{4,8},{8,4},{12,0},{1,13},{5,9},{9,5},{13,1},{2,14},{6,10},... | collective-permute-start | bytes 368648 | tf_op jit(solution)/shard_map/ppermute | solution.py:37
  21.5 4.2 collective-permute-start.4
  25.8 18.4 %collective-permute-done.1 = bf16[32,1920]{1,0:T(8,128)(2,1)S(1)} collective-permute-done((bf16[32,1920]{1,0:T(8,128)(2,1)S(1)}, bf16[32,1920]{1,0:T(8,128)(2,1)S(1)}, u32[]{:S(2)}, u32[]{:S(2)}) %collective-permute-start.1) | collective-permute-done | bytes 122912 | tf_op jit(solution)/shard_map/ppermute | solution.py:37
  45.2 10.6 %collective-permute-done.4 = bf16[256,1024]{1,0:T(8,128)(2,1)S(1)} collective-permute-done((bf16[256,1024]{1,0:T(8,128)(2,1)S(1)}, bf16[256,1024]{1,0:T(8,128)(2,1)S(1)}, u32[]{:S(2)}, u32[]{:S(2)}) %collective-permute-start.4) | collective-permute-done | bytes 524320 | tf_op jit(solution)/shard_map/ppermute | solution.py:37
  58.0 21.6 %collective-permute-done.12 = bf16[256,1024]{1,0:T(8,128)(2,1)S(1)} collective-permute-done((bf16[256,1024]{1,0:T(8,128)(2,1)S(1)}, bf16[256,1024]{1,0:T(8,128)(2,1)S(1)}, u32[]{:S(2)}, u32[]{:S(2)}) %collective-permute-start.12) | collective-permute-done | bytes 524320 | tf_op jit(solution)/shard_map/ppermute | solution.py:37
  82.9 12.2 %collective-permute-done.5 = bf16[2,256,1024]{2,1,0:T(8,128)(2,1)S(1)} collective-permute-done((bf16[2,256,1024]{2,1,0:T(8,128)(2,1)S(1)}, bf16[2,256,1024]{2,1,0:T(8,128)(2,1)S(1)}, u32[]{:S(2)}, u32[]{:S(2)}) %collective-permute-start.5) | collective-permute-done | bytes 1048608 | tf_op jit(solution)/shard_map/ppermute | solution.py:37
  96.7 19.0 %collective-permute-done.13 = bf16[2,256,1024]{2,1,0:T(8,128)(2,1)S(1)} collective-permute-done((bf16[2,256,1024]{2,1,0:T(8,128)(2,1)S(1)}, bf16[2,256,1024]{2,1,0:T(8,128)(2,1)S(1)}, u32[]{:S(2)}, u32[]{:S(2)}) %collective-permute-start.13) | collective-permute-done | bytes 1048608 | tf_op jit(solution)/shard_map/ppermute | solution.py:37
  129.4 5.4 %shard_map.246 = (bf16[4,1024,128]{2,1,0:T(8,128)(2,1)S(1)}, bf16[4,512,128]{2,1,0:T(8,128)(2,1)S(1)}, bf16[1024,1024]{1,0:T(8,128)(2,1)S(1)}, bf16[1024,1024]{1,0:T(8,128)(2,1)S(1)}) custom-call(s32[1]{0:T(128)} %bitcast.3.z_ref, bf16[1024,1024]{1,0:T(8,128)(2,1)S(1)} %bitcast.154, f32[8,1024]{1,0:T(8,128)S(1)} %concatenate.34.norm_ref, ...), custom_call_target="tpu_custom_call" | custom-call | flops 1610612736 | bytes 12582912 | tf_op jit(solution)/shard_map/pallas_call | solution.py:105
  144.1 11.9 %collective-permute-done.10 = bf16[512,128]{1,0:T(8,128)(2,1)} collective-permute-done((bf16[512,128]{1,0:T(8,128)(2,1)}, bf16[512,128]{1,0:T(8,128)(2,1)}, u32[]{:S(2)}, u32[]{:S(2)}) %collective-permute-start.10) | collective-permute-done | bytes 131104 | tf_op jit(solution)/shard_map/ppermute | solution.py:37
  160.2 33.7 %shard_map.249 = (bf16[2048,128]{1,0:T(8,128)(2,1)S(1)}, f32[64,4096]{1,0:T(8,128)S(1)}, f32[1,4096]{1,0:T(1,128)S(1)}) custom-call(s32[64]{0:T(128)S(1)} %fusion.24.source_ref, s32[64]{0:T(128)S(1)} %get-tuple-element.75.packed_ref, s32[4]{0:T(128)S(1)} %bitcast.171, bf16[4096,128]{1,0:T(8,128)(2,1)S(1)} %bitcast.163, bf16[2048,128]{1,0:T(8,128)(2,1)S(1)} %bitcast.165), custom_call_target="tpu_custom_call" | custom-call | flops 4294967296 | bytes 3145728 | tf_op jit(solution)/shard_map/pallas_call | solution.py:478
  209.9 13.3 %shard_map.248 = (bf16[1024,1024]{1,0:T(8,128)(2,1)S(1)}, bf16[1024,1024]{1,0:T(8,128)(2,1)S(1)}, f32[1024,1024]{1,0:T(8,128)}, f32[1024,1024]{1,0:T(8,128)}, f3...) custom-call(bf16[1024,1024]{1,0:T(8,128)(2,1)S(1)} %bitcast.155, bf16[1024,1024]{1,0:T(8,128)(2,1)S(1)} %copy-done.22, ...), custom_call_target="tpu_custom_call" | custom-call | flops 8589934592 | bytes 25165824 | tf_op jit(solution)/shard_map/pallas_call | solution.py:166
  230.7 4.2 add_convert_fusion
  245.5 35.1 %shard_map.251 = (bf16[4096,128]{1,0:T(8,128)(2,1)S(1)}, bf16[2048,128]{1,0:T(8,128)(2,1)S(1)}) custom-call(s32[64]{0:T(128)S(1)} %fusion.24.source_ref, s32[64]{0:T(128)S(1)} %get-tuple-element.75.packed_ref, s32[4]{0:T(128)S(1)} %bitcast.172, bf16[4096,128]{1,0:T(8,128)(2,1)S(1)} %bitcast.164, bf16[2048,128]{1,0:T(8,128)(2,1)S(1)} %bitcast.166, ...), custom_call_target="tpu_custom_call" | custom-call | flops 10737418240 | bytes 6291456 | tf_op jit(solution)/shard_map/pallas_call | solution.py:496
  289.0 9.6 %collective-permute-done.25 = bf16[512,128]{1,0:T(8,128)(2,1)S(1)} collective-permute-done((bf16[512,128]{1,0:T(8,128)(2,1)}, bf16[512,128]{1,0:T(8,128)(2,1)S(1)}, u32[]{:S(2)}, u32[]{:S(2)}) %collective-permute-start.25) | collective-permute-done | bytes 131104 | tf_op jit(solution)/shard_map/ppermute | solution.py:37
  300.2 8.3 %collective-permute-done.28 = bf16[2,256,512]{2,1,0:T(8,128)(2,1)S(1)} collective-permute-done((bf16[2,256,512]{2,1,0:T(8,128)(2,1)S(1)}, bf16[2,256,512]{2,1,0:T(8,128)(2,1)S(1)}, u32[]{:S(2)}, u32[]{:S(2)}) %collective-permute-start.28) | collective-permute-done | bytes 524320 | tf_op jit(solution)/shard_map/ppermute | solution.py:37
  315.1 15.3 %collective-permute-done.27 = bf16[256,512]{1,0:T(8,128)(2,1)S(1)} collective-permute-done((bf16[256,512]{1,0:T(8,128)(2,1)S(1)}, bf16[256,512]{1,0:T(8,128)(2,1)S(1)}, u32[]{:S(2)}, u32[]{:S(2)}) %collective-permute-start.27) | collective-permute-done | bytes 262176 | tf_op jit(solution)/shard_map/ppermute | solution.py:37
  330.5 5.6 %collective-permute-done.29 = bf16[256,512]{1,0:T(8,128)(2,1)S(1)} collective-permute-done((bf16[256,512]{1,0:T(8,128)(2,1)S(1)}, bf16[256,512]{1,0:T(8,128)(2,1)S(1)}, u32[]{:S(2)}, u32[]{:S(2)}) %collective-permute-start.29) | collective-permute-done | bytes 262176 | tf_op jit(solution)/shard_map/ppermute | solution.py:37
  344.0 5.8 %shard_map.252 = (bf16[1024,768]{1,0:T(8,128)(2,1)S(1)}, bf16[1024,1024]{1,0:T(8,128)(2,1)S(1)}, f32[8,1024]{1,0:T(8,128)S(1)}, f32[8,768]{1,0:T(8,128)S(1)}) custom-call(s32[1]{0:T(128)} %bitcast.3.z_ref, bf16[4,1024,128]{2,1,0:T(8,128)(2,1)S(1)} %pad_maximum_fusion.6.dqk_ref, bf16[4,512,128]{2,1,0:T(8,128)(2,1)S(1)} %copy-done.11, ...), custom_call_target="tpu_custom_call" | custom-call | flops 1610612736 | bytes 14680064 | tf_op jit(solution)/shard_map/pallas_call | solution.py:280
  369.4 8.7 %collective-permute-done.30 = bf16[2,256,512]{2,1,0:T(8,128)(2,1)S(1)} collective-permute-done((bf16[2,256,512]{2,1,0:T(8,128)(2,1)S(1)}, bf16[2,256,512]{2,1,0:T(8,128)(2,1)S(1)}, u32[]{:S(2)}, u32[]{:S(2)}) %collective-permute-start.30) | collective-permute-done | bytes 524320 | tf_op jit(solution)/shard_map/ppermute | solution.py:37
  378.1 12.4 %collective-permute-done.32 = bf16[2,256,512]{2,1,0:T(8,128)(2,1)S(1)} collective-permute-done((bf16[2,256,512]{2,1,0:T(8,128)(2,1)S(1)}, bf16[2,256,512]{2,1,0:T(8,128)(2,1)S(1)}, u32[]{:S(2)}, u32[]{:S(2)}) %collective-permute-start.32) | collective-permute-done | bytes 524320 | tf_op jit(solution)/shard_map/ppermute | solution.py:37
  398.0 11.6 %collective-permute-done.31 = bf16[256,512]{1,0:T(8,128)(2,1)S(1)} collective-permute-done((bf16[256,512]{1,0:T(8,128)(2,1)}, bf16[256,512]{1,0:T(8,128)(2,1)S(1)}, u32[]{:S(2)}, u32[]{:S(2)}) %collective-permute-start.31) | collective-permute-done | bytes 262176 | tf_op jit(solution)/shard_map/ppermute | solution.py:37
  409.6 5.6 %collective-permute-done.33 = bf16[256,512]{1,0:T(8,128)(2,1)} collective-permute-done((bf16[256,512]{1,0:T(8,128)(2,1)}, bf16[256,512]{1,0:T(8,128)(2,1)}, u32[]{:S(2)}, u32[]{:S(2)}) %collective-permute-start.33) | collective-permute-done | bytes 262176 | tf_op jit(solution)/shard_map/ppermute | solution.py:37
  419.1 4.1 collective-permute-start.34
  (336 shorter events, 136.4 us)
Async XLA Ops:
  7.2 108.9 %all-gather.5.cloned.1.call-start = ((), (), s32[]{:S(2)}) async-start(), calls=%async_computation.4 | async-start | bytes 2654208 | tf_op jit(solution)/shard_map/all_gather | solution.py:627
  20.2 24.0 %collective-permute-start.1 = (bf16[32,1920]{1,0:T(8,128)(2,1)S(1)}, bf16[32,1920]{1,0:T(8,128)(2,1)S(1)}, u32[]{:S(2)}, u32[]{:S(2)}) collective-permute-start(bf16[32,1920]{1,0:T(8,128)(2,1)S(1)} %get-tuple-element.137), channel_id=1, source_target_pairs={{0,8},{4,12},{8,0},{12,4},{1,9},{5,13},{9,1},{13,5},{2,10},{6,14},... | collective-permute-start | bytes 368648 | tf_op jit(solution)/shard_map/ppermute | solution.py:37
  20.2 24.0 %collective-permute-start = (bf16[32,1920]{1,0:T(8,128)(2,1)S(1)}, bf16[32,1920]{1,0:T(8,128)(2,1)S(1)}, u32[]{:S(2)}, u32[]{:S(2)}) collective-permute-start(bf16[32,1920]{1,0:T(8,128)(2,1)S(1)} %get-tuple-element.138), channel_id=1, source_target_pairs={{0,4},{4,0},{8,12},{12,8},{1,5},{5,1},{9,13},{13,9},{2,6},{6,2},{1... | collective-permute-start | bytes 368648 | tf_op jit(solution)/shard_map/ppermute | solution.py:37
  21.5 34.3 %collective-permute-start.4 = (bf16[256,1024]{1,0:T(8,128)(2,1)S(1)}, bf16[256,1024]{1,0:T(8,128)(2,1)S(1)}, u32[]{:S(2)}, u32[]{:S(2)}) collective-permute-start(bf16[256,1024]{1,0:T(8,128)(2,1)S(1)} %copy-done.25), channel_id=1, source_target_pairs={{0,8},{4,12},{8,0},{12,4},{1,9},{5,13},{9,1},{13,5},{2,10},{6,14},... | collective-permute-start | bytes 1572872 | tf_op jit(solution)/shard_map/ppermute | solution.py:37
  55.9 147.7 %all-gather.7.cloned.1.call-start = ((), (), s32[]{:S(2)}) async-start(), calls=%async_computation.5 | async-start | bytes 4718592 | tf_op jit(solution)/shard_map/all_gather | solution.py:629
  56.8 281.6 %reduce-scatter.3.cloned.1.call-start = ((), (), s32[]{:S(2)}) async-start(), calls=%async_computation.2 | async-start | bytes 4718592 | tf_op jit(solution)/shard_map/reduce_scatter | solution.py:677
  57.5 22.1 %collective-permute-start.12 = (bf16[256,1024]{1,0:T(8,128)(2,1)S(1)}, bf16[256,1024]{1,0:T(8,128)(2,1)S(1)}, u32[]{:S(2)}, u32[]{:S(2)}) collective-permute-start(bf16[256,1024]{1,0:T(8,128)(2,1)S(1)} %copy-done.30), channel_id=1, source_target_pairs={{0,8},{4,12},{8,0},{12,4},{1,9},{5,13},{9,1},{13,5},{2,10},{6,14},... | collective-permute-start | bytes 1572872 | tf_op jit(solution)/shard_map/ppermute | solution.py:37
  57.7 37.3 %collective-permute-start.5 = (bf16[2,256,1024]{2,1,0:T(8,128)(2,1)S(1)}, bf16[2,256,1024]{2,1,0:T(8,128)(2,1)S(1)}, u32[]{:S(2)}, u32[]{:S(2)}) collective-permute-start(bf16[2,256,1024]{2,1,0:T(8,128)(2,1)S(1)} %pad_maximum_fusion.3), channel_id=1, source_target_pairs={{0,4},{4,0},{8,12},{12,8},{1,5},{5,1},{9,13},{13,9},{2,6},{6,2},{1... | collective-permute-start | bytes 3145736 | tf_op jit(solution)/shard_map/ppermute | solution.py:37
  79.8 36.0 %collective-permute-start.13 = (bf16[2,256,1024]{2,1,0:T(8,128)(2,1)S(1)}, bf16[2,256,1024]{2,1,0:T(8,128)(2,1)S(1)}, u32[]{:S(2)}, u32[]{:S(2)}) collective-permute-start(bf16[2,256,1024]{2,1,0:T(8,128)(2,1)S(1)} %pad_maximum_fusion.5), channel_id=1, source_target_pairs={{0,4},{4,0},{8,12},{12,8},{1,5},{5,1},{9,13},{13,9},{2,6},{6,2},{1... | collective-permute-start | bytes 3145736 | tf_op jit(solution)/shard_map/ppermute | solution.py:37
  138.4 20.0 %collective-permute-start.8 = (bf16[1024,128]{1,0:T(8,128)(2,1)}, bf16[1024,128]{1,0:T(8,128)(2,1)}, u32[]{:S(2)}, u32[]{:S(2)}) collective-permute-start(bf16[1024,128]{1,0:T(8,128)(2,1)} %get-tuple-element.106), channel_id=1, source_target_pairs={{0,3},{1,2},{2,1},{3,0},{4,7},{5,6},{6,5},{7,4},{8,11},{9,10},{10,... | collective-permute-start | bytes 786440 | tf_op jit(solution)/shard_map/ppermute | solution.py:37
  155.9 39.9 %collective-permute-start.16 = (bf16[512,128]{1,0:T(8,128)(2,1)S(1)}, bf16[512,128]{1,0:T(8,128)(2,1)S(1)}, u32[]{:S(2)}, u32[]{:S(2)}) collective-permute-start(bf16[512,128]{1,0:T(8,128)(2,1)S(1)} %get-tuple-element.124), channel_id=1, source_target_pairs={{0,3},{1,2},{2,1},{3,0},{4,7},{5,6},{6,5},{7,4},{8,11},{9,10},{10,... | collective-permute-start | bytes 393224 | tf_op jit(solution)/shard_map/ppermute | solution.py:37
  156.8 39.2 %collective-permute-start.15 = (bf16[512,128]{1,0:T(8,128)(2,1)S(1)}, bf16[512,128]{1,0:T(8,128)(2,1)S(1)}, u32[]{:S(2)}, u32[]{:S(2)}) collective-permute-start(bf16[512,128]{1,0:T(8,128)(2,1)S(1)} %get-tuple-element.125), channel_id=1, source_target_pairs={{0,2},{1,3},{2,0},{3,1},{4,6},{5,7},{6,4},{7,5},{8,10},{9,11},{10,... | collective-permute-start | bytes 393224 | tf_op jit(solution)/shard_map/ppermute | solution.py:37
  158.4 37.6 %collective-permute-start.14 = (bf16[512,128]{1,0:T(8,128)(2,1)S(1)}, bf16[512,128]{1,0:T(8,128)(2,1)S(1)}, u32[]{:S(2)}, u32[]{:S(2)}) collective-permute-start(bf16[512,128]{1,0:T(8,128)(2,1)S(1)} %get-tuple-element.126), channel_id=1, source_target_pairs={{0,1},{1,0},{2,3},{3,2},{4,5},{5,4},{6,7},{7,6},{8,9},{9,8},{10,11... | collective-permute-start | bytes 393224 | tf_op jit(solution)/shard_map/ppermute | solution.py:37
  234.9 182.8 %reduce-scatter.5.cloned.1.call-start = ((), (), s32[]{:S(2)}) async-start(), calls=%async_computation.3 | async-start | bytes 2654208 | tf_op jit(solution)/shard_map/reduce_scatter | solution.py:717
  281.4 32.4 %collective-permute-start.22 = (bf16[1024,128]{1,0:T(8,128)(2,1)}, bf16[1024,128]{1,0:T(8,128)(2,1)}, u32[]{:S(2)}, u32[]{:S(2)}) collective-permute-start(bf16[1024,128]{1,0:T(8,128)(2,1)} %get-tuple-element.100), channel_id=1, source_target_pairs={{0,3},{1,2},{2,1},{3,0},{4,7},{5,6},{6,5},{7,4},{8,11},{9,10},{10,... | collective-permute-start | bytes 786440 | tf_op jit(solution)/shard_map/ppermute | solution.py:37
  282.5 31.4 %collective-permute-start.21 = (bf16[1024,128]{1,0:T(8,128)(2,1)}, bf16[1024,128]{1,0:T(8,128)(2,1)}, u32[]{:S(2)}, u32[]{:S(2)}) collective-permute-start(bf16[1024,128]{1,0:T(8,128)(2,1)} %get-tuple-element.101), channel_id=1, source_target_pairs={{0,2},{1,3},{2,0},{3,1},{4,6},{5,7},{6,4},{7,5},{8,10},{9,11},{10,... | collective-permute-start | bytes 786440 | tf_op jit(solution)/shard_map/ppermute | solution.py:37
  283.3 25.3 %collective-permute-start.28 = (bf16[2,256,512]{2,1,0:T(8,128)(2,1)S(1)}, bf16[2,256,512]{2,1,0:T(8,128)(2,1)S(1)}, u32[]{:S(2)}, u32[]{:S(2)}) collective-permute-start(bf16[2,256,512]{2,1,0:T(8,128)(2,1)S(1)} %pad_maximum_fusion.14), channel_id=1, source_target_pairs={{0,4},{4,0},{8,12},{12,8},{1,5},{5,1},{9,13},{13,9},{2,6},{6,2},{1... | collective-permute-start | bytes 1572872 | tf_op jit(solution)/shard_map/ppermute | solution.py:37
  310.0 20.5 %collective-permute-start.27 = (bf16[256,512]{1,0:T(8,128)(2,1)S(1)}, bf16[256,512]{1,0:T(8,128)(2,1)S(1)}, u32[]{:S(2)}, u32[]{:S(2)}) collective-permute-start(bf16[256,512]{1,0:T(8,128)(2,1)S(1)} %get-tuple-element.93), channel_id=1, source_target_pairs={{0,8},{4,12},{8,0},{12,4},{1,9},{5,13},{9,1},{13,5},{2,10},{6,14},... | collective-permute-start | bytes 786440 | tf_op jit(solution)/shard_map/ppermute | solution.py:37
  310.1 26.0 %collective-permute-start.29 = (bf16[256,512]{1,0:T(8,128)(2,1)S(1)}, bf16[256,512]{1,0:T(8,128)(2,1)S(1)}, u32[]{:S(2)}, u32[]{:S(2)}) collective-permute-start(bf16[256,512]{1,0:T(8,128)(2,1)S(1)} %get-tuple-element.94), channel_id=1, source_target_pairs={{0,8},{4,12},{8,0},{12,4},{1,9},{5,13},{9,1},{13,5},{2,10},{6,14},... | collective-permute-start | bytes 786440 | tf_op jit(solution)/shard_map/ppermute | solution.py:37
  362.0 28.6 %collective-permute-start.32 = (bf16[2,256,512]{2,1,0:T(8,128)(2,1)S(1)}, bf16[2,256,512]{2,1,0:T(8,128)(2,1)S(1)}, u32[]{:S(2)}, u32[]{:S(2)}) collective-permute-start(bf16[2,256,512]{2,1,0:T(8,128)(2,1)S(1)} %pad_maximum_fusion.16), channel_id=1, source_target_pairs={{0,4},{4,0},{8,12},{12,8},{1,5},{5,1},{9,13},{13,9},{2,6},{6,2},{1... | collective-permute-start | bytes 1572872 | tf_op jit(solution)/shard_map/ppermute | solution.py:37
  365.0 29.5 %collective-permute-start.40 = (bf16[32,1024]{1,0:T(8,128)(2,1)S(1)}, bf16[32,1024]{1,0:T(8,128)(2,1)S(1)}, u32[]{:S(2)}, u32[]{:S(2)}) collective-permute-start(bf16[32,1024]{1,0:T(8,128)(2,1)S(1)} %get-tuple-element.144), channel_id=1, source_target_pairs={{0,12},{4,8},{8,4},{12,0},{1,13},{5,9},{9,5},{13,1},{2,14},{6,10},... | collective-permute-start | bytes 196616 | tf_op jit(solution)/shard_map/ppermute | solution.py:37
  366.1 28.4 %collective-permute-start.39 = (bf16[32,1024]{1,0:T(8,128)(2,1)S(1)}, bf16[32,1024]{1,0:T(8,128)(2,1)S(1)}, u32[]{:S(2)}, u32[]{:S(2)}) collective-permute-start(bf16[32,1024]{1,0:T(8,128)(2,1)S(1)} %get-tuple-element.145), channel_id=1, source_target_pairs={{0,8},{4,12},{8,0},{12,4},{1,9},{5,13},{9,1},{13,5},{2,10},{6,14},... | collective-permute-start | bytes 196616 | tf_op jit(solution)/shard_map/ppermute | solution.py:37
  366.5 27.9 %collective-permute-start.38 = (bf16[32,1024]{1,0:T(8,128)(2,1)S(1)}, bf16[32,1024]{1,0:T(8,128)(2,1)S(1)}, u32[]{:S(2)}, u32[]{:S(2)}) collective-permute-start(bf16[32,1024]{1,0:T(8,128)(2,1)S(1)} %get-tuple-element.146), channel_id=1, source_target_pairs={{0,4},{4,0},{8,12},{12,8},{1,5},{5,1},{9,13},{13,9},{2,6},{6,2},{1... | collective-permute-start | bytes 196616 | tf_op jit(solution)/shard_map/ppermute | solution.py:37
  391.6 23.6 %collective-permute-start.33 = (bf16[256,512]{1,0:T(8,128)(2,1)}, bf16[256,512]{1,0:T(8,128)(2,1)}, u32[]{:S(2)}, u32[]{:S(2)}) collective-permute-start(bf16[256,512]{1,0:T(8,128)(2,1)} %get-tuple-element.86), channel_id=1, source_target_pairs={{0,8},{4,12},{8,0},{12,4},{1,9},{5,13},{9,1},{13,5},{2,10},{6,14},... | collective-permute-start | bytes 786440 | tf_op jit(solution)/shard_map/ppermute | solution.py:37
  (73 other events, 749.5 us)
Sparse Core Ops, SparseCore 0:
  56.0 29.1 all-gather.4
  87.7 36.7 all-gather.6
  235.1 50.4 reduce-scatter.2
  360.3 40.6 reduce-scatter.4
where the time goes:
time: 436 us; the launch traced here: 438 us
  waiting for transfers between devices  177 us (41%)
  Pallas kernels  95.9 us (22%)
  local copies, waits for them, and re-layouts  60.7 us (14%)
  starting transfers between devices  42.3 us (10%)
  other arithmetic  32.7 us (8%)
  between operations  14.9 us (3%)
  matrix products  14.5 us (3%)
    ppermute x39, waiting for transfers between devices, xor_swap(): return lax.ppermute(value, axis, [(i, i ^ step) for i in range(size)])  177 us
    ppermute x39, starting transfers between devices, xor_swap(): return lax.ppermute(value, axis, [(i, i ^ step) for i in range(size)])  40.8 us
    pallas_call x1, Pallas kernels, attend_backward(): pl.pallas_call(functools.partial(backward_kernel, block, ends.shape[0]),...  35.1 us
    pallas_call x1, Pallas kernels, attend_forward(): pl.pallas_call(functools.partial(forward_kernel, block, ends.shape[0]), i...  33.7 us
    unnamed x104, local copies, waits for them, and re-layouts  21.6 us
    pallas_call x1, Pallas kernels, feed(): pl.pallas_call(feed_kernel, grid=(rows // TILE,), in_specs=[tile, tile, t...  13.3 us
    dot_general x4, matrix products, dot_tn(): lax.dot_general(a, b, (((0,), (0,)), ((), ())), preferred_element_type=F32)  10.2 us
  transfers between devices with their start and end apart: 45, of which 16 were waited for; matrix products, arithmetic and copies ran while one was open for 12% of the time, Pallas kernels for 18%

commit v1 on v0

--- a/solution.py
+++ b/solution.py
@@ -57,7 +57,7 @@
 
 def params(flops, size, exps=0):
     return dict(
-        compiler_params=pltpu.CompilerParams(vmem_limit_bytes=40 * 2**20),
+        compiler_params=pltpu.CompilerParams(vmem_limit_bytes=60 * 2**20),
         cost_estimate=pl.CostEstimate(flops=flops, bytes_accessed=size, transcendentals=exps),
     )
 
@@ -485,7 +485,7 @@
             jax.ShapeDtypeStruct((1, rows), F32),
         ],
         scratch_shapes=[pltpu.VMEM((rows, HEAD), BF16), turned, turned, pltpu.VMEM((rows, HEAD), F32)],
-        **params(rows * rows * HEAD * 4, 6 * rows * HEAD * 2, rows * rows),
+        **params(rows * rows * HEAD * 40, 6 * rows * HEAD * 2, rows * rows),
     )(source, packed, ends, qk, v)
 
 
@@ -513,7 +513,7 @@
             wide,
             wide,
         ],
-        **params(rows * rows * HEAD * 10, 12 * rows * HEAD * 2, rows * rows),
+        **params(rows * rows * HEAD * 40, 12 * rows * HEAD * 2, rows * rows),
     )(source, packed, ends, qk, v, do, o_t, lse)
 
 
@@ -523,16 +523,18 @@
     return jnp.stack([far[0], near[0], far[1], near[1]])
 
 
-def scatter_in(parts):
-    half = parts.shape[-1] // 2
-    sums = []
-    for at in (0, half):
-        cut = slice(at, at + half)
-        near = xor_swap(jnp.stack([parts[1, :, cut], parts[3, :, cut]]), "in", GROUP_IN, 1)
-        far = (parts[2, :, cut].astype(F32) + near[1].astype(F32)).astype(BF16)
-        far = xor_swap(far, "in", GROUP_IN, 2)
-        sums.append(parts[0, :, cut].astype(F32) + near[0].astype(F32) + far.astype(F32))
-    return jnp.concatenate(sums, axis=1)
+def halves(parts):
+    cut = parts.shape[-1] // 2
+    return [parts[..., :cut], parts[..., cut:]]
+
+
+def near_in(parts):
+    return xor_swap(jnp.stack([parts[1], parts[3]]), "in", GROUP_IN, 1)
+
+
+def far_in(parts, near):
+    far = xor_swap((parts[2].astype(F32) + near[1].astype(F32)).astype(BF16), "in", GROUP_IN, 2)
+    return parts[0].astype(F32) + near[0].astype(F32) + far.astype(F32)
 
 
 def exchange_in(parts, t):
@@ -608,22 +610,23 @@
 
     vectors = [ln1_gain, ln1_bias, ln2_gain, ln2_bias, b_qkv, b_out, b_in]
     sizes = [v.shape[0] for v in vectors]
-    n_vec = sum(sizes)
-    vec_cols = n_vec // r_w
-    x_far = xor_swap(tokens, "in", n_in, 2)
+    per_row = -(-len(vectors) // r_w)
+    lanes = 128 // per_row
     qkv_cols = jnp.transpose(w_qkv.reshape(r_w, 3, n_in, cols), (2, 0, 1, 3)).reshape(n_in, r_w, 3 * cols)
     in_cols = jnp.transpose(w_in.reshape(r_w, n_dp, n_in, n_out, r_ff), (2, 0, 1, 3, 4)).reshape(n_in, r_w, ff_in)
-    vec = jnp.pad(jnp.concatenate(vectors).reshape(r_w, vec_cols), ((0, 0), (0, 128 - vec_cols)))
+    vec = jnp.stack([jnp.pad(v, (0, lanes - v.shape[0])) for v in vectors])
+    vec = jnp.pad(vec, ((0, r_w * per_row - len(vectors)), (0, 0))).reshape(r_w, 128)
     vec = jnp.broadcast_to(vec[None], (n_in, r_w, 128))
-    joined_cols = exchange_in(jnp.concatenate([qkv_cols, vec, in_cols], axis=2), t).reshape(n_in * r_w, -1)
+    all_cols = jnp.concatenate([qkv_cols, vec, in_cols], axis=2)
+    joined_cols = exchange_in(all_cols, t).reshape(n_in * r_w, -1)
     home = []
     for b in range(n_all):
         t_to, g_to = b // n_g, b % n_g
         home.append((b, ((g_to // n_out) * n_in + t_to) * n_out + g_to % n_out))
     out_rows = lax.ppermute(w_out, ALL_AXES, home).reshape(n_in * r_w, cols)
     first = jnp.concatenate([joined_cols[:, : 3 * cols + 128], out_rows], axis=1)
-    first, x_far, cotangent = lax.optimization_barrier((first, x_far, cotangent))
-    dy_far = xor_swap(cotangent, "in", n_in, 2)
+    first, to_send = lax.optimization_barrier((first, tokens))
+    x_far = xor_swap(to_send, "in", n_in, 2)
     first = lax.all_gather(first, G_AXES, axis=0, tiled=False)
     second = jnp.concatenate([joined_cols[:, 3 * cols + 128 :], w_fc2], axis=1)
     second = lax.all_gather(second, G_AXES, axis=0, tiled=False)
@@ -640,12 +643,9 @@
     weight_out = first[:, :, 3 * cols + 128 :].reshape(cols, width)
     weight_in = natural(second[:, :, :ff_in])
     weight_fc2 = second[:, :, ff_in:].reshape(ff_in, width)
-    vec_all = first[:, :, 3 * cols : 3 * cols + vec_cols].reshape(n_dp, n_out, n_in, n_vec).astype(F32)
-    vec_all = jnp.transpose(vec_all, (0, 2, 1, 3))
-    spans, at = [], 0
-    for size in sizes:
-        spans.append(vec_all[..., at : at + size])
-        at += size
+    vec_all = first[:, :, 3 * cols : 3 * cols + 128].reshape(n_dp, n_out, n_in, r_w * per_row, lanes)
+    vec_all = jnp.transpose(vec_all[:, :, :, : len(vectors)], (3, 0, 2, 1, 4)).astype(F32)
+    spans = [vec_all[i, ..., :size] for i, size in enumerate(sizes)]
     gain_one, shift_one, gain_two, shift_two = [s.reshape(width) for s in spans[:4]]
     bias_out = spans[5].reshape(width)
     bias_in = lax.dynamic_index_in_dim(spans[6], t, 1, keepdims=False).reshape(ff_in)
@@ -653,40 +653,56 @@
     norms = jnp.concatenate([jnp.stack([gain_one, shift_one, gain_two, shift_two]), jnp.zeros((4, width), F32)])
 
     x_all = join_in(tokens, x_far).reshape(rows, width)
-    dy_all = join_in(cotangent, dy_far).reshape(rows, width)
+    x_all, to_send = lax.optimization_barrier((x_all, cotangent))
+    dy_far = xor_swap(to_send, "in", n_in, 2)
 
     qk, v, n1, n2 = prep(z_arr, x_all, norms, weight_qkv, bias_qkv[None], cos, sin_l, sin_r, block)
     qk = exchange_out(qk, n_out).reshape(n_out * rows, 2 * HEAD)
     v = exchange_out(v, n_out).reshape(n_out * rows // 2, 2 * HEAD)
+    qk, v, dy_far = lax.optimization_barrier((qk, v, dy_far))
+    dy_all = join_in(cotangent, dy_far).reshape(rows, width)
+    o, o_t, lse = attend_forward(source, packed_of, ends, qk, v, block)
+    o, dy_all = lax.optimization_barrier((o, dy_all))
+    o = exchange_out(o.reshape(n_out, rows // 2, 2 * HEAD), n_out)
     do = grad_att(z_arr, dy_all, weight_out, block)
     do = exchange_out(do, n_out).reshape(n_out * rows // 2, 2 * HEAD)
-    o, o_t, lse = attend_forward(source, packed_of, ends, qk, v, block)
-    o = exchange_out(o.reshape(n_out, rows // 2, 2 * HEAD), n_out)
 
     hidden, grad_up, y_ff, dx_ff, sums_two, grad_b_in = feed(x_all, n2, dy_all, norms, weight_in, weight_fc2, bias_in[None])
+    o, y_ff = lax.optimization_barrier((o, y_ff))
+    o = merge_heads(z_arr, o, block)
+    y_part = (y_ff + dot(o, weight_out)).astype(BF16).reshape(n_in, rows_dev, width)
     grad_fc2 = dot_tn(hidden, dy_all)
     grad_in = dot_tn(n2, grad_up)
+    grad_out = dot_tn(o, dy_all)
     second_grads = jnp.concatenate(
-        [by_owner(grad_in.astype(BF16)), grad_fc2.astype(BF16).reshape(n_g, r_ff, width)], axis=2
+        [
+            by_owner(grad_in.astype(BF16)),
+            grad_fc2.astype(BF16).reshape(n_g, r_ff, width),
+            grad_out.astype(BF16).reshape(n_g, n_in * r_w, cols),
+        ],
+        axis=2,
     )
-
-    o = merge_heads(z_arr, o, block)
-    y_part = (y_ff + dot(o, weight_out)).astype(BF16)
 
     do, second_grads, y_part = lax.optimization_barrier((do, second_grads, y_part))
     second_grads = lax.psum_scatter(second_grads, G_AXES, scatter_dimension=0, tiled=False)
+    y_near = near_in(y_part)
     own = tokens.astype(F32)
-    mixed = (own + scatter_in(y_part.reshape(n_in, rows_dev, width)) + bias_out).astype(BF16)
     dqk, dv = attend_backward(source, packed_of, ends, qk, v, do, o_t, lse, block)
+    dqk, dv, y_near = lax.optimization_barrier((dqk, dv, y_near))
     dqk = exchange_out(dqk.reshape(n_out, rows, 2 * HEAD), n_out)
     dv = exchange_out(dv.reshape(n_out, rows // 2, 2 * HEAD), n_out)
-    dqk, dv, mixed, second_grads = lax.optimization_barrier((dqk, dv, mixed, second_grads))
+    mixed = (own + far_in(y_part, y_near) + bias_out).astype(BF16)
     da, w_parts, sums_one, grad_b_qkv = post(
         z_arr, dqk, dv, x_all, dx_ff, norms, weight_qkv, cos, sin_l, sin_r, block
     )
+    in_part = exchange_in(second_grads[:, :ff_in].reshape(n_in, r_w, ff_in), t)
+    w_parts, da, mixed, in_part = lax.optimization_barrier((w_parts, da, mixed, in_part))
+    w_parts = halves(w_parts.reshape(n_in, rows_dev, width))
+    near = near_in(w_parts[0])
+    near, w_next = lax.optimization_barrier((near, w_parts[1]))
+    w_sum = jnp.concatenate([far_in(w_parts[0], near), far_in(w_next, near_in(w_next))], axis=1)
 
     grad_qkv = dot_tn(n1, da)
-    grad_out = dot_tn(o, dy_all)
 
     def placed(vector, axis):
         spread = jnp.expand_dims(vector, axis)
@@ -703,37 +719,32 @@
         jnp.sum(grad_own, axis=0),
         placed(grad_b_in[0].reshape(n_dp, n_out, r_ff), 1),
     ]
-    vec_grads = jnp.concatenate([v.reshape(n_dp, n_in, n_out, -1) for v in vec_grads], axis=3)
-    vec_grads = jnp.transpose(vec_grads, (0, 2, 1, 3)).reshape(n_g, n_in * r_w, vec_cols)
-    vec_grads = jnp.pad(vec_grads, ((0, 0), (0, 0), (0, 128 - vec_cols)))
+    vec_grads = [v.astype(BF16).reshape(n_dp, n_in, n_out, -1) for v in vec_grads]
+    vec_grads = jnp.stack([jnp.pad(v, ((0, 0), (0, 0), (0, 0), (0, lanes - v.shape[-1]))) for v in vec_grads], axis=3)
+    spare = r_w * per_row - len(vectors)
+    vec_grads = jnp.pad(vec_grads, ((0, 0), (0, 0), (0, 0), (0, spare), (0, 0)))
+    vec_grads = jnp.transpose(vec_grads, (0, 2, 1, 3, 4)).reshape(n_g, n_in * r_w, 128)
     first_grads = jnp.concatenate(
         [
             by_owner(grad_qkv.astype(BF16)),
-            vec_grads.astype(BF16),
-            grad_out.astype(BF16).reshape(n_g, n_in * r_w, cols),
+            vec_grads,
         ],
         axis=2,
     )
     first_grads = lax.psum_scatter(first_grads, G_AXES, scatter_dimension=0, tiled=False)
 
-    in_part = exchange_in(second_grads[:, :ff_in].reshape(n_in, r_w, ff_in), t)
     in_part = in_part.reshape(n_in, r_w, n_dp, n_out, r_ff)
     grad_w_in = jnp.transpose(in_part, (1, 2, 0, 3, 4)).reshape(r_w, ff).astype(F32)
-    grad_w_fc2 = second_grads[:, ff_in:].astype(F32)
+    grad_w_fc2 = second_grads[:, ff_in : ff_in + width].astype(F32)
     back_home = [(b, a) for a, b in home]
-    out_part = first_grads[:, 3 * cols + 128 :].reshape(r_w, width)
+    out_part = second_grads[:, ff_in + width :].reshape(r_w, width)
     grad_w_out = lax.ppermute(out_part, ALL_AXES, back_home).astype(F32)
-    qkv_part = exchange_in(first_grads[:, : 3 * cols + 128].reshape(n_in, r_w, 3 * cols + 128), t)
+    qkv_part = exchange_in(first_grads.reshape(n_in, r_w, 3 * cols + 128), t)
     qkv_grad = jnp.transpose(qkv_part[:, :, : 3 * cols].reshape(n_in, r_w, 3, cols), (1, 2, 0, 3))
     grad_w_qkv = qkv_grad.reshape(r_w, 3 * width).astype(F32)
-    vec_part = qkv_part[:, :, 3 * cols : 3 * cols + vec_cols].reshape(n_in, n_vec).astype(F32)
-    vec_part = jnp.sum(vec_part, axis=0)
-    vec_out, at = [], 0
-    for size in sizes:
-        vec_out.append(vec_part[at : at + size])
-        at += size
-
-    w_sum = scatter_in(w_parts.reshape(n_in, rows_dev, width))
+    vec_part = jnp.sum(qkv_part[:, :, 3 * cols :].astype(F32), axis=0).reshape(r_w * per_row, lanes)
+    vec_out = [vec_part[i, :size] for i, size in enumerate(sizes)]
+
     centred = own - jnp.mean(own, axis=-1, keepdims=True)
     own_rstd = lax.rsqrt(jnp.mean(centred * centred, axis=-1, keepdims=True) + EPS)
     own_hat = centred * own_rstd

time: 436 us -> 390 us (0.89)
  waiting for transfers between devices: 177 us -> 118 us
  local copies, waits for them, and re-layouts: 60.7 us -> 43.3 us
  Pallas kernels: 95.9 us -> 113 us
  other arithmetic: 32.7 us -> 40.6 us
    ppermute x39 -> x37, waiting for transfers between devices: 177 us -> 118 us  [xor_swap(): return lax.ppermute(value, axis, [(i, i ^ step) for i in range(size)])]
    unnamed x104 -> x74, local copies, waits for them, and re-layouts: 21.6 us -> 4.21 us
    concatenate x2 -> x0, local copies, waits for them, and re-layouts: 4.9 us -> none  [the longest x1 4.76 us: body(): jnp.concatenate(vectors).reshape(r_w, vec_cols)]
    ppermute x39 -> x37, starting transfers between devices: 40.8 us -> 40.5 us  [xor_swap(): return lax.ppermute(value, axis, [(i, i ^ step) for i in range(size)])]
  transfers between devices with their start and end apart: 45 -> 43, of which waited for: 16 -> 18; matrix products, arithmetic and copies ran while one was open for 12% -> 16% of each run, Pallas kernels for 18% -> 24%
where the time goes in v1:
time: 390 us; the launch traced here: 389 us
  waiting for transfers between devices  118 us (30%)
  Pallas kernels  113 us (29%)
  local copies, waits for them, and re-layouts  43.3 us (11%)
  starting transfers between devices  42.4 us (11%)
  other arithmetic  40.6 us (10%)
  matrix products  16.7 us (4%)
  between operations  14.6 us (4%)
    ppermute x37, waiting for transfers between devices, xor_swap(): return lax.ppermute(value, axis, [(i, i ^ step) for i in range(size)])  118 us
    ppermute x37, starting transfers between devices, xor_swap(): return lax.ppermute(value, axis, [(i, i ^ step) for i in range(size)])  40.5 us
    pallas_call x1, Pallas kernels, attend_backward(): pl.pallas_call(functools.partial(backward_kernel, block, ends.shape[0]),...  37.6 us
    pallas_call x1, Pallas kernels, attend_forward(): pl.pallas_call(functools.partial(forward_kernel, block, ends.shape[0]), i...  35.7 us
    pallas_call x1, Pallas kernels, feed(): pl.pallas_call(feed_kernel, grid=(rows // TILE,), in_specs=[tile, tile, t...  15.2 us
    dot_general x4, matrix products, dot_tn(): lax.dot_general(a, b, (((0,), (0,)), ((), ())), preferred_element_type=F32)  12.2 us
    pallas_call x1, Pallas kernels, prep(): pl.pallas_call(functools.partial(prep_kernel, heads, block), grid_spec=pl...  8.48 us
    pallas_call x1, Pallas kernels, post(): pl.pallas_call(functools.partial(post_kernel, heads, block), grid_spec=pl...  8.45 us
  transfers between devices with their start and end apart: 43, of which 18 were waited for; matrix products, arithmetic and copies ran while one was open for 16% of the time, Pallas kernels for 24%

profile of v1, /device:TPU:0, one launch (start us, length us, event | category | flops | bytes accessed | tf_op | source)
XLA Modules:
  0.0 388.8 jit_solution(7413245724292376558)
XLA Ops:
  10.4 5.1 %collective-permute-start.2 = (bf16[32,1920]{1,0:T(8,128)(2,1)S(1)}, bf16[32,1920]{1,0:T(8,128)(2,1)S(1)}, u32[]{:S(2)}, u32[]{:S(2)}) collective-permute-start(bf16[32,1920]{1,0:T(8,128)(2,1)S(1)} %get-tuple-element.152), channel_id=1, source_target_pairs={{0,12},{4,8},{8,4},{12,0},{1,13},{5,9},{9,5},{13,1},{2,14},{6,10},... | collective-permute-start | bytes 368648 | tf_op jit(solution)/shard_map/ppermute | solution.py:37
  19.8 8.2 %collective-permute-done.1 = bf16[32,1920]{1,0:T(8,128)(2,1)S(1)} collective-permute-done((bf16[32,1920]{1,0:T(8,128)(2,1)S(1)}, bf16[32,1920]{1,0:T(8,128)(2,1)S(1)}, u32[]{:S(2)}, u32[]{:S(2)}) %collective-permute-start.1) | collective-permute-done | bytes 122912 | tf_op jit(solution)/shard_map/ppermute | solution.py:37
  32.1 22.6 %collective-permute-done.4 = bf16[256,1024]{1,0:T(8,128)(2,1)S(1)} collective-permute-done((bf16[256,1024]{1,0:T(8,128)(2,1)S(1)}, bf16[256,1024]{1,0:T(8,128)(2,1)S(1)}, u32[]{:S(2)}, u32[]{:S(2)}) %collective-permute-start.4) | collective-permute-done | bytes 524320 | tf_op jit(solution)/shard_map/ppermute | solution.py:37
  60.7 19.1 %collective-permute-done.5 = bf16[2,256,1024]{2,1,0:T(8,128)(2,1)S(1)} collective-permute-done((bf16[2,256,1024]{2,1,0:T(8,128)(2,1)}, bf16[2,256,1024]{2,1,0:T(8,128)(2,1)S(1)}, u32[]{:S(2)}, u32[]{:S(2)}) %collective-permute-start.5) | collective-permute-done | bytes 1048608 | tf_op jit(solution)/shard_map/ppermute | solution.py:37
  89.1 8.5 %shard_map.246 = (bf16[4,1024,128]{2,1,0:T(8,128)(2,1)}, bf16[4,512,128]{2,1,0:T(8,128)(2,1)}, bf16[1024,1024]{1,0:T(8,128)(2,1)}, bf16[1024,1024]{1,0:T(8,128)(2,1)}) custom-call(s32[1]{0:T(128)} %bitcast.z_ref, bf16[1024,1024]{1,0:T(8,128)(2,1)} %bitcast.199, f32[8,1024]{1,0:T(8,128)} %concatenate.23.norm_ref, bf16[1024,768]{1,0:T(8,128)(2,1)} %bitcast.208, ...), custom_call_target="tpu_custom_call" | custom-call | flops 1610612736 | bytes 12582912 | tf_op jit(solution)/shard_map/pallas_call | solution.py:105
  114.7 4.1 %collective-permute-done.7 = bf16[1024,128]{1,0:T(8,128)(2,1)} collective-permute-done((bf16[1024,128]{1,0:T(8,128)(2,1)S(1)}, bf16[1024,128]{1,0:T(8,128)(2,1)}, u32[]{:S(2)}, u32[]{:S(2)}) %collective-permute-start.7) | collective-permute-done | bytes 262176 | tf_op jit(solution)/shard_map/ppermute | solution.py:37
  122.8 35.7 %shard_map.247 = (bf16[2048,128]{1,0:T(8,128)(2,1)}, f32[64,4096]{1,0:T(8,128)}, f32[1,4096]{1,0:T(1,128)}) custom-call(s32[64]{0:T(128)} %fusion.19.source_ref, s32[64]{0:T(128)} %copy-done.26, s32[4]{0:T(128)} %bitcast.272, bf16[4096,128]{1,0:T(8,128)(2,1)} %bitcast.234, bf16[2048,128]{1,0:T(8,128)(2,1)} %bitcast.239), custom_call_target="tpu_custom_call" | custom-call | flops 42949672960 | bytes 3145728 | tf_op jit(solution)/shard_map/pallas_call | solution.py:478
  162.1 4.4 %shard_map.248 = bf16[4,512,128]{2,1,0:T(8,128)(2,1)} custom-call(s32[1]{0:T(128)} %bitcast.z_ref, bf16[1024,1024]{1,0:T(8,128)(2,1)} %bitcast.190, bf16[256,1024]{1,0:T(8,128)(2,1)} %reshape.392.wo_ref), custom_call_target="tpu_custom_call" | custom-call | flops 536870912 | bytes 4194304 | tf_op jit(solution)/shard_map/pallas_call | solution.py:208
  177.3 4.0 %fusion.32 = (bf16[8,128,1024]{2,1,0:T(8,128)(2,1)}, bf16[8,128,1024]{2,1,0:T(8,128)(2,1)S(1)}) fusion(bf16[8,128,2048]{2,1,0:T(8,128)(2,1)} %bitcast.210), kind=kLoop, calls=%fused_computation.186 | loop fusion | bytes 8388608 | tf_op jit(solution)/shard_map/slice | solution.py:645
  183.0 15.2 %shard_map.249 = (bf16[1024,1024]{1,0:T(8,128)(2,1)}, bf16[1024,1024]{1,0:T(8,128)(2,1)}, f32[1024,1024]{1,0:T(8,128)}, f32[1024,1024]{1,0:T(8,128)}, f32[8,1024]{1,0:T(8,128)}, /*index=5*/f32[8,1024]{1,0:T(8,128)}) custom-call(bf16[1024,1024]{1,0:T(8,128)(2,1)} %bitcast.200, bf16[1024,1024]{1,0:T(8,128)(2,1)} %get-tuple-element.66.n2_ref, ...), custom_call_target="tpu_custom_call" | custom-call | flops 8589934592 | bytes 25165824 | tf_op jit(solution)/shard_map/pallas_call | solution.py:166
  198.2 4.0 %convolution_convert_fusion.1 = bf16[1024,1024]{1,0:T(8,128)(2,1)S(1)} fusion(bf16[1024,1024]{1,0:T(8,128)(2,1)S(1)} %copy-done.32, bf16[1024,1024]{1,0:T(8,128)(2,1)} %get-tuple-element.67), kind=kOutput, calls=%fused_computation.5 | convolution fusion | flops 2148532224 | bytes 6291456 | tf_op jit(solution)/shard_map/dot_general | solution.py:33
  203.7 3.5 shard_map.250
  209.8 4.4 %add_convert_fusion = bf16[1024,1024]{1,0:T(8,128)(2,1)} fusion(f32[1024,1024]{1,0:T(8,128)} %get-tuple-element.72, bf16[1024,256]{1,0:T(8,128)(2,1)S(1)} %copy-done.5, bf16[256,1024]{1,0:T(8,128)(2,1)S(1)} %copy-done.4), kind=kOutput, calls=%fused_computation.1 | convolution fusion | flops 538968064 | bytes 7340032 | tf_op jit(solution)/shard_map/dot_general | solution.py:25
  214.3 3.7 convolution_convert_fusion
  218.3 3.9 %pad_maximum_fusion = bf16[8,128,2304]{2,1,0:T(8,128)(2,1)} fusion(bf16[8,128,256]{2,1,0:T(8,128)(2,1)S(1)} %reshape.400, bf16[8,128,1024]{2,1,0:T(8,128)(2,1)} %bitcast.223, bf16[8,128,1024]{2,1,0:T(8,128)(2,1)} %bitcast.202), kind=kLoop, calls=%fused_computation | loop fusion | flops 14155776 | bytes 9437184 | tf_op jit(solution)/shard_map/concatenate | solution.py:677
  225.2 37.6 %shard_map.251 = (bf16[4096,128]{1,0:T(8,128)(2,1)}, bf16[2048,128]{1,0:T(8,128)(2,1)}) custom-call(s32[64]{0:T(128)} %fusion.19.source_ref, s32[64]{0:T(128)} %copy-done.26, s32[4]{0:T(128)} %bitcast.273, bf16[4096,128]{1,0:T(8,128)(2,1)} %bitcast.235, bf16[2048,128]{1,0:T(8,128)(2,1)} %bitcast.240, bf16[2048,128]{1,0:T(8,128)(2,1)} %bitcast.241, ...), custom_call_target="tpu_custom_call" | custom-call | flops 42949672960 | bytes 6291456 | tf_op jit(solution)/shard_map/pallas_call | solution.py:496
  270.1 3.5 collective-permute-done.26
  275.6 12.6 %collective-permute-done.25 = bf16[512,128]{1,0:T(8,128)(2,1)S(1)} collective-permute-done((bf16[512,128]{1,0:T(8,128)(2,1)S(1)}, bf16[512,128]{1,0:T(8,128)(2,1)S(1)}, u32[]{:S(2)}, u32[]{:S(2)}) %collective-permute-start.25) | collective-permute-done | bytes 131104 | tf_op jit(solution)/shard_map/ppermute | solution.py:37
  292.7 8.4 %shard_map.252 = (bf16[1024,768]{1,0:T(8,128)(2,1)}, bf16[1024,1024]{1,0:T(8,128)(2,1)}, f32[8,1024]{1,0:T(8,128)}, f32[8,768]{1,0:T(8,128)}) custom-call(s32[1]{0:T(128)} %bitcast.z_ref, bf16[4,1024,128]{2,1,0:T(8,128)(2,1)} %pad_maximum_fusion.8.dqk_ref, bf16[4,512,128]{2,1,0:T(8,128)(2,1)} %pad_maximum_fusion.14.dv_ref, bf16[1024,1024]{1,0:T(8,128)(2,1)} %bitcast.201, ...), custom_call_target="tpu_custom_call" | custom-call | flops 1610612736 | bytes 14680064 | tf_op jit(solution)/shard_map/pallas_call | solution.py:280
  309.9 8.4 %collective-permute-done.27 = bf16[256,1024]{1,0:T(8,128)(2,1)} collective-permute-done((bf16[256,1024]{1,0:T(8,128)(2,1)}, bf16[256,1024]{1,0:T(8,128)(2,1)}, u32[]{:S(2)}, u32[]{:S(2)}) %collective-permute-start.27) | collective-permute-done | bytes 524320 | tf_op jit(solution)/shard_map/ppermute | solution.py:37
  327.7 6.8 %collective-permute-done.31 = bf16[2,256,512]{2,1,0:T(8,128)(2,1)} collective-permute-done((bf16[2,256,512]{2,1,0:T(8,128)(2,1)S(1)}, bf16[2,256,512]{2,1,0:T(8,128)(2,1)}, u32[]{:S(2)}, u32[]{:S(2)}) %collective-permute-start.31) | collective-permute-done | bytes 524320 | tf_op jit(solution)/shard_map/ppermute | solution.py:37
  340.0 4.6 %collective-permute-start.32 = (bf16[256,512]{1,0:T(8,128)(2,1)}, bf16[256,512]{1,0:T(8,128)(2,1)}, u32[]{:S(2)}, u32[]{:S(2)}) collective-permute-start(bf16[256,512]{1,0:T(8,128)(2,1)} %fusion.15), channel_id=1, source_target_pairs={{0,8},{4,12},{8,0},{12,4},{1,9},{5,13},{9,1},{13,5},{2,10},{6,14},... | collective-permute-start | bytes 786440 | tf_op jit(solution)/shard_map/ppermute | solution.py:37
  344.6 10.0 %collective-permute-done.33 = bf16[2,256,512]{2,1,0:T(8,128)(2,1)S(1)} collective-permute-done((bf16[2,256,512]{2,1,0:T(8,128)(2,1)S(1)}, bf16[2,256,512]{2,1,0:T(8,128)(2,1)S(1)}, u32[]{:S(2)}, u32[]{:S(2)}) %collective-permute-start.33) | collective-permute-done | bytes 524320 | tf_op jit(solution)/shard_map/ppermute | solution.py:37
  358.8 10.3 %collective-permute-done.34 = bf16[256,512]{1,0:T(8,128)(2,1)} collective-permute-done((bf16[256,512]{1,0:T(8,128)(2,1)S(1)}, bf16[256,512]{1,0:T(8,128)(2,1)}, u32[]{:S(2)}, u32[]{:S(2)}) %collective-permute-start.34) | collective-permute-done | bytes 262176 | tf_op jit(solution)/shard_map/ppermute | solution.py:37
  (298 shorter events, 125.4 us)
Async XLA Ops:
  7.3 76.2 %all-gather.5.cloned.1.call-start = ((), (), s32[]{:S(2)}) async-start(), calls=%async_computation.4 | async-start | bytes 2654208 | tf_op jit(solution)/shard_map/all_gather | solution.py:630
  15.5 12.5 %collective-permute-start.1 = (bf16[32,1920]{1,0:T(8,128)(2,1)S(1)}, bf16[32,1920]{1,0:T(8,128)(2,1)S(1)}, u32[]{:S(2)}, u32[]{:S(2)}) collective-permute-start(bf16[32,1920]{1,0:T(8,128)(2,1)S(1)} %get-tuple-element.153), channel_id=1, source_target_pairs={{0,8},{4,12},{8,0},{12,4},{1,9},{5,13},{9,1},{13,5},{2,10},{6,14},... | collective-permute-start | bytes 368648 | tf_op jit(solution)/shard_map/ppermute | solution.py:37
  29.0 148.2 %all-gather.7.cloned.1.call-start = ((), (), s32[]{:S(2)}) async-start(), calls=%async_computation.5 | async-start | bytes 4718592 | tf_op jit(solution)/shard_map/all_gather | solution.py:632
  30.3 24.4 %collective-permute-start.4 = (bf16[256,1024]{1,0:T(8,128)(2,1)S(1)}, bf16[256,1024]{1,0:T(8,128)(2,1)S(1)}, u32[]{:S(2)}, u32[]{:S(2)}) collective-permute-start(bf16[256,1024]{1,0:T(8,128)(2,1)S(1)} %copy-done.1), channel_id=1, source_target_pairs={{0,8},{4,12},{8,0},{12,4},{1,9},{5,13},{9,1},{13,5},{2,10},{6,14},... | collective-permute-start | bytes 1572872 | tf_op jit(solution)/shard_map/ppermute | solution.py:37
  55.8 24.0 %collective-permute-start.5 = (bf16[2,256,1024]{2,1,0:T(8,128)(2,1)}, bf16[2,256,1024]{2,1,0:T(8,128)(2,1)S(1)}, u32[]{:S(2)}, u32[]{:S(2)}) collective-permute-start(bf16[2,256,1024]{2,1,0:T(8,128)(2,1)} %pad_maximum_fusion.4), channel_id=1, source_target_pairs={{0,4},{4,0},{8,12},{12,8},{1,5},{5,1},{9,13},{13,9},{2,6},{6,2},{1... | collective-permute-start | bytes 3145736 | tf_op jit(solution)/shard_map/ppermute | solution.py:37
  60.4 243.0 %reduce-scatter.3.cloned.1.call-start = ((), (), s32[]{:S(2)}) async-start(), calls=%async_computation.2 | async-start | bytes 5308416 | tf_op jit(solution)/shard_map/reduce_scatter | solution.py:687
  81.5 39.4 %collective-permute-start.12 = (bf16[256,1024]{1,0:T(8,128)(2,1)S(1)}, bf16[256,1024]{1,0:T(8,128)(2,1)S(1)}, u32[]{:S(2)}, u32[]{:S(2)}) collective-permute-start(bf16[256,1024]{1,0:T(8,128)(2,1)S(1)} %copy-done.3), channel_id=1, source_target_pairs={{0,8},{4,12},{8,0},{12,4},{1,9},{5,13},{9,1},{13,5},{2,10},{6,14},... | collective-permute-start | bytes 1572872 | tf_op jit(solution)/shard_map/ppermute | solution.py:37
  103.7 15.0 %collective-permute-start.7 = (bf16[1024,128]{1,0:T(8,128)(2,1)S(1)}, bf16[1024,128]{1,0:T(8,128)(2,1)}, u32[]{:S(2)}, u32[]{:S(2)}) collective-permute-start(bf16[1024,128]{1,0:T(8,128)(2,1)S(1)} %get-tuple-element.123), channel_id=1, source_target_pairs={{0,2},{1,3},{2,0},{3,1},{4,6},{5,7},{6,4},{7,5},{8,10},{9,11},{10,... | collective-permute-start | bytes 786440 | tf_op jit(solution)/shard_map/ppermute | solution.py:37
  104.6 14.2 %collective-permute-start.6 = (bf16[1024,128]{1,0:T(8,128)(2,1)S(1)}, bf16[1024,128]{1,0:T(8,128)(2,1)}, u32[]{:S(2)}, u32[]{:S(2)}) collective-permute-start(bf16[1024,128]{1,0:T(8,128)(2,1)S(1)} %get-tuple-element.124), channel_id=1, source_target_pairs={{0,1},{1,0},{2,3},{3,2},{4,5},{5,4},{6,7},{7,6},{8,9},{9,8},{10,11... | collective-permute-start | bytes 786440 | tf_op jit(solution)/shard_map/ppermute | solution.py:37
  121.0 37.5 %collective-permute-start.13 = (bf16[2,256,1024]{2,1,0:T(8,128)(2,1)S(1)}, bf16[2,256,1024]{2,1,0:T(8,128)(2,1)S(1)}, u32[]{:S(2)}, u32[]{:S(2)}) collective-permute-start(bf16[2,256,1024]{2,1,0:T(8,128)(2,1)S(1)} %pad_maximum_fusion.6), channel_id=1, source_target_pairs={{0,4},{4,0},{8,12},{12,8},{1,5},{5,1},{9,13},{13,9},{2,6},{6,2},{1... | collective-permute-start | bytes 3145736 | tf_op jit(solution)/shard_map/ppermute | solution.py:37
  222.3 148.4 %reduce-scatter.5.cloned.1.call-start = ((), (), s32[]{:S(2)}) async-start(), calls=%async_computation.3 | async-start | bytes 2064384 | tf_op jit(solution)/shard_map/reduce_scatter | solution.py:734
  225.0 38.9 %collective-permute-start.20 = (bf16[2,256,1024]{2,1,0:T(8,128)(2,1)}, bf16[2,256,1024]{2,1,0:T(8,128)(2,1)}, u32[]{:S(2)}, u32[]{:S(2)}) collective-permute-start(bf16[2,256,1024]{2,1,0:T(8,128)(2,1)} %pad_maximum_fusion.7), channel_id=1, source_target_pairs={{0,4},{4,0},{8,12},{12,8},{1,5},{5,1},{9,13},{13,9},{2,6},{6,2},{1... | collective-permute-start | bytes 3145736 | tf_op jit(solution)/shard_map/ppermute | solution.py:37
  266.3 25.3 %collective-permute-start.23 = (bf16[1024,128]{1,0:T(8,128)(2,1)S(1)}, bf16[1024,128]{1,0:T(8,128)(2,1)S(1)}, u32[]{:S(2)}, u32[]{:S(2)}) collective-permute-start(bf16[1024,128]{1,0:T(8,128)(2,1)S(1)} %get-tuple-element.116), channel_id=1, source_target_pairs={{0,3},{1,2},{2,1},{3,0},{4,7},{5,6},{6,5},{7,4},{8,11},{9,10},{10,... | collective-permute-start | bytes 786440 | tf_op jit(solution)/shard_map/ppermute | solution.py:37
  268.1 23.5 %collective-permute-start.22 = (bf16[1024,128]{1,0:T(8,128)(2,1)S(1)}, bf16[1024,128]{1,0:T(8,128)(2,1)S(1)}, u32[]{:S(2)}, u32[]{:S(2)}) collective-permute-start(bf16[1024,128]{1,0:T(8,128)(2,1)S(1)} %get-tuple-element.117), channel_id=1, source_target_pairs={{0,2},{1,3},{2,0},{3,1},{4,6},{5,7},{6,4},{7,5},{8,10},{9,11},{10,... | collective-permute-start | bytes 786440 | tf_op jit(solution)/shard_map/ppermute | solution.py:37
  268.2 23.4 %collective-permute-start.21 = (bf16[1024,128]{1,0:T(8,128)(2,1)S(1)}, bf16[1024,128]{1,0:T(8,128)(2,1)S(1)}, u32[]{:S(2)}, u32[]{:S(2)}) collective-permute-start(bf16[1024,128]{1,0:T(8,128)(2,1)S(1)} %get-tuple-element.118), channel_id=1, source_target_pairs={{0,1},{1,0},{2,3},{3,2},{4,5},{5,4},{6,7},{7,6},{8,9},{9,8},{10,11... | collective-permute-start | bytes 786440 | tf_op jit(solution)/shard_map/ppermute | solution.py:37
  268.3 19.9 %collective-permute-start.25 = (bf16[512,128]{1,0:T(8,128)(2,1)S(1)}, bf16[512,128]{1,0:T(8,128)(2,1)S(1)}, u32[]{:S(2)}, u32[]{:S(2)}) collective-permute-start(bf16[512,128]{1,0:T(8,128)(2,1)S(1)} %get-tuple-element.133), channel_id=1, source_target_pairs={{0,2},{1,3},{2,0},{3,1},{4,6},{5,7},{6,4},{7,5},{8,10},{9,11},{10,... | collective-permute-start | bytes 393224 | tf_op jit(solution)/shard_map/ppermute | solution.py:37
  273.6 17.1 %collective-permute-start.24 = (bf16[512,128]{1,0:T(8,128)(2,1)S(1)}, bf16[512,128]{1,0:T(8,128)(2,1)S(1)}, u32[]{:S(2)}, u32[]{:S(2)}) collective-permute-start(bf16[512,128]{1,0:T(8,128)(2,1)S(1)} %get-tuple-element.134), channel_id=1, source_target_pairs={{0,1},{1,0},{2,3},{3,2},{4,5},{5,4},{6,7},{7,6},{8,9},{9,8},{10,11... | collective-permute-start | bytes 393224 | tf_op jit(solution)/shard_map/ppermute | solution.py:37
  288.2 30.0 %collective-permute-start.27 = (bf16[256,1024]{1,0:T(8,128)(2,1)}, bf16[256,1024]{1,0:T(8,128)(2,1)}, u32[]{:S(2)}, u32[]{:S(2)}) collective-permute-start(bf16[256,1024]{1,0:T(8,128)(2,1)} %fusion.14), channel_id=1, source_target_pairs={{0,8},{4,12},{8,0},{12,4},{1,9},{5,13},{9,1},{13,5},{2,10},{6,14},... | collective-permute-start | bytes 1572872 | tf_op jit(solution)/shard_map/ppermute | solution.py:37
  305.4 15.3 %collective-permute-start.30 = (bf16[32,1024]{1,0:T(8,128)(2,1)S(1)}, bf16[32,1024]{1,0:T(8,128)(2,1)S(1)}, u32[]{:S(2)}, u32[]{:S(2)}) collective-permute-start(bf16[32,1024]{1,0:T(8,128)(2,1)S(1)} %get-tuple-element.160), channel_id=1, source_target_pairs={{0,12},{4,8},{8,4},{12,0},{1,13},{5,9},{9,5},{13,1},{2,14},{6,10},... | collective-permute-start | bytes 196616 | tf_op jit(solution)/shard_map/ppermute | solution.py:37
  306.8 13.9 %collective-permute-start.29 = (bf16[32,1024]{1,0:T(8,128)(2,1)S(1)}, bf16[32,1024]{1,0:T(8,128)(2,1)S(1)}, u32[]{:S(2)}, u32[]{:S(2)}) collective-permute-start(bf16[32,1024]{1,0:T(8,128)(2,1)S(1)} %get-tuple-element.161), channel_id=1, source_target_pairs={{0,8},{4,12},{8,0},{12,4},{1,9},{5,13},{9,1},{13,5},{2,10},{6,14},... | collective-permute-start | bytes 196616 | tf_op jit(solution)/shard_map/ppermute | solution.py:37
  334.7 20.0 %collective-permute-start.33 = (bf16[2,256,512]{2,1,0:T(8,128)(2,1)S(1)}, bf16[2,256,512]{2,1,0:T(8,128)(2,1)S(1)}, u32[]{:S(2)}, u32[]{:S(2)}) collective-permute-start(bf16[2,256,512]{2,1,0:T(8,128)(2,1)S(1)} %pad_maximum_fusion.16), channel_id=1, source_target_pairs={{0,4},{4,0},{8,12},{12,8},{1,5},{5,1},{9,13},{13,9},{2,6},{6,2},{1... | collective-permute-start | bytes 1572872 | tf_op jit(solution)/shard_map/ppermute | solution.py:37
  337.2 19.6 %collective-permute-start.38 = (bf16[32,1024]{1,0:T(8,128)(2,1)S(1)}, bf16[32,1024]{1,0:T(8,128)(2,1)S(1)}, u32[]{:S(2)}, u32[]{:S(2)}) collective-permute-start(bf16[32,1024]{1,0:T(8,128)(2,1)S(1)} %reshape.408), channel_id=1, source_target_pairs={{0,0},{1,1},{2,2},{3,3},{16,4},{17,5},{18,6},{19,7},{4,8},{5,9},{6... | collective-permute-start | bytes 196616 | tf_op jit(solution)/shard_map/ppermute | solution.py:741
  340.0 17.5 %collective-permute-start.32 = (bf16[256,512]{1,0:T(8,128)(2,1)}, bf16[256,512]{1,0:T(8,128)(2,1)}, u32[]{:S(2)}, u32[]{:S(2)}) collective-permute-start(bf16[256,512]{1,0:T(8,128)(2,1)} %fusion.15), channel_id=1, source_target_pairs={{0,8},{4,12},{8,0},{12,4},{1,9},{5,13},{9,1},{13,5},{2,10},{6,14},... | collective-permute-start | bytes 786440 | tf_op jit(solution)/shard_map/ppermute | solution.py:37
  354.7 14.4 %collective-permute-start.34 = (bf16[256,512]{1,0:T(8,128)(2,1)S(1)}, bf16[256,512]{1,0:T(8,128)(2,1)}, u32[]{:S(2)}, u32[]{:S(2)}) collective-permute-start(bf16[256,512]{1,0:T(8,128)(2,1)S(1)} %fusion.16), channel_id=1, source_target_pairs={{0,8},{4,12},{8,0},{12,4},{1,9},{5,13},{9,1},{13,5},{2,10},{6,14},... | collective-permute-start | bytes 786440 | tf_op jit(solution)/shard_map/ppermute | solution.py:37
  (53 other events, 360.0 us)
Sparse Core Ops, SparseCore 0:
  29.2 29.1 all-gather.4
  60.6 36.4 all-gather.6
  222.4 54.3 reduce-scatter.2
  326.6 38.2 reduce-scatter.4

commit v2 on v1

--- a/solution.py
+++ b/solution.py
@@ -13,6 +13,8 @@
 LONGEST = 2048
 GROUP_IN = 4
 TILE = 256
+FQ, FK = 512, 512
+BQ, BK = 512, 256
 EPS = 1e-05
 NEG = -1e30
 F32 = jnp.float32
@@ -70,8 +72,12 @@
     return (0, 0)
 
 
-def slab_at(i, z):
-    return (0, i, 0)
+def piece(size):
+    return pl.BlockSpec((size, 2 * HEAD), row_at)
+
+
+def bf16_rows(rows):
+    return jax.ShapeDtypeStruct((rows, 2 * HEAD), BF16)
 
 
 def normalized(x_ref):
@@ -80,7 +86,17 @@
     return centred * lax.rsqrt(jnp.mean(centred * centred, axis=-1, keepdims=True) + EPS)
 
 
-def prep_kernel(heads, block, z_ref, x_ref, norm_ref, w_ref, b_ref, cos_ref, sl_ref, sr_ref, qk_ref, v_ref, n1_ref, n2_ref):
+def turn(z, parts):
+    out = []
+    for step in range(len(parts)):
+        pick = parts[step]
+        for at in range(1, len(parts)):
+            pick = jnp.where(z == at, parts[at ^ step], pick)
+        out.append(pick)
+    return out
+
+
+def prep_kernel(heads, block, z_ref, x_ref, norm_ref, w_ref, b_ref, cos_ref, sl_ref, sr_ref, n1_ref, n2_ref, *out_refs):
     z = z_ref[0]
     xhat = normalized(x_ref)
     n1 = (xhat * norm_ref[0:1] + norm_ref[1:2]).astype(BF16)
@@ -89,11 +105,14 @@
     joined = dot(n1, w_ref[...]) + b_ref[...]
     cos, sl, sr = cos_ref[...], sl_ref[...], sr_ref[...]
     cols = heads * HEAD
+    qk, v = [], []
     for h in range(heads):
         at = h * HEAD
         part = jnp.concatenate([joined[:, at : at + HEAD], joined[:, cols + at : cols + at + HEAD]], axis=1)
-        qk_ref[z ^ h] = rotary(part, cos, sl, sr, 1.0).astype(BF16)
-        v_ref[z ^ h] = pair_up(joined[:, 2 * cols + at : 2 * cols + at + HEAD], block).astype(BF16)
+        qk.append(rotary(part, cos, sl, sr, 1.0))
+        v.append(pair_up(joined[:, 2 * cols + at : 2 * cols + at + HEAD], block))
+    for ref, part in zip(out_refs, turn(z, qk) + turn(z, v)):
+        ref[...] = part.astype(BF16)
 
 
 def prep(z, x, norms, w, bias, cos, sl, sr, block):
@@ -116,19 +135,9 @@
                 table,
                 table,
             ],
-            out_specs=[
-                pl.BlockSpec((heads, TILE, 2 * HEAD), slab_at),
-                pl.BlockSpec((heads, TILE // 2, 2 * HEAD), slab_at),
-                tile,
-                tile,
-            ],
+            out_specs=[tile, tile] + [piece(TILE)] * heads + [piece(TILE // 2)] * heads,
         ),
-        out_shape=[
-            jax.ShapeDtypeStruct((heads, rows, 2 * HEAD), BF16),
-            jax.ShapeDtypeStruct((heads, rows // 2, 2 * HEAD), BF16),
-            norm,
-            norm,
-        ],
+        out_shape=[norm, norm] + [bf16_rows(rows)] * heads + [bf16_rows(rows // 2)] * heads,
         **params(2 * rows * width * w.shape[1], 12 * 2**20),
     )(z, x, norms, w, bias, cos, sl, sr)
 
@@ -195,11 +204,11 @@
     )(x, n2, dy, norms, w_in, w_fc2, bias)
 
 
-def grad_att_kernel(heads, block, z_ref, dy_ref, wo_ref, do_ref):
-    z = z_ref[0]
+def grad_att_kernel(heads, block, z_ref, dy_ref, wo_ref, *out_refs):
     grad = dot_nt(dy_ref[...], wo_ref[...])
-    for h in range(heads):
-        do_ref[z ^ h] = pair_up(grad[:, h * HEAD : (h + 1) * HEAD], block).astype(BF16)
+    parts = [pair_up(grad[:, h * HEAD : (h + 1) * HEAD], block) for h in range(heads)]
+    for ref, part in zip(out_refs, turn(z_ref[0], parts)):
+        ref[...] = part.astype(BF16)
 
 
 def grad_att(z, dy, wo, block):
@@ -211,49 +220,57 @@
             num_scalar_prefetch=1,
             grid=(rows // TILE,),
             in_specs=[pl.BlockSpec((TILE, width), row_at), pl.BlockSpec(wo.shape, whole_at)],
-            out_specs=pl.BlockSpec((heads, TILE // 2, 2 * HEAD), slab_at),
+            out_specs=[piece(TILE // 2)] * heads,
         ),
-        out_shape=jax.ShapeDtypeStruct((heads, rows // 2, 2 * HEAD), BF16),
+        out_shape=[bf16_rows(rows // 2)] * heads,
         **params(2 * rows * width * wo.shape[0], 4 * 2**20),
     )(z, dy, wo)
 
 
-def merge_heads_kernel(heads, block, z_ref, part_ref, o_ref):
-    z = z_ref[0]
+def project_kernel(heads, block, z_ref, y_ref, wo_ref, *refs):
+    parts = turn(z_ref[0], [unpair(ref[...].astype(F32), block) for ref in refs[:heads]])
+    o_ref, out_ref = refs[heads:]
     for h in range(0, heads, 2):
-        one, two = unpair(part_ref[z ^ h].astype(F32), block), unpair(part_ref[z ^ (h + 1)].astype(F32), block)
-        o_ref[:, h * HEAD : (h + 2) * HEAD] = jnp.concatenate([one, two], axis=1).astype(BF16)
-
-
-def merge_heads(z, parts, block):
-    heads, half_rows, _ = parts.shape
+        o_ref[:, h * HEAD : (h + 2) * HEAD] = jnp.concatenate(parts[h : h + 2], axis=1).astype(BF16)
+    out_ref[...] = (y_ref[...] + dot(o_ref[...], wo_ref[...])).astype(BF16)
+
+
+def project(z, parts, y, wo, block):
+    heads = len(parts)
+    rows, width = y.shape
+    tile = pl.BlockSpec((TILE, width), row_at)
     return pl.pallas_call(
-        functools.partial(merge_heads_kernel, heads, block),
+        functools.partial(project_kernel, heads, block),
         grid_spec=pltpu.PrefetchScalarGridSpec(
             num_scalar_prefetch=1,
-            grid=(2 * half_rows // TILE,),
-            in_specs=[pl.BlockSpec((heads, TILE // 2, 2 * HEAD), slab_at)],
-            out_specs=pl.BlockSpec((TILE, heads * HEAD), row_at),
+            grid=(rows // TILE,),
+            in_specs=[tile, pl.BlockSpec(wo.shape, whole_at)] + [piece(TILE // 2)] * heads,
+            out_specs=[pl.BlockSpec((TILE, heads * HEAD), row_at), tile],
         ),
-        out_shape=jax.ShapeDtypeStruct((2 * half_rows, heads * HEAD), BF16),
-        **params(half_rows * 1024, 2**20),
-    )(z, parts)
+        out_shape=[
+            jax.ShapeDtypeStruct((rows, heads * HEAD), BF16),
+            jax.ShapeDtypeStruct((rows, width), BF16),
+        ],
+        **params(2 * rows * width * wo.shape[0], 8 * 2**20),
+    )(z, y, wo, *parts)
 
 
 def post_kernel(
-    heads, block, z_ref, dqk_ref, dv_ref, x_ref, dx_ref, norm_ref, w_ref, cos_ref, sl_ref, sr_ref, da_ref, sum_ref, sums_ref, db_ref
+    heads, block, z_ref, x_ref, dx_ref, norm_ref, w_ref, cos_ref, sl_ref, sr_ref, *refs
 ):
     z = z_ref[0]
+    dqk = turn(z, [ref[...].astype(F32) for ref in refs[:heads]])
+    dv = turn(z, [unpair(ref[...].astype(F32), block) for ref in refs[heads : 2 * heads]])
+    da_ref, sum_ref, sums_ref, db_ref = refs[2 * heads :]
     cos, sl, sr = cos_ref[...], sl_ref[...], sr_ref[...]
     cols = heads * HEAD
     for h in range(0, heads, 2):
         at = h * HEAD
-        one = rotary(dqk_ref[z ^ h].astype(F32), cos, sl, sr, -1.0)
-        two = rotary(dqk_ref[z ^ (h + 1)].astype(F32), cos, sl, sr, -1.0)
+        one = rotary(dqk[h], cos, sl, sr, -1.0)
+        two = rotary(dqk[h + 1], cos, sl, sr, -1.0)
         da_ref[:, at : at + 2 * HEAD] = jnp.concatenate([one[:, :HEAD], two[:, :HEAD]], axis=1).astype(BF16)
         da_ref[:, cols + at : cols + at + 2 * HEAD] = jnp.concatenate([one[:, HEAD:], two[:, HEAD:]], axis=1).astype(BF16)
-        one, two = unpair(dv_ref[z ^ h].astype(F32), block), unpair(dv_ref[z ^ (h + 1)].astype(F32), block)
-        da_ref[:, 2 * cols + at : 2 * cols + at + 2 * HEAD] = jnp.concatenate([one, two], axis=1).astype(BF16)
+        da_ref[:, 2 * cols + at : 2 * cols + at + 2 * HEAD] = jnp.concatenate(dv[h : h + 2], axis=1).astype(BF16)
     grad = da_ref[...]
     grad_norm = dot_nt(grad, w_ref[...])
     sum_ref[...] = (dx_ref[...] + grad_norm * norm_ref[0:1]).astype(BF16)
@@ -272,8 +289,8 @@
 
 
 def post(z, dqk, dv, x, dx, norms, w, cos, sl, sr, block):
-    heads, rows, _ = dqk.shape
-    width = x.shape[1]
+    heads = len(dqk)
+    rows, width = x.shape
     three = heads * 3 * HEAD
     table = pl.BlockSpec((TILE, 2 * HEAD), row_at)
     tile = pl.BlockSpec((TILE, width), row_at)
@@ -283,8 +300,6 @@
             num_scalar_prefetch=1,
             grid=(rows // TILE,),
             in_specs=[
-                pl.BlockSpec((heads, TILE, 2 * HEAD), slab_at),
-                pl.BlockSpec((heads, TILE // 2, 2 * HEAD), slab_at),
                 tile,
                 tile,
                 pl.BlockSpec(norms.shape, whole_at),
@@ -292,7 +307,9 @@
                 table,
                 table,
                 table,
-            ],
+            ]
+            + [piece(TILE)] * heads
+            + [piece(TILE // 2)] * heads,
             out_specs=[
                 pl.BlockSpec((TILE, three), row_at),
                 tile,
@@ -307,7 +324,7 @@
             jax.ShapeDtypeStruct((8, three), F32),
         ],
         **params(2 * rows * width * three, 14 * 2**20),
-    )(z, dqk, dv, x, dx, norms, w, cos, sl, sr)
+    )(z, x, dx, norms, w, cos, sl, sr, *dqk, *dv)
 
 
 def doc_start(packed, ends_ref, count):
@@ -324,8 +341,8 @@
     return end
 
 
-def tile_at(i):
-    return pl.ds(pl.multiple_of(i * TILE, TILE), TILE)
+def tile_at(i, size=TILE):
+    return pl.ds(pl.multiple_of(i * size, size), size)
 
 
 def load_half(ref, source, block):
@@ -333,18 +350,29 @@
     return jnp.where(source % 2 == 0, both[:, :HEAD], both[:, HEAD:])
 
 
-def masked_scores(k_s, q_t, ends_ref, count, i, j):
-    s = dot(k_s[tile_at(j), :], q_t[:HEAD, tile_at(i)])
-    key_at = lax.broadcasted_iota(jnp.int32, (TILE, TILE), 0)
-    query_at = lax.broadcasted_iota(jnp.int32, (TILE, TILE), 1)
-    query_row = i * TILE + lax.broadcasted_iota(jnp.int32, (1, TILE), 1)
-    first = doc_start(query_row, ends_ref, count) - j * TILE
-    last = (i - j) * TILE + query_at
+def masked_scores(k_s, q_t, ends_ref, count, i, j, q_size, k_size):
+    s = dot(k_s[tile_at(j, k_size), :], q_t[:HEAD, tile_at(i, q_size)])
+    key_at = lax.broadcasted_iota(jnp.int32, (k_size, q_size), 0)
+    query_at = lax.broadcasted_iota(jnp.int32, (k_size, q_size), 1)
+    query_row = i * q_size + lax.broadcasted_iota(jnp.int32, (1, q_size), 1)
+    first = doc_start(query_row, ends_ref, count) - j * k_size
+    last = i * q_size - j * k_size + query_at
     return jnp.where((key_at >= first) & (key_at <= last), s, NEG)
 
 
-def forward_kernel(block, count, source_ref, packed_ref, ends_ref, qk_ref, v_ref, o_ref, o_t, lse_ref, k_s, q_t, v_t, o_s):
+def lay_out(pieces, whole):
+    size = pieces[0].shape[0]
+    for i, ref in enumerate(pieces):
+        whole[i * size : (i + 1) * size, :] = ref[...]
+
+
+def forward_kernel(block, count, source_ref, packed_ref, ends_ref, *refs):
+    pieces = (len(refs) - 8) // 3
+    qk_in, v_in, o_out = refs[:pieces], refs[pieces : 2 * pieces], refs[2 * pieces : 3 * pieces]
+    o_t, lse_ref, k_s, q_t, v_t, o_s, qk_ref, v_ref = refs[3 * pieces :]
     rows = qk_ref.shape[0]
+    lay_out(qk_in, qk_ref)
+    lay_out(v_in, v_ref)
     tiles = rows // TILE
     per = TILE // block
     scale = HEAD ** (-0.5)
@@ -364,40 +392,57 @@
     lax.fori_loop(0, tiles, gather, 0)
 
     def forward(i, carry):
+        here = tile_at(i, FQ)
+
         def step(j, state):
             top, total, acc = state
-            s = masked_scores(k_s, q_t, ends_ref, count, i, j)
+            s = masked_scores(k_s, q_t, ends_ref, count, i, j, FQ, FK)
             new_top = jnp.maximum(top, jnp.max(s, axis=0, keepdims=True))
             p = jnp.exp(s - new_top)
             fade = jnp.exp(top - new_top)
             total = total * fade + jnp.sum(p, axis=0, keepdims=True)
-            acc = acc * fade + dot(v_t[:, tile_at(j)], p.astype(BF16))
+            acc = acc * fade + dot(v_t[:, tile_at(j, FK)], p.astype(BF16))
             return new_top, total, acc
 
-        low = doc_start(i * TILE, ends_ref, count) // TILE
+        low = doc_start(i * FQ, ends_ref, count) // FK
+        high = (i * FQ + FQ - 1) // FK
         top, total, acc = lax.fori_loop(
-            low, i + 1, step, (jnp.full((1, TILE), NEG, F32), jnp.zeros((1, TILE), F32), jnp.zeros((HEAD, TILE), F32))
+            low, high + 1, step, (jnp.full((1, FQ), NEG, F32), jnp.zeros((1, FQ), F32), jnp.zeros((HEAD, FQ), F32))
         )
         out = acc / total
-        lse_ref[:, tile_at(i)] = top + jnp.log(total)
-        o_t[:, tile_at(i)] = out
-        o_s[tile_at(i), :] = out.T
+        lse_ref[:, here] = top + jnp.log(total)
+        o_t[:, here] = out
+        o_s[here, :] = out.T
         return carry
 
-    lax.fori_loop(0, tiles, forward, 0)
-
-    def scatter(i, carry):
-        both = [o_s[pl.ds(pl.multiple_of(packed_ref[2 * i + b] * block, block), block), :] for b in range(2)]
-        o_ref[pl.ds(pl.multiple_of(i * block, block), block), :] = jnp.concatenate(both, axis=1).astype(BF16)
-        return carry
-
-    lax.fori_loop(0, rows // (2 * block), scatter, 0)
-
-
-def backward_kernel(
-    block, count, source_ref, packed_ref, ends_ref, qk_ref, v_ref, do_ref, o_t, lse_ref, dqk_ref, dv_ref, q_s, k_s, v_s, do_s, qk_t, do_t, dq_t, delta_s, dk_s, dv_s
-):
+    lax.fori_loop(0, rows // FQ, forward, 0)
+
+    send_pairs(o_s, o_out, packed_ref, block)
+
+
+def send_pairs(whole, out_refs, packed_ref, block):
+    per = out_refs[0].shape[0] // block
+    for at, ref in enumerate(out_refs):
+
+        def one(i, carry):
+            row = 2 * (at * per + i)
+            both = [whole[pl.ds(pl.multiple_of(packed_ref[row + b] * block, block), block), :] for b in range(2)]
+            ref[pl.ds(pl.multiple_of(i * block, block), block), :] = jnp.concatenate(both, axis=1).astype(BF16)
+            return carry
+
+        lax.fori_loop(0, per, one, 0)
+
+
+def backward_kernel(block, count, source_ref, packed_ref, ends_ref, *refs):
+    pieces = (len(refs) - 16) // 5
+    qk_in, v_in, do_in = [refs[i * pieces : (i + 1) * pieces] for i in range(3)]
+    o_t, lse_ref = refs[3 * pieces : 3 * pieces + 2]
+    dqk_out, dv_out = [refs[i * pieces + 2 : (i + 1) * pieces + 2] for i in (3, 4)]
+    q_s, k_s, v_s, do_s, qk_t, do_t, dq_t, delta_s, dk_s, dv_s, qk_ref, v_ref, do_ref, dqk_ref = refs[5 * pieces + 2 :]
     rows = qk_ref.shape[0]
+    lay_out(qk_in, qk_ref)
+    lay_out(v_in, v_ref)
+    lay_out(do_in, do_ref)
     tiles = rows // TILE
     per = TILE // block
     scale = HEAD ** (-0.5)
@@ -427,12 +472,12 @@
     lax.fori_loop(0, tiles, gather, 0)
 
     def backward(j, carry):
-        keys = tile_at(j)
+        keys = tile_at(j, BK)
 
         def step(i, state):
             dk, dv = state
-            here = tile_at(i)
-            p = jnp.exp(masked_scores(k_s, qk_t, ends_ref, count, i, j) - lse_ref[:, here])
+            here = tile_at(i, BQ)
+            p = jnp.exp(masked_scores(k_s, qk_t, ends_ref, count, i, j, BQ, BK) - lse_ref[:, here])
             dp = dot(v_s[keys, :], do_t[:, here])
             ds = (p * (dp - delta_s[:, here])).astype(BF16)
             dv = dv + dot(p.astype(BF16), do_s[here, :])
@@ -440,14 +485,14 @@
             dq_t[:, here] += dot(qk_t[HEAD:, keys], ds)
             return dk, dv
 
-        high = (doc_end(j * TILE + TILE - 1, ends_ref, count) - 1) // TILE
-        zero = jnp.zeros((TILE, HEAD), F32)
-        dk, dv = lax.fori_loop(j, high + 1, step, (zero, zero))
+        high = (doc_end(j * BK + BK - 1, ends_ref, count) - 1) // BQ
+        zero = jnp.zeros((BK, HEAD), F32)
+        dk, dv = lax.fori_loop(j * BK // BQ, high + 1, step, (zero, zero))
         dk_s[keys, :] = dk
         dv_s[keys, :] = dv
         return carry
 
-    lax.fori_loop(0, tiles, backward, 0)
+    lax.fori_loop(0, rows // BK, backward, 0)
 
     def scatter(i, carry):
         here = tile_at(i)
@@ -460,12 +505,10 @@
 
     lax.fori_loop(0, tiles, scatter, 0)
 
-    def scatter_v(i, carry):
-        both = [dv_s[pl.ds(pl.multiple_of(packed_ref[2 * i + b] * block, block), block), :] for b in range(2)]
-        dv_ref[pl.ds(pl.multiple_of(i * block, block), block), :] = jnp.concatenate(both, axis=1).astype(BF16)
-        return carry
-
-    lax.fori_loop(0, rows // (2 * block), scatter_v, 0)
+    size = rows // pieces
+    for i, ref in enumerate(dqk_out):
+        ref[...] = dqk_ref[i * size : (i + 1) * size, :]
+    send_pairs(dv_s, dv_out, packed_ref, block)
 
 
 IN_VMEM = pl.BlockSpec(memory_space=pltpu.VMEM)
@@ -473,34 +516,42 @@
 
 
 def attend_forward(source, packed, ends, qk, v, block):
-    rows = qk.shape[0]
+    pieces = len(qk)
+    rows = pieces * qk[0].shape[0]
     turned = pltpu.VMEM((HEAD, rows), BF16)
     return pl.pallas_call(
         functools.partial(forward_kernel, block, ends.shape[0]),
-        in_specs=[IN_SMEM] * 3 + [IN_VMEM] * 2,
-        out_specs=[IN_VMEM] * 3,
-        out_shape=[
-            jax.ShapeDtypeStruct((rows // 2, 2 * HEAD), BF16),
+        in_specs=[IN_SMEM] * 3 + [IN_VMEM] * (2 * pieces),
+        out_specs=[IN_VMEM] * (pieces + 2),
+        out_shape=[bf16_rows(rows // (2 * pieces))] * pieces
+        + [
             jax.ShapeDtypeStruct((HEAD, rows), F32),
             jax.ShapeDtypeStruct((1, rows), F32),
         ],
-        scratch_shapes=[pltpu.VMEM((rows, HEAD), BF16), turned, turned, pltpu.VMEM((rows, HEAD), F32)],
+        scratch_shapes=[
+            pltpu.VMEM((rows, HEAD), BF16),
+            turned,
+            turned,
+            pltpu.VMEM((rows, HEAD), F32),
+            pltpu.VMEM((rows, 2 * HEAD), BF16),
+            pltpu.VMEM((rows // 2, 2 * HEAD), BF16),
+        ],
         **params(rows * rows * HEAD * 40, 6 * rows * HEAD * 2, rows * rows),
-    )(source, packed, ends, qk, v)
+    )(source, packed, ends, *qk, *v)
 
 
 def attend_backward(source, packed, ends, qk, v, do, o_t, lse, block):
-    rows = qk.shape[0]
+    pieces = len(qk)
+    rows = pieces * qk[0].shape[0]
     half = pltpu.VMEM((rows, HEAD), BF16)
     wide = pltpu.VMEM((rows, HEAD), F32)
+    pairs = pltpu.VMEM((rows // 2, 2 * HEAD), BF16)
+    whole = pltpu.VMEM((rows, 2 * HEAD), BF16)
     return pl.pallas_call(
         functools.partial(backward_kernel, block, ends.shape[0]),
-        in_specs=[IN_SMEM] * 3 + [IN_VMEM] * 5,
-        out_specs=[IN_VMEM] * 2,
-        out_shape=[
-            jax.ShapeDtypeStruct((rows, 2 * HEAD), BF16),
-            jax.ShapeDtypeStruct((rows // 2, 2 * HEAD), BF16),
-        ],
+        in_specs=[IN_SMEM] * 3 + [IN_VMEM] * (3 * pieces + 2),
+        out_specs=[IN_VMEM] * (2 * pieces),
+        out_shape=[bf16_rows(rows // pieces)] * pieces + [bf16_rows(rows // (2 * pieces))] * pieces,
         scratch_shapes=[
             half,
             half,
@@ -512,15 +563,17 @@
             pltpu.VMEM((1, rows), F32),
             wide,
             wide,
+            whole,
+            pairs,
+            pairs,
+            whole,
         ],
         **params(rows * rows * HEAD * 40, 12 * rows * HEAD * 2, rows * rows),
-    )(source, packed, ends, qk, v, do, o_t, lse)
-
-
-def join_in(value, far):
-    far = jnp.stack([value, far])
-    near = xor_swap(far, "in", GROUP_IN, 1)
-    return jnp.stack([far[0], near[0], far[1], near[1]])
+    )(source, packed, ends, *qk, *v, *do, o_t, lse)
+
+
+def join_in(value, far, near):
+    return jnp.concatenate([value, near[0], far, near[1]])
 
 
 def halves(parts):
@@ -544,8 +597,9 @@
     return jnp.stack([lax.dynamic_index_in_dim(stacked, t ^ u, 0, keepdims=False) for u in range(GROUP_IN)])
 
 
-def exchange_out(parts, size):
-    return jnp.stack([parts[0]] + [xor_swap(parts[s], "out", size, s) for s in range(1, size)])
+def exchange_out(parts):
+    size = len(parts)
+    return [parts[0]] + [xor_swap(parts[s], "out", size, s) for s in range(1, size)]
 
 
 def body(
@@ -617,8 +671,7 @@
     vec = jnp.stack([jnp.pad(v, (0, lanes - v.shape[0])) for v in vectors])
     vec = jnp.pad(vec, ((0, r_w * per_row - len(vectors)), (0, 0))).reshape(r_w, 128)
     vec = jnp.broadcast_to(vec[None], (n_in, r_w, 128))
-    all_cols = jnp.concatenate([qkv_cols, vec, in_cols], axis=2)
-    joined_cols = exchange_in(all_cols, t).reshape(n_in * r_w, -1)
+    joined_cols = exchange_in(jnp.concatenate([qkv_cols, vec, in_cols], axis=2), t).reshape(n_in * r_w, -1)
     home = []
     for b in range(n_all):
         t_to, g_to = b // n_g, b % n_g
@@ -652,25 +705,27 @@
     bias_qkv = lax.dynamic_index_in_dim(spans[4].reshape(3, n_in, cols), t, 1, keepdims=False).reshape(-1)
     norms = jnp.concatenate([jnp.stack([gain_one, shift_one, gain_two, shift_two]), jnp.zeros((4, width), F32)])
 
-    x_all = join_in(tokens, x_far).reshape(rows, width)
+    x_near = xor_swap(jnp.stack([tokens, x_far]), "in", n_in, 1)
+    x_near, weight_qkv, norms, bias_qkv = lax.optimization_barrier((x_near, weight_qkv, norms, bias_qkv))
+    x_all = join_in(tokens, x_far, x_near)
     x_all, to_send = lax.optimization_barrier((x_all, cotangent))
     dy_far = xor_swap(to_send, "in", n_in, 2)
 
-    qk, v, n1, n2 = prep(z_arr, x_all, norms, weight_qkv, bias_qkv[None], cos, sin_l, sin_r, block)
-    qk = exchange_out(qk, n_out).reshape(n_out * rows, 2 * HEAD)
-    v = exchange_out(v, n_out).reshape(n_out * rows // 2, 2 * HEAD)
+    n1, n2, *parts = prep(z_arr, x_all, norms, weight_qkv, bias_qkv[None], cos, sin_l, sin_r, block)
+    qk = exchange_out(parts[:h_in])
+    v = exchange_out(parts[h_in:])
     qk, v, dy_far = lax.optimization_barrier((qk, v, dy_far))
-    dy_all = join_in(cotangent, dy_far).reshape(rows, width)
-    o, o_t, lse = attend_forward(source, packed_of, ends, qk, v, block)
-    o, dy_all = lax.optimization_barrier((o, dy_all))
-    o = exchange_out(o.reshape(n_out, rows // 2, 2 * HEAD), n_out)
-    do = grad_att(z_arr, dy_all, weight_out, block)
-    do = exchange_out(do, n_out).reshape(n_out * rows // 2, 2 * HEAD)
+    dy_near = xor_swap(jnp.stack([cotangent, dy_far]), "in", n_in, 1)
+    *o, o_t, lse = attend_forward(source, packed_of, ends, qk, v, block)
+    o, dy_near = lax.optimization_barrier((o, dy_near))
+    dy_all = join_in(cotangent, dy_far, dy_near)
+    o = exchange_out(o)
+    do = exchange_out(grad_att(z_arr, dy_all, weight_out, block))
 
     hidden, grad_up, y_ff, dx_ff, sums_two, grad_b_in = feed(x_all, n2, dy_all, norms, weight_in, weight_fc2, bias_in[None])
     o, y_ff = lax.optimization_barrier((o, y_ff))
-    o = merge_heads(z_arr, o, block)
-    y_part = (y_ff + dot(o, weight_out)).astype(BF16).reshape(n_in, rows_dev, width)
+    o, y_part = project(z_arr, o, y_ff, weight_out, block)
+    y_part = y_part.reshape(n_in, rows_dev, width)
     grad_fc2 = dot_tn(hidden, dy_all)
     grad_in = dot_tn(n2, grad_up)
     grad_out = dot_tn(o, dy_all)
@@ -687,16 +742,19 @@
     second_grads = lax.psum_scatter(second_grads, G_AXES, scatter_dimension=0, tiled=False)
     y_near = near_in(y_part)
     own = tokens.astype(F32)
-    dqk, dv = attend_backward(source, packed_of, ends, qk, v, do, o_t, lse, block)
-    dqk, dv, y_near = lax.optimization_barrier((dqk, dv, y_near))
-    dqk = exchange_out(dqk.reshape(n_out, rows, 2 * HEAD), n_out)
-    dv = exchange_out(dv.reshape(n_out, rows // 2, 2 * HEAD), n_out)
-    mixed = (own + far_in(y_part, y_near) + bias_out).astype(BF16)
+    parts = attend_backward(source, packed_of, ends, qk, v, do, o_t, lse, block)
+    parts, y_near = lax.optimization_barrier((parts, y_near))
+    dqk = exchange_out(parts[:h_in])
+    dv = exchange_out(parts[h_in:])
+    y_far = xor_swap((y_part[2].astype(F32) + y_near[1].astype(F32)).astype(BF16), "in", n_in, 2)
+    dqk, dv, y_far = lax.optimization_barrier((dqk, dv, y_far))
+    y_sum = y_part[0].astype(F32) + y_near[0].astype(F32) + y_far.astype(F32)
+    mixed = (own + y_sum + bias_out).astype(BF16)
     da, w_parts, sums_one, grad_b_qkv = post(
         z_arr, dqk, dv, x_all, dx_ff, norms, weight_qkv, cos, sin_l, sin_r, block
     )
+    w_parts, da, mixed, second_grads = lax.optimization_barrier((w_parts, da, mixed, second_grads))
     in_part = exchange_in(second_grads[:, :ff_in].reshape(n_in, r_w, ff_in), t)
-    w_parts, da, mixed, in_part = lax.optimization_barrier((w_parts, da, mixed, in_part))
     w_parts = halves(w_parts.reshape(n_in, rows_dev, width))
     near = near_in(w_parts[0])
     near, w_next = lax.optimization_barrier((near, w_parts[1]))

time: 390 us -> 351 us (0.900)
  waiting for transfers between devices: 118 us -> 101 us
  Pallas kernels: 113 us -> 104 us
    ppermute x37, waiting for transfers between devices: 118 us -> 101 us  [xor_swap(): return lax.ppermute(value, axis, [(i, i ^ step) for i in range(size)])]
    pallas_call x1, Pallas kernels: 35.7 us -> 25.5 us  [attend_forward(): pl.pallas_call(functools.partial(forward_kernel, block, ends.shape[0]), i...]
    another operation x13 -> x5, other arithmetic: 13 us -> 3.82 us  [the longest x6 7.69 us: exchange_out(): jnp.stack([parts[0]] + [xor_swap(parts[s], 'out', size, s) for s in range...]
    slice x8 -> x0, local copies, waits for them, and re-layouts: 6.8 us -> none  [the longest x6 6.67 us: exchange_out(): parts[0]]
    dot_general x1 -> x0, matrix products: 4.44 us -> none  [dot(): return jnp.dot(a, b, preferred_element_type=F32)]
    ppermute x37, starting transfers between devices: 40.5 us -> 36.2 us  [xor_swap(): return lax.ppermute(value, axis, [(i, i ^ step) for i in range(size)])]
  transfers between devices with their start and end apart: 43 -> 43, of which waited for: 18 -> 15; matrix products, arithmetic and copies ran while one was open for 16% -> 23% of each run, Pallas kernels for 24% -> 29%
where the time goes in v2:
time: 351 us
  Pallas kernels  104 us (30%)
  waiting for transfers between devices  101 us (29%)
  local copies, waits for them, and re-layouts  42.7 us (12%)
  starting transfers between devices  38.5 us (11%)
  other arithmetic  37.5 us (11%)
  between operations  14.7 us (4%)
  matrix products  13.9 us (4%)
    ppermute x37, waiting for transfers between devices, xor_swap(): return lax.ppermute(value, axis, [(i, i ^ step) for i in range(size)])  101 us
    ppermute x37, starting transfers between devices, xor_swap(): return lax.ppermute(value, axis, [(i, i ^ step) for i in range(size)])  36.2 us
    pallas_call x1, Pallas kernels, attend_backward(): pl.pallas_call(functools.partial(backward_kernel, block, ends.shape[0]),...  35.8 us
    pallas_call x1, Pallas kernels, attend_forward(): pl.pallas_call(functools.partial(forward_kernel, block, ends.shape[0]), i...  25.5 us
    pallas_call x1, Pallas kernels, feed(): pl.pallas_call(feed_kernel, grid=(rows // TILE,), in_specs=[tile, tile, t...  15.3 us
    dot_general x4, matrix products, dot_tn(): lax.dot_general(a, b, (((0,), (0,)), ((), ())), preferred_element_type=F32)  13.9 us
    pallas_call x1, Pallas kernels, post(): pl.pallas_call(functools.partial(post_kernel, heads, block), grid_spec=pl...  8.64 us
    pallas_call x1, Pallas kernels, prep(): pl.pallas_call(functools.partial(prep_kernel, heads, block), grid_spec=pl...  8.32 us
  transfers between devices with their start and end apart: 43, of which 15 were waited for; matrix products, arithmetic and copies ran while one was open for 23% of the time, Pallas kernels for 29%

profile of v2, /device:TPU:0, one launch (start us, length us, event | category | flops | bytes accessed | tf_op | source)
XLA Modules:
  0.0 351.4 jit_solution(8462570217914724203)
XLA Ops:
  10.4 5.1 %collective-permute-start.2 = (bf16[32,1920]{1,0:T(8,128)(2,1)S(1)}, bf16[32,1920]{1,0:T(8,128)(2,1)S(1)}, u32[]{:S(2)}, u32[]{:S(2)}) collective-permute-start(bf16[32,1920]{1,0:T(8,128)(2,1)S(1)} %get-tuple-element.238), channel_id=1, source_target_pairs={{0,12},{4,8},{8,4},{12,0},{1,13},{5,9},{9,5},{13,1},{2,14},{6,10},... | collective-permute-start | bytes 368648 | tf_op jit(solution)/shard_map/ppermute | solution.py:39
  19.8 8.2 %collective-permute-done.1 = bf16[32,1920]{1,0:T(8,128)(2,1)S(1)} collective-permute-done((bf16[32,1920]{1,0:T(8,128)(2,1)S(1)}, bf16[32,1920]{1,0:T(8,128)(2,1)S(1)}, u32[]{:S(2)}, u32[]{:S(2)}) %collective-permute-start.1) | collective-permute-done | bytes 122912 | tf_op jit(solution)/shard_map/ppermute | solution.py:39
  32.1 21.8 %collective-permute-done.4 = bf16[256,1024]{1,0:T(8,128)(2,1)S(1)} collective-permute-done((bf16[256,1024]{1,0:T(8,128)(2,1)S(1)}, bf16[256,1024]{1,0:T(8,128)(2,1)S(1)}, u32[]{:S(2)}, u32[]{:S(2)}) %collective-permute-start.4) | collective-permute-done | bytes 524320 | tf_op jit(solution)/shard_map/ppermute | solution.py:39
  54.9 3.4 fusion.11
  63.4 15.6 %collective-permute-done.5 = bf16[2,256,1024]{2,1,0:T(8,128)(2,1)} collective-permute-done((bf16[2,256,1024]{2,1,0:T(8,128)(2,1)}, bf16[2,256,1024]{2,1,0:T(8,128)(2,1)}, u32[]{:S(2)}, u32[]{:S(2)}) %collective-permute-start.5) | collective-permute-done | bytes 1048608 | tf_op jit(solution)/shard_map/ppermute | solution.py:39
  84.4 8.3 %shard_map.246 = (bf16[1024,1024]{1,0:T(8,128)(2,1)}, bf16[1024,1024]{1,0:T(8,128)(2,1)}, bf16[1024,128]{1,0:T(8,128)(2,1)}, bf16[1024,128]{1,0:T(8,128)(2,1)}, ...) custom-call(s32[1]{0:T(128)} %bitcast.z_ref, ...), custom_call_target="tpu_custom_call" | custom-call | flops 1610612736 | bytes 12582912 | tf_op jit(solution)/shard_map/pallas_call | solution.py:124
  103.1 4.7 %collective-permute-done.7.refs_2_ = bf16[1024,128]{1,0:T(8,128)(2,1)S(1)} collective-permute-done((bf16[1024,128]{1,0:T(8,128)(2,1)}, bf16[1024,128]{1,0:T(8,128)(2,1)S(1)}, u32[]{:S(2)}, u32[]{:S(2)}) %collective-permute-start.7) | collective-permute-done | bytes 262176 | tf_op jit(solution)/shard_map/ppermute | solution.py:39
  107.9 4.7 %collective-permute-done.8.refs_3_ = bf16[1024,128]{1,0:T(8,128)(2,1)S(1)} collective-permute-done((bf16[1024,128]{1,0:T(8,128)(2,1)}, bf16[1024,128]{1,0:T(8,128)(2,1)S(1)}, u32[]{:S(2)}, u32[]{:S(2)}) %collective-permute-start.8) | collective-permute-done | bytes 262176 | tf_op jit(solution)/shard_map/ppermute | solution.py:39
  116.1 25.5 %shard_map.247 = (bf16[512,128]{1,0:T(8,128)(2,1)}, bf16[512,128]{1,0:T(8,128)(2,1)}, bf16[512,128]{1,0:T(8,128)(2,1)}, bf16[512,128]{1,0:T(8,128)(2,1)}, f32[64,4096]{1,0:T(8,128)}, /*index=5*/f32[1,4096]{1,0:T(1,128)}) custom-call(s32[64]{0:T(128)} %fusion.20.source_ref, s32[64]{0:T(128)} %copy-done.22, s32[4]{0:T(128)} %bitcast.196, ...), custom_call_target="tpu_custom_call" | custom-call | flops 42949672960 | bytes 3145728 | tf_op jit(solution)/shard_map/pallas_call | solution.py:522
  145.1 4.4 %shard_map.249 = (bf16[512,128]{1,0:T(8,128)(2,1)}, bf16[512,128]{1,0:T(8,128)(2,1)}, bf16[512,128]{1,0:T(8,128)(2,1)}, bf16[512,128]{1,0:T(8,128)(2,1)}) custom-call(s32[1]{0:T(128)} %bitcast.z_ref, bf16[1024,1024]{1,0:T(8,128)(2,1)} %pad_maximum_fusion.2.dy_ref, bf16[256,1024]{1,0:T(8,128)(2,1)} %reshape.356.wo_ref), custom_call_target="tpu_custom_call" | custom-call | flops 536870912 | bytes 4194304 | tf_op jit(solution)/shard_map/pallas_call | solution.py:217
  151.3 4.0 %fusion.33 = (bf16[8,128,1024]{2,1,0:T(8,128)(2,1)}, bf16[8,128,1024]{2,1,0:T(8,128)(2,1)S(1)}) fusion(bf16[8,128,2048]{2,1,0:T(8,128)(2,1)} %bitcast.156), kind=kLoop, calls=%fused_computation.172 | loop fusion | bytes 8388608 | tf_op jit(solution)/shard_map/slice | solution.py:698
  157.0 15.3 %shard_map.248 = (bf16[1024,1024]{1,0:T(8,128)(2,1)}, bf16[1024,1024]{1,0:T(8,128)(2,1)}, f32[1024,1024]{1,0:T(8,128)}, f32[1024,1024]{1,0:T(8,128)}, f32[8,1024]{1,0:T(8,128)}, /*index=5*/f32[8,1024]{1,0:T(8,128)}) custom-call(bf16[1024,1024]{1,0:T(8,128)(2,1)} %pad_maximum_fusion.1.x_ref, bf16[1024,1024]{1,0:T(8,128)(2,1)} %get-tuple-element.117.n2_ref, ...), custom_call_target="tpu_custom_call" | custom-call | flops 8589934592 | bytes 25165824 | tf_op jit(solution)/shard_map/pallas_call | solution.py:175
  172.3 4.0 %convolution_convert_fusion.1 = bf16[1024,1024]{1,0:T(8,128)(2,1)S(1)} fusion(bf16[1024,1024]{1,0:T(8,128)(2,1)S(1)} %copy-done.34, bf16[1024,1024]{1,0:T(8,128)(2,1)} %get-tuple-element.146), kind=kOutput, calls=%fused_computation.4 | convolution fusion | flops 2148532224 | bytes 6291456 | tf_op jit(solution)/shard_map/dot_general | solution.py:35
  178.6 5.5 %shard_map.250 = (bf16[1024,256]{1,0:T(8,128)(2,1)}, bf16[1024,1024]{1,0:T(8,128)(2,1)}) custom-call(s32[1]{0:T(128)} %bitcast.z_ref, f32[1024,1024]{1,0:T(8,128)} %get-tuple-element.153.y_ref, bf16[256,1024]{1,0:T(8,128)(2,1)} %reshape.356.wo_ref, bf16[512,128]{1,0:T(8,128)(2,1)} %get-tuple-element.154.refs_0_, bf16[512,128]{1,0:T(8,128)(2,1)} %copy-done.9, ...), custom_call_target="tpu_custom_call" | custom-call | flops 536870912 | bytes 8388608 | tf_op jit(solution)/shard_map/pallas_call | solution.py:242
  186.9 3.7 %convolution_convert_fusion = bf16[1024,1024]{1,0:T(8,128)(2,1)} fusion(bf16[1024,1024]{1,0:T(8,128)(2,1)S(1)} %copy-done.35, bf16[1024,1024]{1,0:T(8,128)(2,1)S(1)} %copy-done), kind=kOutput, calls=%fused_computation.3 | convolution fusion | flops 2148532224 | bytes 6291456 | tf_op jit(solution)/shard_map/dot_general | solution.py:35
  192.0 3.9 %pad_maximum_fusion = bf16[8,128,2304]{2,1,0:T(8,128)(2,1)} fusion(bf16[8,128,256]{2,1,0:T(8,128)(2,1)S(1)} %reshape.360, bf16[8,128,1024]{2,1,0:T(8,128)(2,1)} %bitcast.172, bf16[8,128,1024]{2,1,0:T(8,128)(2,1)} %bitcast.149), kind=kLoop, calls=%fused_computation | loop fusion | flops 14155776 | bytes 9437184 | tf_op jit(solution)/shard_map/concatenate | solution.py:732
  198.9 35.8 %shard_map.251 = (bf16[1024,128]{1,0:T(8,128)(2,1)}, bf16[1024,128]{1,0:T(8,128)(2,1)}, bf16[1024,128]{1,0:T(8,128)(2,1)}, bf16[1024,128]{1,0:T(8,128)(2,1)}, bf...) custom-call(s32[64]{0:T(128)} %fusion.20.source_ref, ...), custom_call_target="tpu_custom_call" | custom-call | flops 42949672960 | bytes 6291456 | tf_op jit(solution)/shard_map/pallas_call | solution.py:550
  242.2 5.7 %collective-permute-done.25.refs_6_ = bf16[512,128]{1,0:T(8,128)(2,1)} collective-permute-done((bf16[512,128]{1,0:T(8,128)(2,1)S(1)}, bf16[512,128]{1,0:T(8,128)(2,1)}, u32[]{:S(2)}, u32[]{:S(2)}) %collective-permute-start.25) | collective-permute-done | bytes 131104 | tf_op jit(solution)/shard_map/ppermute | solution.py:39
  255.3 9.3 %collective-permute-done.26.refs_7_ = bf16[512,128]{1,0:T(8,128)(2,1)} collective-permute-done((bf16[512,128]{1,0:T(8,128)(2,1)}, bf16[512,128]{1,0:T(8,128)(2,1)}, u32[]{:S(2)}, u32[]{:S(2)}) %collective-permute-start.26) | collective-permute-done | bytes 131104 | tf_op jit(solution)/shard_map/ppermute | solution.py:39
  265.3 8.6 %shard_map.252 = (bf16[1024,768]{1,0:T(8,128)(2,1)}, bf16[1024,1024]{1,0:T(8,128)(2,1)}, f32[8,1024]{1,0:T(8,128)}, f32[8,768]{1,0:T(8,128)}) custom-call(s32[1]{0:T(128)} %bitcast.z_ref, bf16[1024,1024]{1,0:T(8,128)(2,1)} %pad_maximum_fusion.1.x_ref, f32[1024,1024]{1,0:T(8,128)} %get-tuple-element.141.dx_ref, f32[8,1024]{1,0:T(8,128)} %concatenate.29.norm_ref, ...), custom_call_target="tpu_custom_call" | custom-call | flops 1610612736 | bytes 14680064 | tf_op jit(solution)/shard_map/pallas_call | solution.py:297
  284.2 3.5 convolution_convert_fusion.2
  296.5 2.9 collective-permute-done.28
  307.4 11.9 %collective-permute-done.30 = bf16[2,256,512]{2,1,0:T(8,128)(2,1)S(1)} collective-permute-done((bf16[2,256,512]{2,1,0:T(8,128)(2,1)}, bf16[2,256,512]{2,1,0:T(8,128)(2,1)S(1)}, u32[]{:S(2)}, u32[]{:S(2)}) %collective-permute-start.30) | collective-permute-done | bytes 524320 | tf_op jit(solution)/shard_map/ppermute | solution.py:39
  323.6 7.8 %collective-permute-done.31 = bf16[256,512]{1,0:T(8,128)(2,1)} collective-permute-done((bf16[256,512]{1,0:T(8,128)(2,1)S(1)}, bf16[256,512]{1,0:T(8,128)(2,1)}, u32[]{:S(2)}, u32[]{:S(2)}) %collective-permute-start.31) | collective-permute-done | bytes 262176 | tf_op jit(solution)/shard_map/ppermute | solution.py:39
  (291 shorter events, 113.0 us)
Async XLA Ops:
  7.3 51.1 %all-gather.5.cloned.1.call-start = ((), (), s32[]{:S(2)}) async-start(), calls=%async_computation.4 | async-start | bytes 2654208 | tf_op jit(solution)/shard_map/all_gather | solution.py:683
  29.1 122.3 %all-gather.7.cloned.1.call-start = ((), (), s32[]{:S(2)}) async-start(), calls=%async_computation.5 | async-start | bytes 4718592 | tf_op jit(solution)/shard_map/all_gather | solution.py:685
  29.4 24.5 %collective-permute-start.4 = (bf16[256,1024]{1,0:T(8,128)(2,1)S(1)}, bf16[256,1024]{1,0:T(8,128)(2,1)S(1)}, u32[]{:S(2)}, u32[]{:S(2)}) collective-permute-start(bf16[256,1024]{1,0:T(8,128)(2,1)S(1)} %copy-done.1), channel_id=1, source_target_pairs={{0,8},{4,12},{8,0},{12,4},{1,9},{5,13},{9,1},{13,5},{2,10},{6,14},... | collective-permute-start | bytes 1572872 | tf_op jit(solution)/shard_map/ppermute | solution.py:39
  31.6 249.1 %reduce-scatter.3.cloned.1.call-start = ((), (), s32[]{:S(2)}) async-start(), calls=%async_computation.2 | async-start | bytes 5308416 | tf_op jit(solution)/shard_map/reduce_scatter | solution.py:742
  54.9 24.1 %collective-permute-start.5 = (bf16[2,256,1024]{2,1,0:T(8,128)(2,1)}, bf16[2,256,1024]{2,1,0:T(8,128)(2,1)}, u32[]{:S(2)}, u32[]{:S(2)}) collective-permute-start(bf16[2,256,1024]{2,1,0:T(8,128)(2,1)} %pad_maximum_fusion.4), channel_id=1, source_target_pairs={{0,4},{4,0},{8,12},{12,8},{1,5},{5,1},{9,13},{13,9},{2,6},{6,2},{1... | collective-permute-start | bytes 3145736 | tf_op jit(solution)/shard_map/ppermute | solution.py:39
  82.5 30.1 %collective-permute-start.12 = (bf16[256,1024]{1,0:T(8,128)(2,1)S(1)}, bf16[256,1024]{1,0:T(8,128)(2,1)S(1)}, u32[]{:S(2)}, u32[]{:S(2)}) collective-permute-start(bf16[256,1024]{1,0:T(8,128)(2,1)S(1)} %copy-done.2), channel_id=1, source_target_pairs={{0,8},{4,12},{8,0},{12,4},{1,9},{5,13},{9,1},{13,5},{2,10},{6,14},... | collective-permute-start | bytes 1572872 | tf_op jit(solution)/shard_map/ppermute | solution.py:39
  114.4 27.2 %collective-permute-start.13 = (bf16[2,256,1024]{2,1,0:T(8,128)(2,1)}, bf16[2,256,1024]{2,1,0:T(8,128)(2,1)S(1)}, u32[]{:S(2)}, u32[]{:S(2)}) collective-permute-start(bf16[2,256,1024]{2,1,0:T(8,128)(2,1)} %pad_maximum_fusion.5), channel_id=1, source_target_pairs={{0,4},{4,0},{8,12},{12,8},{1,5},{5,1},{9,13},{13,9},{2,6},{6,2},{1... | collective-permute-start | bytes 3145736 | tf_op jit(solution)/shard_map/ppermute | solution.py:39
  141.6 36.2 %collective-permute-start.17 = (bf16[512,128]{1,0:T(8,128)(2,1)}, bf16[512,128]{1,0:T(8,128)(2,1)S(1)}, u32[]{:S(2)}, u32[]{:S(2)}) collective-permute-start(bf16[512,128]{1,0:T(8,128)(2,1)} %get-tuple-element.149), channel_id=1, source_target_pairs={{0,1},{1,0},{2,3},{3,2},{4,5},{5,4},{6,7},{7,6},{8,9},{9,8},{10,11... | collective-permute-start | bytes 393224 | tf_op jit(solution)/shard_map/ppermute | solution.py:39
  141.7 36.2 %collective-permute-start.18 = (bf16[512,128]{1,0:T(8,128)(2,1)}, bf16[512,128]{1,0:T(8,128)(2,1)S(1)}, u32[]{:S(2)}, u32[]{:S(2)}) collective-permute-start(bf16[512,128]{1,0:T(8,128)(2,1)} %get-tuple-element.150), channel_id=1, source_target_pairs={{0,2},{1,3},{2,0},{3,1},{4,6},{5,7},{6,4},{7,5},{8,10},{9,11},{10,... | collective-permute-start | bytes 393224 | tf_op jit(solution)/shard_map/ppermute | solution.py:39
  143.2 34.7 %collective-permute-start.19 = (bf16[512,128]{1,0:T(8,128)(2,1)}, bf16[512,128]{1,0:T(8,128)(2,1)S(1)}, u32[]{:S(2)}, u32[]{:S(2)}) collective-permute-start(bf16[512,128]{1,0:T(8,128)(2,1)} %get-tuple-element.151), channel_id=1, source_target_pairs={{0,3},{1,2},{2,1},{3,0},{4,7},{5,6},{6,5},{7,4},{8,11},{9,10},{10,... | collective-permute-start | bytes 393224 | tf_op jit(solution)/shard_map/ppermute | solution.py:39
  149.5 46.3 %collective-permute-start.14 = (bf16[512,128]{1,0:T(8,128)(2,1)}, bf16[512,128]{1,0:T(8,128)(2,1)}, u32[]{:S(2)}, u32[]{:S(2)}) collective-permute-start(bf16[512,128]{1,0:T(8,128)(2,1)} %get-tuple-element.143), channel_id=1, source_target_pairs={{0,1},{1,0},{2,3},{3,2},{4,5},{5,4},{6,7},{7,6},{8,9},{9,8},{10,11... | collective-permute-start | bytes 393224 | tf_op jit(solution)/shard_map/ppermute | solution.py:39
  149.9 46.0 %collective-permute-start.15 = (bf16[512,128]{1,0:T(8,128)(2,1)}, bf16[512,128]{1,0:T(8,128)(2,1)}, u32[]{:S(2)}, u32[]{:S(2)}) collective-permute-start(bf16[512,128]{1,0:T(8,128)(2,1)} %get-tuple-element.144), channel_id=1, source_target_pairs={{0,2},{1,3},{2,0},{3,1},{4,6},{5,7},{6,4},{7,5},{8,10},{9,11},{10,... | collective-permute-start | bytes 393224 | tf_op jit(solution)/shard_map/ppermute | solution.py:39
  177.8 18.1 %collective-permute-start.16 = (bf16[512,128]{1,0:T(8,128)(2,1)}, bf16[512,128]{1,0:T(8,128)(2,1)}, u32[]{:S(2)}, u32[]{:S(2)}) collective-permute-start(bf16[512,128]{1,0:T(8,128)(2,1)} %get-tuple-element.145), channel_id=1, source_target_pairs={{0,3},{1,2},{2,1},{3,0},{4,7},{5,6},{6,5},{7,4},{8,11},{9,10},{10,... | collective-permute-start | bytes 393224 | tf_op jit(solution)/shard_map/ppermute | solution.py:39
  195.9 137.0 %reduce-scatter.5.cloned.1.call-start = ((), (), s32[]{:S(2)}) async-start(), calls=%async_computation.3 | async-start | bytes 2064384 | tf_op jit(solution)/shard_map/reduce_scatter | solution.py:792
  198.6 36.2 %collective-permute-start.20 = (bf16[2,256,1024]{2,1,0:T(8,128)(2,1)}, bf16[2,256,1024]{2,1,0:T(8,128)(2,1)}, u32[]{:S(2)}, u32[]{:S(2)}) collective-permute-start(bf16[2,256,1024]{2,1,0:T(8,128)(2,1)} %pad_maximum_fusion.6), channel_id=1, source_target_pairs={{0,4},{4,0},{8,12},{12,8},{1,5},{5,1},{9,13},{13,9},{2,6},{6,2},{1... | collective-permute-start | bytes 3145736 | tf_op jit(solution)/shard_map/ppermute | solution.py:39
  237.1 27.5 %collective-permute-start.27 = (bf16[256,1024]{1,0:T(8,128)(2,1)}, bf16[256,1024]{1,0:T(8,128)(2,1)}, u32[]{:S(2)}, u32[]{:S(2)}) collective-permute-start(bf16[256,1024]{1,0:T(8,128)(2,1)} %fusion.14), channel_id=1, source_target_pairs={{0,8},{4,12},{8,0},{12,4},{1,9},{5,13},{9,1},{13,5},{2,10},{6,14},... | collective-permute-start | bytes 1572872 | tf_op jit(solution)/shard_map/ppermute | solution.py:39
  239.8 24.8 %collective-permute-start.21 = (bf16[1024,128]{1,0:T(8,128)(2,1)}, bf16[1024,128]{1,0:T(8,128)(2,1)S(1)}, u32[]{:S(2)}, u32[]{:S(2)}) collective-permute-start(bf16[1024,128]{1,0:T(8,128)(2,1)} %get-tuple-element.176), channel_id=1, source_target_pairs={{0,1},{1,0},{2,3},{3,2},{4,5},{5,4},{6,7},{7,6},{8,9},{9,8},{10,11... | collective-permute-start | bytes 786440 | tf_op jit(solution)/shard_map/ppermute | solution.py:39
  239.8 24.8 %collective-permute-start.22 = (bf16[1024,128]{1,0:T(8,128)(2,1)}, bf16[1024,128]{1,0:T(8,128)(2,1)}, u32[]{:S(2)}, u32[]{:S(2)}) collective-permute-start(bf16[1024,128]{1,0:T(8,128)(2,1)} %get-tuple-element.177), channel_id=1, source_target_pairs={{0,2},{1,3},{2,0},{3,1},{4,6},{5,7},{6,4},{7,5},{8,10},{9,11},{10,... | collective-permute-start | bytes 786440 | tf_op jit(solution)/shard_map/ppermute | solution.py:39
  241.1 23.5 %collective-permute-start.23 = (bf16[1024,128]{1,0:T(8,128)(2,1)}, bf16[1024,128]{1,0:T(8,128)(2,1)}, u32[]{:S(2)}, u32[]{:S(2)}) collective-permute-start(bf16[1024,128]{1,0:T(8,128)(2,1)} %get-tuple-element.178), channel_id=1, source_target_pairs={{0,3},{1,2},{2,1},{3,0},{4,7},{5,6},{6,5},{7,4},{8,11},{9,10},{10,... | collective-permute-start | bytes 786440 | tf_op jit(solution)/shard_map/ppermute | solution.py:39
  247.9 16.7 %collective-permute-start.26 = (bf16[512,128]{1,0:T(8,128)(2,1)}, bf16[512,128]{1,0:T(8,128)(2,1)}, u32[]{:S(2)}, u32[]{:S(2)}) collective-permute-start(bf16[512,128]{1,0:T(8,128)(2,1)} %get-tuple-element.182), channel_id=1, source_target_pairs={{0,3},{1,2},{2,1},{3,0},{4,7},{5,6},{6,5},{7,4},{8,11},{9,10},{10,... | collective-permute-start | bytes 393224 | tf_op jit(solution)/shard_map/ppermute | solution.py:39
  282.7 16.7 %collective-permute-start.28 = (bf16[2,256,512]{2,1,0:T(8,128)(2,1)}, bf16[2,256,512]{2,1,0:T(8,128)(2,1)}, u32[]{:S(2)}, u32[]{:S(2)}) collective-permute-start(bf16[2,256,512]{2,1,0:T(8,128)(2,1)} %pad_maximum_fusion.9), channel_id=1, source_target_pairs={{0,4},{4,0},{8,12},{12,8},{1,5},{5,1},{9,13},{13,9},{2,6},{6,2},{1... | collective-permute-start | bytes 1572872 | tf_op jit(solution)/shard_map/ppermute | solution.py:39
  300.3 19.0 %collective-permute-start.30 = (bf16[2,256,512]{2,1,0:T(8,128)(2,1)}, bf16[2,256,512]{2,1,0:T(8,128)(2,1)S(1)}, u32[]{:S(2)}, u32[]{:S(2)}) collective-permute-start(bf16[2,256,512]{2,1,0:T(8,128)(2,1)} %pad_maximum_fusion.10), channel_id=1, source_target_pairs={{0,4},{4,0},{8,12},{12,8},{1,5},{5,1},{9,13},{13,9},{2,6},{6,2},{1... | collective-permute-start | bytes 1572872 | tf_op jit(solution)/shard_map/ppermute | solution.py:39
  301.0 20.6 %collective-permute-start.35 = (bf16[32,1024]{1,0:T(8,128)(2,1)}, bf16[32,1024]{1,0:T(8,128)(2,1)S(1)}, u32[]{:S(2)}, u32[]{:S(2)}) collective-permute-start(bf16[32,1024]{1,0:T(8,128)(2,1)} %reshape.367), channel_id=1, source_target_pairs={{0,0},{1,1},{2,2},{3,3},{16,4},{17,5},{18,6},{19,7},{4,8},{5,9},{6... | collective-permute-start | bytes 196616 | tf_op jit(solution)/shard_map/ppermute | solution.py:799
  305.3 17.0 %collective-permute-start.29 = (bf16[256,512]{1,0:T(8,128)(2,1)}, bf16[256,512]{1,0:T(8,128)(2,1)}, u32[]{:S(2)}, u32[]{:S(2)}) collective-permute-start(bf16[256,512]{1,0:T(8,128)(2,1)} %fusion.15), channel_id=1, source_target_pairs={{0,8},{4,12},{8,0},{12,4},{1,9},{5,13},{9,1},{13,5},{2,10},{6,14},... | collective-permute-start | bytes 786440 | tf_op jit(solution)/shard_map/ppermute | solution.py:39
  (55 other events, 385.0 us)
Sparse Core Ops, SparseCore 0:
  29.2 29.1 all-gather.4
  60.2 36.7 all-gather.6
  196.0 59.3 reduce-scatter.2
  289.4 37.5 reduce-scatter.4

commit v3 on v2

--- a/solution.py
+++ b/solution.py
@@ -13,6 +13,7 @@
 LONGEST = 2048
 GROUP_IN = 4
 TILE = 256
+JOINT = TILE + TILE // 2
 FQ, FK = 512, 512
 BQ, BK = 512, 256
 EPS = 1e-05
@@ -111,8 +112,9 @@
         part = jnp.concatenate([joined[:, at : at + HEAD], joined[:, cols + at : cols + at + HEAD]], axis=1)
         qk.append(rotary(part, cos, sl, sr, 1.0))
         v.append(pair_up(joined[:, 2 * cols + at : 2 * cols + at + HEAD], block))
-    for ref, part in zip(out_refs, turn(z, qk) + turn(z, v)):
-        ref[...] = part.astype(BF16)
+    for ref, one, two in zip(out_refs, turn(z, qk), turn(z, v)):
+        ref[:TILE, :] = one.astype(BF16)
+        ref[TILE:, :] = two.astype(BF16)
 
 
 def prep(z, x, norms, w, bias, cos, sl, sr, block):
@@ -135,14 +137,42 @@
                 table,
                 table,
             ],
-            out_specs=[tile, tile] + [piece(TILE)] * heads + [piece(TILE // 2)] * heads,
+            out_specs=[tile, tile] + [piece(JOINT)] * heads,
         ),
-        out_shape=[norm, norm] + [bf16_rows(rows)] * heads + [bf16_rows(rows // 2)] * heads,
+        out_shape=[norm, norm] + [bf16_rows(rows // TILE * JOINT)] * heads,
         **params(2 * rows * width * w.shape[1], 12 * 2**20),
     )(z, x, norms, w, bias, cos, sl, sr)
 
 
-def feed_kernel(x_ref, n2_ref, dy_ref, norm_ref, w_in_ref, w_fc2_ref, b_ref, h_ref, du_ref, y_ref, dx_ref, sums_ref, db_ref):
+class Rows:
+    def __init__(self, n_dp, n_in, n_out, r_w):
+        self.n_in, self.n_out, self.r_w = n_in, n_out, r_w
+        self.count = n_dp * n_in * n_out
+        self.aligned = r_w % 16 == 0
+
+    def place(self, block):
+        out = block % self.n_out
+        unit = (block // self.n_out) % self.n_in
+        return block // (self.n_out * self.n_in) * self.n_out + out, unit * self.r_w
+
+
+def feed_kernel(
+    layout, x_ref, n2_ref, dy_ref, norm_ref, w_ref, b_ref, h_ref, du_ref, y_ref, dx_ref, sums_ref, db_ref, w_in_ref, w_fc2_ref
+):
+    units = w_in_ref.shape[1]
+
+    @pl.when(pl.program_id(0) == 0)
+    def _():
+        size = w_ref.shape[1]
+        for part in range(w_ref.shape[0]):
+            w_fc2_ref[part * size : (part + 1) * size, :] = w_ref[part, :, units:]
+            if not layout.aligned:
+                w_in_ref[part * size : (part + 1) * size, :] = w_ref[part, :, :units]
+        if layout.aligned:
+            for at in range(layout.count):
+                part, row = layout.place(at)
+                w_in_ref[at * layout.r_w : (at + 1) * layout.r_w, :] = w_ref[part, row : row + layout.r_w, :units]
+
     up = dot(n2_ref[...], w_in_ref[...]) + b_ref[...]
     cdf = 0.5 + 0.5 * lax.erf(up * (0.5**0.5))
     hidden = (up * cdf).astype(BF16)
@@ -167,21 +197,20 @@
     db_ref[0:1] += bias
 
 
-def feed(x, n2, dy, norms, w_in, w_fc2, bias):
+def feed(layout, x, n2, dy, norms, w, bias):
     rows, width = x.shape
-    units = w_in.shape[1]
+    units = bias.shape[1]
     row, whole = lambda i: (i, 0), lambda i: (0, 0)
     tile, tile_ff = pl.BlockSpec((TILE, width), row), pl.BlockSpec((TILE, units), row)
     return pl.pallas_call(
-        feed_kernel,
+        functools.partial(feed_kernel, layout),
         grid=(rows // TILE,),
         in_specs=[
             tile,
             tile,
             tile,
             pl.BlockSpec(norms.shape, whole),
-            pl.BlockSpec(w_in.shape, whole),
-            pl.BlockSpec(w_fc2.shape, whole),
+            pl.BlockSpec(w.shape, lambda i: (0, 0, 0)),
             pl.BlockSpec(bias.shape, whole),
         ],
         out_specs=[
@@ -200,8 +229,80 @@
             jax.ShapeDtypeStruct((8, width), F32),
             jax.ShapeDtypeStruct((8, units), F32),
         ],
+        scratch_shapes=[pltpu.VMEM((width, units), BF16), pltpu.VMEM((units, width), BF16)],
         **params(8 * rows * width * units, 24 * 2**20, 2 * rows * units),
-    )(x, n2, dy, norms, w_in, w_fc2, bias)
+    )(x, n2, dy, norms, w, bias)
+
+
+def feed_grads_kernel(layout, n2_ref, du_ref, h_ref, dy_ref, o_ref, out_ref):
+    step = pl.program_id(0)
+    size = out_ref.shape[1] // 9 * 4
+    grad = dot_tn(n2_ref[...], du_ref[...]).astype(BF16)
+    for b in range(TILE // layout.r_w):
+        part, row = layout.place(step * (TILE // layout.r_w) + b)
+        out_ref[part, pl.ds(pl.multiple_of(row, 16), layout.r_w), :] = grad[b * layout.r_w : (b + 1) * layout.r_w]
+    grad = dot_tn(h_ref[...], dy_ref[...]).astype(BF16)
+    for b in range(TILE // size):
+        out_ref[step * (TILE // size) + b, size : 2 * size, :] = grad[b * size : (b + 1) * size]
+
+    @pl.when(step == 0)
+    def _():
+        grad = dot_tn(o_ref[...], dy_ref[...]).astype(BF16)
+        for part in range(out_ref.shape[0]):
+            out_ref[part, 2 * size :, :] = grad[part * layout.r_w : (part + 1) * layout.r_w]
+
+
+def feed_grads(layout, n2, du, h, dy, o):
+    rows, width = n2.shape
+    units = h.shape[1]
+    parts = layout.count // layout.n_in
+    shape = (parts, units // parts + layout.n_in * layout.r_w + layout.r_w, width)
+    columns = pl.BlockSpec((rows, TILE), lambda i: (0, i))
+    whole = lambda i: (0, 0)
+    return pl.pallas_call(
+        functools.partial(feed_grads_kernel, layout),
+        grid=(width // TILE,),
+        in_specs=[
+            columns,
+            pl.BlockSpec(du.shape, whole),
+            columns,
+            pl.BlockSpec(dy.shape, whole),
+            pl.BlockSpec(o.shape, whole),
+        ],
+        out_specs=pl.BlockSpec(shape, lambda i: (0, 0, 0)),
+        out_shape=jax.ShapeDtypeStruct(shape, BF16),
+        **params(4 * rows * width * units, 14 * 2**20),
+    )(n2, du, h, dy, o)
+
+
+def qkv_grads_kernel(layout, n1_ref, da_ref, vec_ref, out_ref):
+    step = pl.program_id(0)
+    cols = da_ref.shape[1]
+    grad = dot_tn(n1_ref[...], da_ref[...]).astype(BF16)
+    for b in range(TILE // layout.r_w):
+        part, row = layout.place(step * (TILE // layout.r_w) + b)
+        out_ref[part, pl.ds(pl.multiple_of(row, 16), layout.r_w), :cols] = grad[b * layout.r_w : (b + 1) * layout.r_w]
+
+    @pl.when(step == 0)
+    def _():
+        out_ref[:, :, cols:] = vec_ref[...]
+
+
+def qkv_grads(layout, n1, da, vec):
+    rows, width = n1.shape
+    shape = (vec.shape[0], vec.shape[1], da.shape[1] + vec.shape[2])
+    return pl.pallas_call(
+        functools.partial(qkv_grads_kernel, layout),
+        grid=(width // TILE,),
+        in_specs=[
+            pl.BlockSpec((rows, TILE), lambda i: (0, i)),
+            pl.BlockSpec(da.shape, lambda i: (0, 0)),
+            pl.BlockSpec(vec.shape, lambda i: (0, 0, 0)),
+        ],
+        out_specs=pl.BlockSpec(shape, lambda i: (0, 0, 0)),
+        out_shape=jax.ShapeDtypeStruct(shape, BF16),
+        **params(2 * rows * width * da.shape[1], 6 * 2**20),
+    )(n1, da, vec)
 
 
 def grad_att_kernel(heads, block, z_ref, dy_ref, wo_ref, *out_refs):
@@ -259,9 +360,9 @@
     heads, block, z_ref, x_ref, dx_ref, norm_ref, w_ref, cos_ref, sl_ref, sr_ref, *refs
 ):
     z = z_ref[0]
-    dqk = turn(z, [ref[...].astype(F32) for ref in refs[:heads]])
-    dv = turn(z, [unpair(ref[...].astype(F32), block) for ref in refs[heads : 2 * heads]])
-    da_ref, sum_ref, sums_ref, db_ref = refs[2 * heads :]
+    dqk = turn(z, [ref[:TILE, :].astype(F32) for ref in refs[:heads]])
+    dv = turn(z, [unpair(ref[TILE:, :].astype(F32), block) for ref in refs[:heads]])
+    da_ref, sum_ref, sums_ref, db_ref = refs[heads:]
     cos, sl, sr = cos_ref[...], sl_ref[...], sr_ref[...]
     cols = heads * HEAD
     for h in range(0, heads, 2):
@@ -288,8 +389,8 @@
     db_ref[0:1] += bias
 
 
-def post(z, dqk, dv, x, dx, norms, w, cos, sl, sr, block):
-    heads = len(dqk)
+def post(z, grads, x, dx, norms, w, cos, sl, sr, block):
+    heads = len(grads)
     rows, width = x.shape
     three = heads * 3 * HEAD
     table = pl.BlockSpec((TILE, 2 * HEAD), row_at)
@@ -308,8 +409,7 @@
                 table,
                 table,
             ]
-            + [piece(TILE)] * heads
-            + [piece(TILE // 2)] * heads,
+            + [piece(JOINT)] * heads,
             out_specs=[
                 pl.BlockSpec((TILE, three), row_at),
                 tile,
@@ -324,7 +424,7 @@
             jax.ShapeDtypeStruct((8, three), F32),
         ],
         **params(2 * rows * width * three, 14 * 2**20),
-    )(z, x, dx, norms, w, cos, sl, sr, *dqk, *dv)
+    )(z, x, dx, norms, w, cos, sl, sr, *grads)
 
 
 def doc_start(packed, ends_ref, count):
@@ -366,13 +466,21 @@
         whole[i * size : (i + 1) * size, :] = ref[...]
 
 
+def lay_out_joint(pieces, qk, v):
+    at = 0
+    for ref in pieces:
+        for i in range(0, ref.shape[0], JOINT):
+            qk[at : at + TILE, :] = ref[i : i + TILE, :]
+            v[at // 2 : (at + TILE) // 2, :] = ref[i + TILE : i + JOINT, :]
+            at += TILE
+
+
 def forward_kernel(block, count, source_ref, packed_ref, ends_ref, *refs):
-    pieces = (len(refs) - 8) // 3
-    qk_in, v_in, o_out = refs[:pieces], refs[pieces : 2 * pieces], refs[2 * pieces : 3 * pieces]
-    o_t, lse_ref, k_s, q_t, v_t, o_s, qk_ref, v_ref = refs[3 * pieces :]
+    pieces = (len(refs) - 8) // 2
+    qkv_in, o_out = refs[:pieces], refs[pieces : 2 * pieces]
+    o_t, lse_ref, k_s, q_t, v_t, o_s, qk_ref, v_ref = refs[2 * pieces :]
     rows = qk_ref.shape[0]
-    lay_out(qk_in, qk_ref)
-    lay_out(v_in, v_ref)
+    lay_out_joint(qkv_in, qk_ref, v_ref)
     tiles = rows // TILE
     per = TILE // block
     scale = HEAD ** (-0.5)
@@ -420,28 +528,30 @@
     send_pairs(o_s, o_out, packed_ref, block)
 
 
+def load_pair(whole, row, packed_ref, block):
+    both = [whole[pl.ds(pl.multiple_of(packed_ref[row + b] * block, block), block), :] for b in range(2)]
+    return jnp.concatenate(both, axis=1).astype(BF16)
+
+
 def send_pairs(whole, out_refs, packed_ref, block):
     per = out_refs[0].shape[0] // block
     for at, ref in enumerate(out_refs):
 
         def one(i, carry):
-            row = 2 * (at * per + i)
-            both = [whole[pl.ds(pl.multiple_of(packed_ref[row + b] * block, block), block), :] for b in range(2)]
-            ref[pl.ds(pl.multiple_of(i * block, block), block), :] = jnp.concatenate(both, axis=1).astype(BF16)
+            ref[pl.ds(pl.multiple_of(i * block, block), block), :] = load_pair(whole, 2 * (at * per + i), packed_ref, block)
             return carry
 
         lax.fori_loop(0, per, one, 0)
 
 
 def backward_kernel(block, count, source_ref, packed_ref, ends_ref, *refs):
-    pieces = (len(refs) - 16) // 5
-    qk_in, v_in, do_in = [refs[i * pieces : (i + 1) * pieces] for i in range(3)]
-    o_t, lse_ref = refs[3 * pieces : 3 * pieces + 2]
-    dqk_out, dv_out = [refs[i * pieces + 2 : (i + 1) * pieces + 2] for i in (3, 4)]
-    q_s, k_s, v_s, do_s, qk_t, do_t, dq_t, delta_s, dk_s, dv_s, qk_ref, v_ref, do_ref, dqk_ref = refs[5 * pieces + 2 :]
+    pieces = (len(refs) - 16) // 3
+    qkv_in, do_in = refs[:pieces], refs[pieces : 2 * pieces]
+    o_t, lse_ref = refs[2 * pieces : 2 * pieces + 2]
+    grads_out = refs[2 * pieces + 2 : 3 * pieces + 2]
+    q_s, k_s, v_s, do_s, qk_t, do_t, dq_t, delta_s, dk_s, dv_s, qk_ref, v_ref, do_ref, dqk_ref = refs[3 * pieces + 2 :]
     rows = qk_ref.shape[0]
-    lay_out(qk_in, qk_ref)
-    lay_out(v_in, v_ref)
+    lay_out_joint(qkv_in, qk_ref, v_ref)
     lay_out(do_in, do_ref)
     tiles = rows // TILE
     per = TILE // block
@@ -505,23 +615,32 @@
 
     lax.fori_loop(0, tiles, scatter, 0)
 
-    size = rows // pieces
-    for i, ref in enumerate(dqk_out):
-        ref[...] = dqk_ref[i * size : (i + 1) * size, :]
-    send_pairs(dv_s, dv_out, packed_ref, block)
+    per_piece = rows // pieces // TILE
+    for at, ref in enumerate(grads_out):
+
+        def one(i, carry):
+            start = at * per_piece + i
+            out = pl.multiple_of(i * JOINT, JOINT)
+            ref[pl.ds(out, TILE), :] = dqk_ref[tile_at(start), :]
+            for b in range(0, per, 2):
+                row = pl.multiple_of(out + TILE + b // 2 * block, block)
+                ref[pl.ds(row, block), :] = load_pair(dv_s, start * per + b, packed_ref, block)
+            return carry
+
+        lax.fori_loop(0, per_piece, one, 0)
 
 
 IN_VMEM = pl.BlockSpec(memory_space=pltpu.VMEM)
 IN_SMEM = pl.BlockSpec(memory_space=pltpu.SMEM)
 
 
-def attend_forward(source, packed, ends, qk, v, block):
-    pieces = len(qk)
-    rows = pieces * qk[0].shape[0]
+def attend_forward(source, packed, ends, qkv, block):
+    pieces = len(qkv)
+    rows = pieces * (qkv[0].shape[0] // JOINT * TILE)
     turned = pltpu.VMEM((HEAD, rows), BF16)
     return pl.pallas_call(
         functools.partial(forward_kernel, block, ends.shape[0]),
-        in_specs=[IN_SMEM] * 3 + [IN_VMEM] * (2 * pieces),
+        in_specs=[IN_SMEM] * 3 + [IN_VMEM] * pieces,
         out_specs=[IN_VMEM] * (pieces + 2),
         out_shape=[bf16_rows(rows // (2 * pieces))] * pieces
         + [
@@ -537,21 +656,21 @@
             pltpu.VMEM((rows // 2, 2 * HEAD), BF16),
         ],
         **params(rows * rows * HEAD * 40, 6 * rows * HEAD * 2, rows * rows),
-    )(source, packed, ends, *qk, *v)
-
-
-def attend_backward(source, packed, ends, qk, v, do, o_t, lse, block):
-    pieces = len(qk)
-    rows = pieces * qk[0].shape[0]
+    )(source, packed, ends, *qkv)
+
+
+def attend_backward(source, packed, ends, qkv, do, o_t, lse, block):
+    pieces = len(qkv)
+    rows = pieces * (qkv[0].shape[0] // JOINT * TILE)
     half = pltpu.VMEM((rows, HEAD), BF16)
     wide = pltpu.VMEM((rows, HEAD), F32)
     pairs = pltpu.VMEM((rows // 2, 2 * HEAD), BF16)
     whole = pltpu.VMEM((rows, 2 * HEAD), BF16)
     return pl.pallas_call(
         functools.partial(backward_kernel, block, ends.shape[0]),
-        in_specs=[IN_SMEM] * 3 + [IN_VMEM] * (3 * pieces + 2),
-        out_specs=[IN_VMEM] * (2 * pieces),
-        out_shape=[bf16_rows(rows // pieces)] * pieces + [bf16_rows(rows // (2 * pieces))] * pieces,
+        in_specs=[IN_SMEM] * 3 + [IN_VMEM] * (2 * pieces + 2),
+        out_specs=[IN_VMEM] * pieces,
+        out_shape=[bf16_rows(qkv[0].shape[0])] * pieces,
         scratch_shapes=[
             half,
             half,
@@ -569,7 +688,7 @@
             whole,
         ],
         **params(rows * rows * HEAD * 40, 12 * rows * HEAD * 2, rows * rows),
-    )(source, packed, ends, *qk, *v, *do, o_t, lse)
+    )(source, packed, ends, *qkv, *do, o_t, lse)
 
 
 def join_in(value, far, near):
@@ -633,6 +752,7 @@
     h_in = heads // n_in
     cols = h_in * HEAD
     rows = rows_dev * n_in
+    layout = Rows(n_dp, n_in, n_out, r_w)
     z, t = lax.axis_index("out"), lax.axis_index("in")
     z_arr = z[None].astype(jnp.int32)
     lengths, order = seq_lengths[0], dealing[0]
@@ -694,8 +814,9 @@
 
     weight_qkv = natural(first[:, :, : 3 * cols])
     weight_out = first[:, :, 3 * cols + 128 :].reshape(cols, width)
-    weight_in = natural(second[:, :, :ff_in])
-    weight_fc2 = second[:, :, ff_in:].reshape(ff_in, width)
+    if not layout.aligned:
+        in_rows = natural(second[:, :, :ff_in]).reshape(n_g, n_in * r_w, ff_in)
+        second = jnp.concatenate([in_rows, second[:, :, ff_in:]], axis=2)
     vec_all = first[:, :, 3 * cols : 3 * cols + 128].reshape(n_dp, n_out, n_in, r_w * per_row, lanes)
     vec_all = jnp.transpose(vec_all[:, :, :, : len(vectors)], (3, 0, 2, 1, 4)).astype(F32)
     spans = [vec_all[i, ..., :size] for i, size in enumerate(sizes)]
@@ -711,56 +832,54 @@
     x_all, to_send = lax.optimization_barrier((x_all, cotangent))
     dy_far = xor_swap(to_send, "in", n_in, 2)
 
-    n1, n2, *parts = prep(z_arr, x_all, norms, weight_qkv, bias_qkv[None], cos, sin_l, sin_r, block)
-    qk = exchange_out(parts[:h_in])
-    v = exchange_out(parts[h_in:])
-    qk, v, dy_far = lax.optimization_barrier((qk, v, dy_far))
+    n1, n2, *qkv = prep(z_arr, x_all, norms, weight_qkv, bias_qkv[None], cos, sin_l, sin_r, block)
+    qkv = exchange_out(qkv)
+    qkv, dy_far = lax.optimization_barrier((qkv, dy_far))
     dy_near = xor_swap(jnp.stack([cotangent, dy_far]), "in", n_in, 1)
-    *o, o_t, lse = attend_forward(source, packed_of, ends, qk, v, block)
+    *o, o_t, lse = attend_forward(source, packed_of, ends, qkv, block)
     o, dy_near = lax.optimization_barrier((o, dy_near))
     dy_all = join_in(cotangent, dy_far, dy_near)
     o = exchange_out(o)
     do = exchange_out(grad_att(z_arr, dy_all, weight_out, block))
 
-    hidden, grad_up, y_ff, dx_ff, sums_two, grad_b_in = feed(x_all, n2, dy_all, norms, weight_in, weight_fc2, bias_in[None])
+    hidden, grad_up, y_ff, dx_ff, sums_two, grad_b_in = feed(
+        layout, x_all, n2, dy_all, norms, second, bias_in[None]
+    )
     o, y_ff = lax.optimization_barrier((o, y_ff))
     o, y_part = project(z_arr, o, y_ff, weight_out, block)
     y_part = y_part.reshape(n_in, rows_dev, width)
-    grad_fc2 = dot_tn(hidden, dy_all)
-    grad_in = dot_tn(n2, grad_up)
-    grad_out = dot_tn(o, dy_all)
-    second_grads = jnp.concatenate(
-        [
-            by_owner(grad_in.astype(BF16)),
-            grad_fc2.astype(BF16).reshape(n_g, r_ff, width),
-            grad_out.astype(BF16).reshape(n_g, n_in * r_w, cols),
-        ],
-        axis=2,
-    )
+    if layout.aligned:
+        second_grads = feed_grads(layout, n2, grad_up, hidden, dy_all, o)
+    else:
+        second_grads = jnp.concatenate(
+            [
+                by_owner(dot_tn(n2, grad_up).astype(BF16)),
+                dot_tn(hidden, dy_all).astype(BF16).reshape(n_g, r_ff, width),
+                dot_tn(o, dy_all).astype(BF16).reshape(n_g, r_w, width),
+            ],
+            axis=1,
+        )
 
     do, second_grads, y_part = lax.optimization_barrier((do, second_grads, y_part))
     second_grads = lax.psum_scatter(second_grads, G_AXES, scatter_dimension=0, tiled=False)
     y_near = near_in(y_part)
     own = tokens.astype(F32)
-    parts = attend_backward(source, packed_of, ends, qk, v, do, o_t, lse, block)
+    parts = attend_backward(source, packed_of, ends, qkv, do, o_t, lse, block)
     parts, y_near = lax.optimization_barrier((parts, y_near))
-    dqk = exchange_out(parts[:h_in])
-    dv = exchange_out(parts[h_in:])
+    parts = exchange_out(parts)
     y_far = xor_swap((y_part[2].astype(F32) + y_near[1].astype(F32)).astype(BF16), "in", n_in, 2)
-    dqk, dv, y_far = lax.optimization_barrier((dqk, dv, y_far))
+    parts, y_far = lax.optimization_barrier((parts, y_far))
     y_sum = y_part[0].astype(F32) + y_near[0].astype(F32) + y_far.astype(F32)
     mixed = (own + y_sum + bias_out).astype(BF16)
     da, w_parts, sums_one, grad_b_qkv = post(
-        z_arr, dqk, dv, x_all, dx_ff, norms, weight_qkv, cos, sin_l, sin_r, block
+        z_arr, parts, x_all, dx_ff, norms, weight_qkv, cos, sin_l, sin_r, block
     )
     w_parts, da, mixed, second_grads = lax.optimization_barrier((w_parts, da, mixed, second_grads))
-    in_part = exchange_in(second_grads[:, :ff_in].reshape(n_in, r_w, ff_in), t)
+    in_part = exchange_in(second_grads[: n_in * r_w].reshape(n_in, r_w, ff_in), t)
     w_parts = halves(w_parts.reshape(n_in, rows_dev, width))
     near = near_in(w_parts[0])
     near, w_next = lax.optimization_barrier((near, w_parts[1]))
     w_sum = jnp.concatenate([far_in(w_parts[0], near), far_in(w_next, near_in(w_next))], axis=1)
-
-    grad_qkv = dot_tn(n1, da)
 
     def placed(vector, axis):
         spread = jnp.expand_dims(vector, axis)
@@ -782,20 +901,17 @@
     spare = r_w * per_row - len(vectors)
     vec_grads = jnp.pad(vec_grads, ((0, 0), (0, 0), (0, 0), (0, spare), (0, 0)))
     vec_grads = jnp.transpose(vec_grads, (0, 2, 1, 3, 4)).reshape(n_g, n_in * r_w, 128)
-    first_grads = jnp.concatenate(
-        [
-            by_owner(grad_qkv.astype(BF16)),
-            vec_grads,
-        ],
-        axis=2,
-    )
+    if layout.aligned:
+        first_grads = qkv_grads(layout, n1, da, vec_grads)
+    else:
+        first_grads = jnp.concatenate([by_owner(dot_tn(n1, da).astype(BF16)), vec_grads], axis=2)
     first_grads = lax.psum_scatter(first_grads, G_AXES, scatter_dimension=0, tiled=False)
 
     in_part = in_part.reshape(n_in, r_w, n_dp, n_out, r_ff)
     grad_w_in = jnp.transpose(in_part, (1, 2, 0, 3, 4)).reshape(r_w, ff).astype(F32)
-    grad_w_fc2 = second_grads[:, ff_in : ff_in + width].astype(F32)
+    grad_w_fc2 = second_grads[n_in * r_w : n_in * r_w + r_ff].astype(F32)
     back_home = [(b, a) for a, b in home]
-    out_part = second_grads[:, ff_in + width :].reshape(r_w, width)
+    out_part = second_grads[n_in * r_w + r_ff :]
     grad_w_out = lax.ppermute(out_part, ALL_AXES, back_home).astype(F32)
     qkv_part = exchange_in(first_grads.reshape(n_in, r_w, 3 * cols + 128), t)
     qkv_grad = jnp.transpose(qkv_part[:, :, : 3 * cols].reshape(n_in, r_w, 3, cols), (1, 2, 0, 3))

time: 351 us -> 341 us (0.972)
  Pallas kernels: 104 us -> 119 us
  matrix products: 13.9 us -> 0 us
  local copies, waits for them, and re-layouts: 42.7 us -> 33.7 us
  other arithmetic: 37.5 us -> 30.5 us
  waiting for transfers between devices: 101 us -> 106 us
    pallas_call x1 -> x3, Pallas kernels: 15.3 us -> 31.8 us  [the longest x1 15.1 us: feed(): pl.pallas_call(functools.partial(feed_kernel, layout), grid=(rows // TILE...]
    dot_general x4 -> x0, matrix products: 13.9 us -> none  [dot_tn(): lax.dot_general(a, b, (((0,), (0,)), ((), ())), preferred_element_type=F32)]
    concatenate x2 -> x0, other arithmetic: 5.38 us -> none  [the longest x1 3.9 us: body(): jnp.concatenate([by_owner(grad_in.astype(BF16)), grad_fc2.astype(BF16).re...]
    ppermute x37 -> x31, waiting for transfers between devices: 101 us -> 106 us  [xor_swap(): return lax.ppermute(value, axis, [(i, i ^ step) for i in range(size)])]
    reshape x4 -> x0, local copies, waits for them, and re-layouts: 3.8 us -> none  [the longest x1 1.64 us: natural(): value = value.reshape(n_dp, n_out, n_in, r_w, -1)]
    ppermute x37 -> x31, starting transfers between devices: 36.2 us -> 33.2 us  [xor_swap(): return lax.ppermute(value, axis, [(i, i ^ step) for i in range(size)])]
  transfers between devices with their start and end apart: 43 -> 37, of which waited for: 15 -> 14; matrix products, arithmetic and copies ran while one was open for 23% -> 15% of each run, Pallas kernels for 29% -> 35%
where the time goes in v3:
time: 341 us; the launch traced here: 339 us
  Pallas kernels  119 us (35%)
  waiting for transfers between devices  106 us (31%)
  starting transfers between devices  35.6 us (10%)
  local copies, waits for them, and re-layouts  33.7 us (10%)
  other arithmetic  30.5 us (9%)
  between operations  14.6 us (4%)
    ppermute x31, waiting for transfers between devices, xor_swap(): return lax.ppermute(value, axis, [(i, i ^ step) for i in range(size)])  106 us
    pallas_call x1, Pallas kernels, attend_backward(): pl.pallas_call(functools.partial(backward_kernel, block, ends.shape[0]),...  34.9 us
    ppermute x31, starting transfers between devices, xor_swap(): return lax.ppermute(value, axis, [(i, i ^ step) for i in range(size)])  33.2 us
    pallas_call x1, Pallas kernels, attend_forward(): pl.pallas_call(functools.partial(forward_kernel, block, ends.shape[0]), i...  25.4 us
    pallas_call x1, Pallas kernels, feed(): pl.pallas_call(functools.partial(feed_kernel, layout), grid=(rows // TILE...  15.1 us
    pallas_call x1, Pallas kernels, feed_grads(): pl.pallas_call(functools.partial(feed_grads_kernel, layout), grid=(width...  10.8 us
    pallas_call x1, Pallas kernels, post(): pl.pallas_call(functools.partial(post_kernel, heads, block), grid_spec=pl...  9.08 us
    pallas_call x1, Pallas kernels, prep(): pl.pallas_call(functools.partial(prep_kernel, heads, block), grid_spec=pl...  7.95 us
  transfers between devices with their start and end apart: 37, of which 14 were waited for; matrix products, arithmetic and copies ran while one was open for 15% of the time, Pallas kernels for 35%

profile of v3, /device:TPU:0, one launch (start us, length us, event | category | flops | bytes accessed | tf_op | source)
XLA Modules:
  0.0 339.1 jit_solution(4644382559074955689)
XLA Ops:
  10.4 5.1 %collective-permute-start.2 = (bf16[32,1920]{1,0:T(8,128)(2,1)S(1)}, bf16[32,1920]{1,0:T(8,128)(2,1)S(1)}, u32[]{:S(2)}, u32[]{:S(2)}) collective-permute-start(bf16[32,1920]{1,0:T(8,128)(2,1)S(1)} %get-tuple-element.196), channel_id=1, source_target_pairs={{0,12},{4,8},{8,4},{12,0},{1,13},{5,9},{9,5},{13,1},{2,14},{6,10},... | collective-permute-start | bytes 368648 | tf_op jit(solution)/shard_map/ppermute | solution.py:40
  16.9 2.9 collective-permute-done.2
  19.8 8.2 %collective-permute-done.1 = bf16[32,1920]{1,0:T(8,128)(2,1)S(1)} collective-permute-done((bf16[32,1920]{1,0:T(8,128)(2,1)S(1)}, bf16[32,1920]{1,0:T(8,128)(2,1)S(1)}, u32[]{:S(2)}, u32[]{:S(2)}) %collective-permute-start.1) | collective-permute-done | bytes 122912 | tf_op jit(solution)/shard_map/ppermute | solution.py:40
  32.3 21.8 %collective-permute-done.4 = bf16[256,1024]{1,0:T(8,128)(2,1)S(1)} collective-permute-done((bf16[256,1024]{1,0:T(8,128)(2,1)S(1)}, bf16[256,1024]{1,0:T(8,128)(2,1)S(1)}, u32[]{:S(2)}, u32[]{:S(2)}) %collective-permute-start.4) | collective-permute-done | bytes 524320 | tf_op jit(solution)/shard_map/ppermute | solution.py:40
  55.1 3.2 fusion.11
  63.5 15.7 %collective-permute-done.5 = bf16[2,256,1024]{2,1,0:T(8,128)(2,1)} collective-permute-done((bf16[2,256,1024]{2,1,0:T(8,128)(2,1)}, bf16[2,256,1024]{2,1,0:T(8,128)(2,1)}, u32[]{:S(2)}, u32[]{:S(2)}) %collective-permute-start.5) | collective-permute-done | bytes 1048608 | tf_op jit(solution)/shard_map/ppermute | solution.py:40
  84.5 7.9 %shard_map.246 = (bf16[1024,1024]{1,0:T(8,128)(2,1)}, bf16[1024,1024]{1,0:T(8,128)(2,1)}, bf16[1536,128]{1,0:T(8,128)(2,1)}, bf16[1536,128]{1,0:T(8,128)(2,1)}, ...) custom-call(s32[1]{0:T(128)} %bitcast.z_ref, bf16[1024,1024]{1,0:T(8,128)(2,1)} %pad_maximum_fusion.x_ref, ...), custom_call_target="tpu_custom_call" | custom-call | flops 1610612736 | bytes 12582912 | tf_op jit(solution)/shard_map/pallas_call | solution.py:126
  97.8 7.0 %collective-permute-done.7.refs_2_ = bf16[1536,128]{1,0:T(8,128)(2,1)S(1)} collective-permute-done((bf16[1536,128]{1,0:T(8,128)(2,1)}, bf16[1536,128]{1,0:T(8,128)(2,1)S(1)}, u32[]{:S(2)}, u32[]{:S(2)}) %collective-permute-start.7) | collective-permute-done | bytes 393248 | tf_op jit(solution)/shard_map/ppermute | solution.py:40
  104.8 7.6 %collective-permute-done.8.refs_3_ = bf16[1536,128]{1,0:T(8,128)(2,1)} collective-permute-done((bf16[1536,128]{1,0:T(8,128)(2,1)}, bf16[1536,128]{1,0:T(8,128)(2,1)}, u32[]{:S(2)}, u32[]{:S(2)}) %collective-permute-start.8) | collective-permute-done | bytes 393248 | tf_op jit(solution)/shard_map/ppermute | solution.py:40
  114.3 25.4 %shard_map.247 = (bf16[512,128]{1,0:T(8,128)(2,1)}, bf16[512,128]{1,0:T(8,128)(2,1)}, bf16[512,128]{1,0:T(8,128)(2,1)}, bf16[512,128]{1,0:T(8,128)(2,1)}, f32[64,4096]{1,0:T(8,128)}, /*index=5*/f32[1,4096]{1,0:T(1,128)}) custom-call(s32[64]{0:T(128)} %fusion.20.source_ref, s32[64]{0:T(128)} %copy-done.21, s32[4]{0:T(128)} %bitcast.167, ...), custom_call_target="tpu_custom_call" | custom-call | flops 42949672960 | bytes 3145728 | tf_op jit(solution)/shard_map/pallas_call | solution.py:641
  143.3 4.4 %shard_map.249 = (bf16[512,128]{1,0:T(8,128)(2,1)}, bf16[512,128]{1,0:T(8,128)(2,1)}, bf16[512,128]{1,0:T(8,128)(2,1)}, bf16[512,128]{1,0:T(8,128)(2,1)}) custom-call(s32[1]{0:T(128)} %bitcast.z_ref, bf16[1024,1024]{1,0:T(8,128)(2,1)} %pad_maximum_fusion.1.dy_ref, bf16[256,1024]{1,0:T(8,128)(2,1)} %reshape.323.wo_ref), custom_call_target="tpu_custom_call" | custom-call | flops 536870912 | bytes 4194304 | tf_op jit(solution)/shard_map/pallas_call | solution.py:318
  149.5 15.1 %shard_map.248 = (bf16[1024,1024]{1,0:T(8,128)(2,1)}, bf16[1024,1024]{1,0:T(8,128)(2,1)}, f32[1024,1024]{1,0:T(8,128)}, f32[1024,1024]{1,0:T(8,128)}, f32[8,1024]{1,0:T(8,128)}, /*index=5*/f32[8,1024]{1,0:T(8,128)}) custom-call(bf16[1024,1024]{1,0:T(8,128)(2,1)} %pad_maximum_fusion.x_ref, bf16[1024,1024]{1,0:T(8,128)(2,1)} %get-tuple-element.97.n2_ref, ...), custom_call_target="tpu_custom_call" | custom-call | flops 8589934592 | bytes 25165824 | tf_op jit(solution)/shard_map/pallas_call | solution.py:205
  165.4 5.3 %shard_map.250 = (bf16[1024,256]{1,0:T(8,128)(2,1)}, bf16[1024,1024]{1,0:T(8,128)(2,1)}) custom-call(s32[1]{0:T(128)} %bitcast.z_ref, f32[1024,1024]{1,0:T(8,128)} %get-tuple-element.125.y_ref, bf16[256,1024]{1,0:T(8,128)(2,1)} %reshape.323.wo_ref, bf16[512,128]{1,0:T(8,128)(2,1)} %get-tuple-element.126.refs_0_, bf16[512,128]{1,0:T(8,128)(2,1)} %copy-done.8, ...), custom_call_target="tpu_custom_call" | custom-call | flops 536870912 | bytes 8388608 | tf_op jit(solution)/shard_map/pallas_call | solution.py:343
  170.8 10.8 %shard_map.251 = bf16[8,288,1024]{2,1,0:T(8,128)(2,1)} custom-call(bf16[1024,1024]{1,0:T(8,128)(2,1)} %get-tuple-element.97.n2_ref, bf16[1024,1024]{1,0:T(8,128)(2,1)} %get-tuple-element.118.du_ref, bf16[1024,1024]{1,0:T(8,128)(2,1)} %get-tuple-element.119.h_ref, bf16[1024,1024]{1,0:T(8,128)(2,1)} %pad_maximum_fusion.1.dy_ref, ...), custom_call_target="tpu_custom_call" | custom-call | flops 4294967296 | bytes 14680064 | tf_op jit(solution)/shard_map/pallas_call | solution.py:262
  184.8 34.9 %shard_map.252 = (bf16[1536,128]{1,0:T(8,128)(2,1)}, bf16[1536,128]{1,0:T(8,128)(2,1)}, bf16[1536,128]{1,0:T(8,128)(2,1)}, bf16[1536,128]{1,0:T(8,128)(2,1)}) custom-call(s32[64]{0:T(128)} %fusion.20.source_ref, s32[64]{0:T(128)} %copy-done.21, s32[4]{0:T(128)} %bitcast.168, bf16[1536,128]{1,0:T(8,128)(2,1)} %get-tuple-element.103.refs_0_, ...), custom_call_target="tpu_custom_call" | custom-call | flops 42949672960 | bytes 6291456 | tf_op jit(solution)/shard_map/pallas_call | solution.py:669
  234.9 6.8 %collective-permute-done.19.refs_2_ = bf16[1536,128]{1,0:T(8,128)(2,1)} collective-permute-done((bf16[1536,128]{1,0:T(8,128)(2,1)}, bf16[1536,128]{1,0:T(8,128)(2,1)}, u32[]{:S(2)}, u32[]{:S(2)}) %collective-permute-start.19) | collective-permute-done | bytes 393248 | tf_op jit(solution)/shard_map/ppermute | solution.py:40
  241.8 7.9 %collective-permute-done.20.refs_3_ = bf16[1536,128]{1,0:T(8,128)(2,1)} collective-permute-done((bf16[1536,128]{1,0:T(8,128)(2,1)}, bf16[1536,128]{1,0:T(8,128)(2,1)}, u32[]{:S(2)}, u32[]{:S(2)}) %collective-permute-start.20) | collective-permute-done | bytes 393248 | tf_op jit(solution)/shard_map/ppermute | solution.py:40
  249.7 9.1 %shard_map.253 = (bf16[1024,768]{1,0:T(8,128)(2,1)}, bf16[1024,1024]{1,0:T(8,128)(2,1)}, f32[8,1024]{1,0:T(8,128)}, f32[8,768]{1,0:T(8,128)}) custom-call(s32[1]{0:T(128)} %bitcast.z_ref, bf16[1024,1024]{1,0:T(8,128)(2,1)} %pad_maximum_fusion.x_ref, f32[1024,1024]{1,0:T(8,128)} %get-tuple-element.113.dx_ref, f32[8,1024]{1,0:T(8,128)} %concatenate.23.norm_ref, ...), custom_call_target="tpu_custom_call" | custom-call | flops 1610612736 | bytes 14680064 | tf_op jit(solution)/shard_map/pallas_call | solution.py:398
  262.9 2.4 fusion.8
  269.6 5.9 %shard_map.254 = bf16[8,128,896]{2,1,0:T(8,128)(2,1)} custom-call(bf16[1024,1024]{1,0:T(8,128)(2,1)} %get-tuple-element.160.n1_ref, bf16[1024,768]{1,0:T(8,128)(2,1)} %get-tuple-element.161.da_ref, bf16[8,128,128]{2,1,0:T(8,128)(2,1)} %bitcast.153), custom_call_target="tpu_custom_call" | custom-call | flops 1610612736 | bytes 6291456 | tf_op jit(solution)/shard_map/pallas_call | solution.py:294
  285.8 2.1 collective-permute-done.31
  291.5 14.1 %collective-permute-done.24 = bf16[2,256,512]{2,1,0:T(8,128)(2,1)S(1)} collective-permute-done((bf16[2,256,512]{2,1,0:T(8,128)(2,1)S(1)}, bf16[2,256,512]{2,1,0:T(8,128)(2,1)S(1)}, u32[]{:S(2)}, u32[]{:S(2)}) %collective-permute-start.24) | collective-permute-done | bytes 524320 | tf_op jit(solution)/shard_map/ppermute | solution.py:40
  309.9 9.2 %collective-permute-done.25 = bf16[256,512]{1,0:T(8,128)(2,1)} collective-permute-done((bf16[256,512]{1,0:T(8,128)(2,1)S(1)}, bf16[256,512]{1,0:T(8,128)(2,1)}, u32[]{:S(2)}, u32[]{:S(2)}) %collective-permute-start.25) | collective-permute-done | bytes 262176 | tf_op jit(solution)/shard_map/ppermute | solution.py:40
  323.2 2.8 collective-permute-start.26
  (259 shorter events, 88.8 us)
Async XLA Ops:
  7.3 51.1 %all-gather.5.cloned.1.call-start = ((), (), s32[]{:S(2)}) async-start(), calls=%async_computation.4 | async-start | bytes 2654208 | tf_op jit(solution)/shard_map/all_gather | solution.py:803
  29.1 120.5 %all-gather.7.cloned.1.call-start = ((), (), s32[]{:S(2)}) async-start(), calls=%async_computation.5 | async-start | bytes 4718592 | tf_op jit(solution)/shard_map/all_gather | solution.py:805
  29.6 24.5 %collective-permute-start.4 = (bf16[256,1024]{1,0:T(8,128)(2,1)S(1)}, bf16[256,1024]{1,0:T(8,128)(2,1)S(1)}, u32[]{:S(2)}, u32[]{:S(2)}) collective-permute-start(bf16[256,1024]{1,0:T(8,128)(2,1)S(1)} %copy-done), channel_id=1, source_target_pairs={{0,8},{4,12},{8,0},{12,4},{1,9},{5,13},{9,1},{13,5},{2,10},{6,14},... | collective-permute-start | bytes 1572872 | tf_op jit(solution)/shard_map/ppermute | solution.py:40
  31.8 233.5 %reduce-scatter.3.cloned.1.call-start = ((), (), s32[]{:S(2)}) async-start(), calls=%async_computation.2 | async-start | bytes 5308416 | tf_op jit(solution)/shard_map/reduce_scatter | solution.py:864
  55.1 24.1 %collective-permute-start.5 = (bf16[2,256,1024]{2,1,0:T(8,128)(2,1)}, bf16[2,256,1024]{2,1,0:T(8,128)(2,1)}, u32[]{:S(2)}, u32[]{:S(2)}) collective-permute-start(bf16[2,256,1024]{2,1,0:T(8,128)(2,1)} %pad_maximum_fusion.2), channel_id=1, source_target_pairs={{0,4},{4,0},{8,12},{12,8},{1,5},{5,1},{9,13},{13,9},{2,6},{6,2},{1... | collective-permute-start | bytes 3145736 | tf_op jit(solution)/shard_map/ppermute | solution.py:40
  82.6 29.8 %collective-permute-start.9 = (bf16[256,1024]{1,0:T(8,128)(2,1)S(1)}, bf16[256,1024]{1,0:T(8,128)(2,1)S(1)}, u32[]{:S(2)}, u32[]{:S(2)}) collective-permute-start(bf16[256,1024]{1,0:T(8,128)(2,1)S(1)} %copy-done.1), channel_id=1, source_target_pairs={{0,8},{4,12},{8,0},{12,4},{1,9},{5,13},{9,1},{13,5},{2,10},{6,14},... | collective-permute-start | bytes 1572872 | tf_op jit(solution)/shard_map/ppermute | solution.py:40
  94.1 18.2 %collective-permute-start.8 = (bf16[1536,128]{1,0:T(8,128)(2,1)}, bf16[1536,128]{1,0:T(8,128)(2,1)}, u32[]{:S(2)}, u32[]{:S(2)}) collective-permute-start(bf16[1536,128]{1,0:T(8,128)(2,1)} %get-tuple-element.101), channel_id=1, source_target_pairs={{0,3},{1,2},{2,1},{3,0},{4,7},{5,6},{6,5},{7,4},{8,11},{9,10},{10,... | collective-permute-start | bytes 1179656 | tf_op jit(solution)/shard_map/ppermute | solution.py:40
  112.5 27.3 %collective-permute-start.10 = (bf16[2,256,1024]{2,1,0:T(8,128)(2,1)S(1)}, bf16[2,256,1024]{2,1,0:T(8,128)(2,1)S(1)}, u32[]{:S(2)}, u32[]{:S(2)}) collective-permute-start(bf16[2,256,1024]{2,1,0:T(8,128)(2,1)S(1)} %pad_maximum_fusion.3), channel_id=1, source_target_pairs={{0,4},{4,0},{8,12},{12,8},{1,5},{5,1},{9,13},{13,9},{2,6},{6,2},{1... | collective-permute-start | bytes 3145736 | tf_op jit(solution)/shard_map/ppermute | solution.py:40
  139.8 24.9 %collective-permute-start.14 = (bf16[512,128]{1,0:T(8,128)(2,1)}, bf16[512,128]{1,0:T(8,128)(2,1)S(1)}, u32[]{:S(2)}, u32[]{:S(2)}) collective-permute-start(bf16[512,128]{1,0:T(8,128)(2,1)} %get-tuple-element.121), channel_id=1, source_target_pairs={{0,1},{1,0},{2,3},{3,2},{4,5},{5,4},{6,7},{7,6},{8,9},{9,8},{10,11... | collective-permute-start | bytes 393224 | tf_op jit(solution)/shard_map/ppermute | solution.py:40
  139.8 24.9 %collective-permute-start.15 = (bf16[512,128]{1,0:T(8,128)(2,1)}, bf16[512,128]{1,0:T(8,128)(2,1)S(1)}, u32[]{:S(2)}, u32[]{:S(2)}) collective-permute-start(bf16[512,128]{1,0:T(8,128)(2,1)} %get-tuple-element.122), channel_id=1, source_target_pairs={{0,2},{1,3},{2,0},{3,1},{4,6},{5,7},{6,4},{7,5},{8,10},{9,11},{10,... | collective-permute-start | bytes 393224 | tf_op jit(solution)/shard_map/ppermute | solution.py:40
  141.4 23.4 %collective-permute-start.16 = (bf16[512,128]{1,0:T(8,128)(2,1)}, bf16[512,128]{1,0:T(8,128)(2,1)S(1)}, u32[]{:S(2)}, u32[]{:S(2)}) collective-permute-start(bf16[512,128]{1,0:T(8,128)(2,1)} %get-tuple-element.123), channel_id=1, source_target_pairs={{0,3},{1,2},{2,1},{3,0},{4,7},{5,6},{6,5},{7,4},{8,11},{9,10},{10,... | collective-permute-start | bytes 393224 | tf_op jit(solution)/shard_map/ppermute | solution.py:40
  147.7 33.9 %collective-permute-start.11 = (bf16[512,128]{1,0:T(8,128)(2,1)}, bf16[512,128]{1,0:T(8,128)(2,1)S(1)}, u32[]{:S(2)}, u32[]{:S(2)}) collective-permute-start(bf16[512,128]{1,0:T(8,128)(2,1)} %get-tuple-element.115), channel_id=1, source_target_pairs={{0,1},{1,0},{2,3},{3,2},{4,5},{5,4},{6,7},{7,6},{8,9},{9,8},{10,11... | collective-permute-start | bytes 393224 | tf_op jit(solution)/shard_map/ppermute | solution.py:40
  148.0 33.5 %collective-permute-start.12 = (bf16[512,128]{1,0:T(8,128)(2,1)}, bf16[512,128]{1,0:T(8,128)(2,1)S(1)}, u32[]{:S(2)}, u32[]{:S(2)}) collective-permute-start(bf16[512,128]{1,0:T(8,128)(2,1)} %get-tuple-element.116), channel_id=1, source_target_pairs={{0,2},{1,3},{2,0},{3,1},{4,6},{5,7},{6,4},{7,5},{8,10},{9,11},{10,... | collective-permute-start | bytes 393224 | tf_op jit(solution)/shard_map/ppermute | solution.py:40
  164.6 16.9 %collective-permute-start.13 = (bf16[512,128]{1,0:T(8,128)(2,1)S(1)}, bf16[512,128]{1,0:T(8,128)(2,1)S(1)}, u32[]{:S(2)}, u32[]{:S(2)}) collective-permute-start(bf16[512,128]{1,0:T(8,128)(2,1)S(1)} %copy-done.28), channel_id=1, source_target_pairs={{0,3},{1,2},{2,1},{3,0},{4,7},{5,6},{6,5},{7,4},{8,11},{9,10},{10,... | collective-permute-start | bytes 393224 | tf_op jit(solution)/shard_map/ppermute | solution.py:40
  182.3 138.3 %reduce-scatter.5.cloned.1.call-start = ((), (), s32[]{:S(2)}) async-start(), calls=%async_computation.3 | async-start | bytes 2064384 | tf_op jit(solution)/shard_map/reduce_scatter | solution.py:908
  184.5 35.2 %collective-permute-start.17 = (bf16[2,256,1024]{2,1,0:T(8,128)(2,1)}, bf16[2,256,1024]{2,1,0:T(8,128)(2,1)}, u32[]{:S(2)}, u32[]{:S(2)}) collective-permute-start(bf16[2,256,1024]{2,1,0:T(8,128)(2,1)} %pad_maximum_fusion.4), channel_id=1, source_target_pairs={{0,4},{4,0},{8,12},{12,8},{1,5},{5,1},{9,13},{13,9},{2,6},{6,2},{1... | collective-permute-start | bytes 3145736 | tf_op jit(solution)/shard_map/ppermute | solution.py:40
  221.8 27.9 %collective-permute-start.21 = (bf16[256,1024]{1,0:T(8,128)(2,1)}, bf16[256,1024]{1,0:T(8,128)(2,1)}, u32[]{:S(2)}, u32[]{:S(2)}) collective-permute-start(bf16[256,1024]{1,0:T(8,128)(2,1)} %fusion.14), channel_id=1, source_target_pairs={{0,8},{4,12},{8,0},{12,4},{1,9},{5,13},{9,1},{13,5},{2,10},{6,14},... | collective-permute-start | bytes 1572872 | tf_op jit(solution)/shard_map/ppermute | solution.py:40
  224.6 17.2 %collective-permute-start.19 = (bf16[1536,128]{1,0:T(8,128)(2,1)}, bf16[1536,128]{1,0:T(8,128)(2,1)}, u32[]{:S(2)}, u32[]{:S(2)}) collective-permute-start(bf16[1536,128]{1,0:T(8,128)(2,1)} %get-tuple-element.145), channel_id=1, source_target_pairs={{0,2},{1,3},{2,0},{3,1},{4,6},{5,7},{6,4},{7,5},{8,10},{9,11},{10,... | collective-permute-start | bytes 1179656 | tf_op jit(solution)/shard_map/ppermute | solution.py:40
  224.7 25.0 %collective-permute-start.20 = (bf16[1536,128]{1,0:T(8,128)(2,1)}, bf16[1536,128]{1,0:T(8,128)(2,1)}, u32[]{:S(2)}, u32[]{:S(2)}) collective-permute-start(bf16[1536,128]{1,0:T(8,128)(2,1)} %get-tuple-element.146), channel_id=1, source_target_pairs={{0,3},{1,2},{2,1},{3,0},{4,7},{5,6},{6,5},{7,4},{8,11},{9,10},{10,... | collective-permute-start | bytes 1179656 | tf_op jit(solution)/shard_map/ppermute | solution.py:40
  267.2 16.0 %collective-permute-start.22 = (bf16[2,256,512]{2,1,0:T(8,128)(2,1)}, bf16[2,256,512]{2,1,0:T(8,128)(2,1)S(1)}, u32[]{:S(2)}, u32[]{:S(2)}) collective-permute-start(bf16[2,256,512]{2,1,0:T(8,128)(2,1)} %pad_maximum_fusion.7), channel_id=1, source_target_pairs={{0,4},{4,0},{8,12},{12,8},{1,5},{5,1},{9,13},{13,9},{2,6},{6,2},{1... | collective-permute-start | bytes 1572872 | tf_op jit(solution)/shard_map/ppermute | solution.py:40
  283.3 22.3 %collective-permute-start.24 = (bf16[2,256,512]{2,1,0:T(8,128)(2,1)S(1)}, bf16[2,256,512]{2,1,0:T(8,128)(2,1)S(1)}, u32[]{:S(2)}, u32[]{:S(2)}) collective-permute-start(bf16[2,256,512]{2,1,0:T(8,128)(2,1)S(1)} %pad_maximum_fusion.8), channel_id=1, source_target_pairs={{0,4},{4,0},{8,12},{12,8},{1,5},{5,1},{9,13},{13,9},{2,6},{6,2},{1... | collective-permute-start | bytes 1572872 | tf_op jit(solution)/shard_map/ppermute | solution.py:40
  284.3 23.6 %collective-permute-start.29 = (bf16[32,1024]{1,0:T(8,128)(2,1)}, bf16[32,1024]{1,0:T(8,128)(2,1)S(1)}, u32[]{:S(2)}, u32[]{:S(2)}) collective-permute-start(bf16[32,1024]{1,0:T(8,128)(2,1)} %slice.224), channel_id=1, source_target_pairs={{0,0},{1,1},{2,2},{3,3},{16,4},{17,5},{18,6},{19,7},{4,8},{5,9},{6... | collective-permute-start | bytes 196616 | tf_op jit(solution)/shard_map/ppermute | solution.py:915
  289.8 18.7 %collective-permute-start.23 = (bf16[256,512]{1,0:T(8,128)(2,1)}, bf16[256,512]{1,0:T(8,128)(2,1)}, u32[]{:S(2)}, u32[]{:S(2)}) collective-permute-start(bf16[256,512]{1,0:T(8,128)(2,1)} %fusion.15), channel_id=1, source_target_pairs={{0,8},{4,12},{8,0},{12,4},{1,9},{5,13},{9,1},{13,5},{2,10},{6,14},... | collective-permute-start | bytes 786440 | tf_op jit(solution)/shard_map/ppermute | solution.py:40
  305.7 13.3 %collective-permute-start.25 = (bf16[256,512]{1,0:T(8,128)(2,1)S(1)}, bf16[256,512]{1,0:T(8,128)(2,1)}, u32[]{:S(2)}, u32[]{:S(2)}) collective-permute-start(bf16[256,512]{1,0:T(8,128)(2,1)S(1)} %fusion.16), channel_id=1, source_target_pairs={{0,8},{4,12},{8,0},{12,4},{1,9},{5,13},{9,1},{13,5},{2,10},{6,14},... | collective-permute-start | bytes 786440 | tf_op jit(solution)/shard_map/ppermute | solution.py:40
  (44 other events, 299.0 us)
Sparse Core Ops, SparseCore 0:
  29.2 29.1 all-gather.4
  60.2 36.7 all-gather.6
  181.8 57.9 reduce-scatter.2
  275.7 38.1 reduce-scatter.4

commit v4 on v3

--- a/solution.py
+++ b/solution.py
@@ -328,12 +328,36 @@
     )(z, dy, wo)
 
 
+def split_parts(step, total, keep_refs, near_refs):
+    low = total.astype(BF16)
+    half = total.shape[1] // 2
+
+    @pl.when(step % 2 == 0)
+    def _():
+        for at, ref in enumerate(keep_refs):
+            ref[...] = low[:, at * half : (at + 1) * half]
+
+    @pl.when(step % 2 == 1)
+    def _():
+        for at, ref in enumerate(near_refs):
+            ref[...] = low[:, at * half : (at + 1) * half]
+
+
+def half_tile(width):
+    return pl.BlockSpec((TILE, width // 2), lambda i, z: (i // 2, 0))
+
+
+def half_parts(rows, width):
+    return jax.ShapeDtypeStruct((rows // 2, width // 2), BF16)
+
+
 def project_kernel(heads, block, z_ref, y_ref, wo_ref, *refs):
     parts = turn(z_ref[0], [unpair(ref[...].astype(F32), block) for ref in refs[:heads]])
-    o_ref, out_ref = refs[heads:]
+    o_ref = refs[heads]
     for h in range(0, heads, 2):
         o_ref[:, h * HEAD : (h + 2) * HEAD] = jnp.concatenate(parts[h : h + 2], axis=1).astype(BF16)
-    out_ref[...] = (y_ref[...] + dot(o_ref[...], wo_ref[...])).astype(BF16)
+    total = y_ref[...] + dot(o_ref[...], wo_ref[...])
+    split_parts(pl.program_id(0), total, refs[heads + 1 : heads + 3], refs[heads + 3 :])
 
 
 def project(z, parts, y, wo, block):
@@ -346,12 +370,9 @@
             num_scalar_prefetch=1,
             grid=(rows // TILE,),
             in_specs=[tile, pl.BlockSpec(wo.shape, whole_at)] + [piece(TILE // 2)] * heads,
-            out_specs=[pl.BlockSpec((TILE, heads * HEAD), row_at), tile],
+            out_specs=[pl.BlockSpec((TILE, heads * HEAD), row_at)] + [half_tile(width)] * 4,
         ),
-        out_shape=[
-            jax.ShapeDtypeStruct((rows, heads * HEAD), BF16),
-            jax.ShapeDtypeStruct((rows, width), BF16),
-        ],
+        out_shape=[jax.ShapeDtypeStruct((rows, heads * HEAD), BF16)] + [half_parts(rows, width)] * 4,
         **params(2 * rows * width * wo.shape[0], 8 * 2**20),
     )(z, y, wo, *parts)
 
@@ -362,7 +383,7 @@
     z = z_ref[0]
     dqk = turn(z, [ref[:TILE, :].astype(F32) for ref in refs[:heads]])
     dv = turn(z, [unpair(ref[TILE:, :].astype(F32), block) for ref in refs[:heads]])
-    da_ref, sum_ref, sums_ref, db_ref = refs[heads:]
+    da_ref, sums_ref, db_ref = refs[heads : heads + 3]
     cos, sl, sr = cos_ref[...], sl_ref[...], sr_ref[...]
     cols = heads * HEAD
     for h in range(0, heads, 2):
@@ -374,7 +395,8 @@
         da_ref[:, 2 * cols + at : 2 * cols + at + 2 * HEAD] = jnp.concatenate(dv[h : h + 2], axis=1).astype(BF16)
     grad = da_ref[...]
     grad_norm = dot_nt(grad, w_ref[...])
-    sum_ref[...] = (dx_ref[...] + grad_norm * norm_ref[0:1]).astype(BF16)
+    total = dx_ref[...] + grad_norm * norm_ref[0:1]
+    split_parts(pl.program_id(0), total, refs[heads + 3 : heads + 5], refs[heads + 5 :])
     gain = jnp.sum(grad_norm * normalized(x_ref), axis=0, keepdims=True)
     shift = jnp.sum(grad_norm, axis=0, keepdims=True)
     bias = jnp.sum(grad.astype(F32), axis=0, keepdims=True)
@@ -412,17 +434,17 @@
             + [piece(JOINT)] * heads,
             out_specs=[
                 pl.BlockSpec((TILE, three), row_at),
-                tile,
                 pl.BlockSpec((8, width), whole_at),
                 pl.BlockSpec((8, three), whole_at),
-            ],
+            ]
+            + [half_tile(width)] * 4,
         ),
         out_shape=[
             jax.ShapeDtypeStruct((rows, three), BF16),
-            jax.ShapeDtypeStruct((rows, width), BF16),
             jax.ShapeDtypeStruct((8, width), F32),
             jax.ShapeDtypeStruct((8, three), F32),
-        ],
+        ]
+        + [half_parts(rows, width)] * 4,
         **params(2 * rows * width * three, 14 * 2**20),
     )(z, x, dx, norms, w, cos, sl, sr, *grads)
 
@@ -450,8 +472,10 @@
     return jnp.where(source % 2 == 0, both[:, :HEAD], both[:, HEAD:])
 
 
-def masked_scores(k_s, q_t, ends_ref, count, i, j, q_size, k_size):
+def scores(masked, k_s, q_t, ends_ref, count, i, j, q_size, k_size):
     s = dot(k_s[tile_at(j, k_size), :], q_t[:HEAD, tile_at(i, q_size)])
+    if not masked:
+        return s
     key_at = lax.broadcasted_iota(jnp.int32, (k_size, q_size), 0)
     query_at = lax.broadcasted_iota(jnp.int32, (k_size, q_size), 1)
     query_row = i * q_size + lax.broadcasted_iota(jnp.int32, (1, q_size), 1)
@@ -497,14 +521,14 @@
         v_t[:, tile_at(i)] = v.T.astype(BF16)
         return carry
 
-    lax.fori_loop(0, tiles, gather, 0)
+    lax.fori_loop(0, tiles, gather, 0, unroll=4)
 
     def forward(i, carry):
         here = tile_at(i, FQ)
 
-        def step(j, state):
+        def step(masked, j, state):
             top, total, acc = state
-            s = masked_scores(k_s, q_t, ends_ref, count, i, j, FQ, FK)
+            s = scores(masked, k_s, q_t, ends_ref, count, i, j, FQ, FK)
             new_top = jnp.maximum(top, jnp.max(s, axis=0, keepdims=True))
             p = jnp.exp(s - new_top)
             fade = jnp.exp(top - new_top)
@@ -513,10 +537,14 @@
             return new_top, total, acc
 
         low = doc_start(i * FQ, ends_ref, count) // FK
-        high = (i * FQ + FQ - 1) // FK
-        top, total, acc = lax.fori_loop(
-            low, high + 1, step, (jnp.full((1, FQ), NEG, F32), jnp.zeros((1, FQ), F32), jnp.zeros((HEAD, FQ), F32))
-        )
+        high = (i * FQ + FQ - 1) // FK + 1
+        inner_low = (doc_start(i * FQ + FQ - 1, ends_ref, count) + FK - 1) // FK
+        inner_high = jnp.maximum((i * FQ + 1) // FK, low)
+        inner_low = jnp.clip(inner_low, low, inner_high)
+        state = (jnp.full((1, FQ), NEG, F32), jnp.zeros((1, FQ), F32), jnp.zeros((HEAD, FQ), F32))
+        state = lax.fori_loop(low, inner_low, functools.partial(step, True), state)
+        state = lax.fori_loop(inner_low, inner_high, functools.partial(step, False), state)
+        top, total, acc = lax.fori_loop(inner_high, high, functools.partial(step, True), state)
         out = acc / total
         lse_ref[:, here] = top + jnp.log(total)
         o_t[:, here] = out
@@ -541,7 +569,7 @@
             ref[pl.ds(pl.multiple_of(i * block, block), block), :] = load_pair(whole, 2 * (at * per + i), packed_ref, block)
             return carry
 
-        lax.fori_loop(0, per, one, 0)
+        lax.fori_loop(0, per, one, 0, unroll=4)
 
 
 def backward_kernel(block, count, source_ref, packed_ref, ends_ref, *refs):
@@ -579,15 +607,15 @@
         delta_s[:, here] = jnp.sum(o_t[:, here] * do_turned, axis=0, keepdims=True)
         return carry
 
-    lax.fori_loop(0, tiles, gather, 0)
+    lax.fori_loop(0, tiles, gather, 0, unroll=4)
 
     def backward(j, carry):
         keys = tile_at(j, BK)
 
-        def step(i, state):
+        def step(masked, i, state):
             dk, dv = state
             here = tile_at(i, BQ)
-            p = jnp.exp(masked_scores(k_s, qk_t, ends_ref, count, i, j, BQ, BK) - lse_ref[:, here])
+            p = jnp.exp(scores(masked, k_s, qk_t, ends_ref, count, i, j, BQ, BK) - lse_ref[:, here])
             dp = dot(v_s[keys, :], do_t[:, here])
             ds = (p * (dp - delta_s[:, here])).astype(BF16)
             dv = dv + dot(p.astype(BF16), do_s[here, :])
@@ -595,9 +623,14 @@
             dq_t[:, here] += dot(qk_t[HEAD:, keys], ds)
             return dk, dv
 
-        high = (doc_end(j * BK + BK - 1, ends_ref, count) - 1) // BQ
+        low = j * BK // BQ
+        high = (doc_end(j * BK + BK - 1, ends_ref, count) - 1) // BQ + 1
+        inner_low = jnp.minimum((j * BK + BK - 1 + BQ - 1) // BQ, high)
+        inner_high = jnp.clip(doc_end(j * BK, ends_ref, count) // BQ, inner_low, high)
         zero = jnp.zeros((BK, HEAD), F32)
-        dk, dv = lax.fori_loop(j * BK // BQ, high + 1, step, (zero, zero))
+        state = lax.fori_loop(low, inner_low, functools.partial(step, True), (zero, zero))
+        state = lax.fori_loop(inner_low, inner_high, functools.partial(step, False), state)
+        dk, dv = lax.fori_loop(inner_high, high, functools.partial(step, True), state)
         dk_s[keys, :] = dk
         dv_s[keys, :] = dv
         return carry
@@ -613,7 +646,7 @@
             dqk_ref[dst, :] = dqk[b * block : (b + 1) * block, :]
         return carry
 
-    lax.fori_loop(0, tiles, scatter, 0)
+    lax.fori_loop(0, tiles, scatter, 0, unroll=4)
 
     per_piece = rows // pieces // TILE
     for at, ref in enumerate(grads_out):
@@ -627,7 +660,7 @@
                 ref[pl.ds(row, block), :] = load_pair(dv_s, start * per + b, packed_ref, block)
             return carry
 
-        lax.fori_loop(0, per_piece, one, 0)
+        lax.fori_loop(0, per_piece, one, 0, unroll=2)
 
 
 IN_VMEM = pl.BlockSpec(memory_space=pltpu.VMEM)
@@ -695,18 +728,19 @@
     return jnp.concatenate([value, near[0], far, near[1]])
 
 
-def halves(parts):
-    cut = parts.shape[-1] // 2
-    return [parts[..., :cut], parts[..., cut:]]
-
-
-def near_in(parts):
-    return xor_swap(jnp.stack([parts[1], parts[3]]), "in", GROUP_IN, 1)
-
-
-def far_in(parts, near):
-    far = xor_swap((parts[2].astype(F32) + near[1].astype(F32)).astype(BF16), "in", GROUP_IN, 2)
-    return parts[0].astype(F32) + near[0].astype(F32) + far.astype(F32)
+def near_in(near):
+    return xor_swap(near, "in", GROUP_IN, 1)
+
+
+def far_in(keep, near):
+    size = keep.shape[0] // 2
+    return xor_swap((keep[size:].astype(F32) + near[size:].astype(F32)).astype(BF16), "in", GROUP_IN, 2)
+
+
+def total(keep, near, far):
+    size = far[0].shape[0]
+    parts = [k[:size].astype(F32) + n[:size].astype(F32) + f.astype(F32) for k, n, f in zip(keep, near, far)]
+    return jnp.concatenate(parts, axis=1)
 
 
 def exchange_in(parts, t):
@@ -773,15 +807,6 @@
     packed = packed.reshape(rows)
     starts = jnp.max(jnp.where(packed[:, None] >= ends[None, :], ends[None, :], 0), axis=1)
     position = (packed - starts).astype(F32)
-    lane = jnp.arange(2 * HEAD, dtype=jnp.int32) % HEAD
-    half = ROT // 2
-    freq = 10000.0 ** (-2.0 * (lane % half).astype(F32) / ROT)
-    phase = position[:, None] * freq[None, :]
-    cos = jnp.where(lane < ROT, jnp.cos(phase), 1.0)
-    sine = jnp.sin(phase)
-    sin_l = jnp.where(lane < half, sine, 0.0)
-    sin_r = jnp.where((lane >= half) & (lane < ROT), sine, 0.0)
-
     vectors = [ln1_gain, ln1_bias, ln2_gain, ln2_bias, b_qkv, b_out, b_in]
     sizes = [v.shape[0] for v in vectors]
     per_row = -(-len(vectors) // r_w)
@@ -800,7 +825,7 @@
     first = jnp.concatenate([joined_cols[:, : 3 * cols + 128], out_rows], axis=1)
     first, to_send = lax.optimization_barrier((first, tokens))
     x_far = xor_swap(to_send, "in", n_in, 2)
-    first = lax.all_gather(first, G_AXES, axis=0, tiled=False)
+    first, position = lax.optimization_barrier((lax.all_gather(first, G_AXES, axis=0, tiled=False), position))
     second = jnp.concatenate([joined_cols[:, 3 * cols + 128 :], w_fc2], axis=1)
     second = lax.all_gather(second, G_AXES, axis=0, tiled=False)
 
@@ -826,8 +851,19 @@
     bias_qkv = lax.dynamic_index_in_dim(spans[4].reshape(3, n_in, cols), t, 1, keepdims=False).reshape(-1)
     norms = jnp.concatenate([jnp.stack([gain_one, shift_one, gain_two, shift_two]), jnp.zeros((4, width), F32)])
 
+    lane = jnp.arange(2 * HEAD, dtype=jnp.int32) % HEAD
+    half = ROT // 2
+    freq = 10000.0 ** (-2.0 * (lane % half).astype(F32) / ROT)
+    phase = position[:, None] * freq[None, :]
+    cos = jnp.where(lane < ROT, jnp.cos(phase), 1.0)
+    sine = jnp.sin(phase)
+    sin_l = jnp.where(lane < half, sine, 0.0)
+    sin_r = jnp.where((lane >= half) & (lane < ROT), sine, 0.0)
+
     x_near = xor_swap(jnp.stack([tokens, x_far]), "in", n_in, 1)
-    x_near, weight_qkv, norms, bias_qkv = lax.optimization_barrier((x_near, weight_qkv, norms, bias_qkv))
+    x_near, weight_qkv, norms, bias_qkv, cos, sin_l, sin_r = lax.optimization_barrier(
+        (x_near, weight_qkv, norms, bias_qkv, cos, sin_l, sin_r)
+    )
     x_all = join_in(tokens, x_far, x_near)
     x_all, to_send = lax.optimization_barrier((x_all, cotangent))
     dy_far = xor_swap(to_send, "in", n_in, 2)
@@ -846,8 +882,7 @@
         layout, x_all, n2, dy_all, norms, second, bias_in[None]
     )
     o, y_ff = lax.optimization_barrier((o, y_ff))
-    o, y_part = project(z_arr, o, y_ff, weight_out, block)
-    y_part = y_part.reshape(n_in, rows_dev, width)
+    o, *y_parts = project(z_arr, o, y_ff, weight_out, block)
     if layout.aligned:
         second_grads = feed_grads(layout, n2, grad_up, hidden, dy_all, o)
     else:
@@ -860,26 +895,28 @@
             axis=1,
         )
 
-    do, second_grads, y_part = lax.optimization_barrier((do, second_grads, y_part))
+    do, second_grads, y_parts = lax.optimization_barrier((do, second_grads, y_parts))
     second_grads = lax.psum_scatter(second_grads, G_AXES, scatter_dimension=0, tiled=False)
-    y_near = near_in(y_part)
+    y_keep, y_near = y_parts[:2], [near_in(p) for p in y_parts[2:]]
     own = tokens.astype(F32)
     parts = attend_backward(source, packed_of, ends, qkv, do, o_t, lse, block)
     parts, y_near = lax.optimization_barrier((parts, y_near))
     parts = exchange_out(parts)
-    y_far = xor_swap((y_part[2].astype(F32) + y_near[1].astype(F32)).astype(BF16), "in", n_in, 2)
+    y_far = [far_in(k, n) for k, n in zip(y_keep, y_near)]
     parts, y_far = lax.optimization_barrier((parts, y_far))
-    y_sum = y_part[0].astype(F32) + y_near[0].astype(F32) + y_far.astype(F32)
-    mixed = (own + y_sum + bias_out).astype(BF16)
-    da, w_parts, sums_one, grad_b_qkv = post(
+    da, sums_one, grad_b_qkv, *w_parts = post(
         z_arr, parts, x_all, dx_ff, norms, weight_qkv, cos, sin_l, sin_r, block
     )
-    w_parts, da, mixed, second_grads = lax.optimization_barrier((w_parts, da, mixed, second_grads))
-    in_part = exchange_in(second_grads[: n_in * r_w].reshape(n_in, r_w, ff_in), t)
-    w_parts = halves(w_parts.reshape(n_in, rows_dev, width))
-    near = near_in(w_parts[0])
-    near, w_next = lax.optimization_barrier((near, w_parts[1]))
-    w_sum = jnp.concatenate([far_in(w_parts[0], near), far_in(w_next, near_in(w_next))], axis=1)
+    w_parts, da, second_grads = lax.optimization_barrier((w_parts, da, second_grads))
+    w_keep, w_near = w_parts[:2], [near_in(w_parts[2])]
+    w_near[0], w_next, tokens, y_far = lax.optimization_barrier((w_near[0], w_parts[3], tokens, y_far))
+    own = tokens.astype(F32)
+    mixed = (own + total(y_keep, y_near, y_far) + bias_out).astype(BF16)
+    w_near.append(near_in(w_next))
+    w_far = [far_in(w_keep[0], w_near[0])]
+    w_near[1], second_grads = lax.optimization_barrier((w_near[1], second_grads))
+    w_far.append(far_in(w_keep[1], w_near[1]))
+    w_sum = total(w_keep, w_near, w_far)
 
     def placed(vector, axis):
         spread = jnp.expand_dims(vector, axis)
@@ -907,13 +944,15 @@
         first_grads = jnp.concatenate([by_owner(dot_tn(n1, da).astype(BF16)), vec_grads], axis=2)
     first_grads = lax.psum_scatter(first_grads, G_AXES, scatter_dimension=0, tiled=False)
 
+    last = [first_grads.reshape(n_in, r_w, -1), second_grads[: n_in * r_w].reshape(n_in, r_w, ff_in)]
+    last = exchange_in(jnp.concatenate(last, axis=2), t)
+    qkv_part, in_part = last[:, :, : 3 * cols + 128], last[:, :, 3 * cols + 128 :]
     in_part = in_part.reshape(n_in, r_w, n_dp, n_out, r_ff)
     grad_w_in = jnp.transpose(in_part, (1, 2, 0, 3, 4)).reshape(r_w, ff).astype(F32)
     grad_w_fc2 = second_grads[n_in * r_w : n_in * r_w + r_ff].astype(F32)
     back_home = [(b, a) for a, b in home]
     out_part = second_grads[n_in * r_w + r_ff :]
     grad_w_out = lax.ppermute(out_part, ALL_AXES, back_home).astype(F32)
-    qkv_part = exchange_in(first_grads.reshape(n_in, r_w, 3 * cols + 128), t)
     qkv_grad = jnp.transpose(qkv_part[:, :, : 3 * cols].reshape(n_in, r_w, 3, cols), (1, 2, 0, 3))
     grad_w_qkv = qkv_grad.reshape(r_w, 3 * width).astype(F32)
     vec_part = jnp.sum(qkv_part[:, :, 3 * cols :].astype(F32), axis=0).reshape(r_w * per_row, lanes)

time: 341 us -> 332 us (0.974)
  waiting for transfers between devices: 106 us -> 126 us
  Pallas kernels: 119 us -> 106 us
  local copies, waits for them, and re-layouts: 33.7 us -> 21.9 us
  other arithmetic: 30.5 us -> 23.4 us
    ppermute x31 -> x30, waiting for transfers between devices: 106 us -> 123 us  [xor_swap(): return lax.ppermute(value, axis, [(i, i ^ step) for i in range(size)])]
    pallas_call x1, Pallas kernels: 34.9 us -> 26.7 us  [attend_backward(): pl.pallas_call(functools.partial(backward_kernel, block, ends.shape[0]),...]
    pallas_call x1, Pallas kernels: 25.4 us -> 19.3 us  [attend_forward(): pl.pallas_call(functools.partial(forward_kernel, block, ends.shape[0]), i...]
    ppermute x31 -> x30, starting transfers between devices: 33.2 us -> 35.8 us  [xor_swap(): return lax.ppermute(value, axis, [(i, i ^ step) for i in range(size)])]
  transfers between devices with their start and end apart: 37 -> 36, of which waited for: 14 -> 15; matrix products, arithmetic and copies ran while one was open for 15% -> 10% of each run, Pallas kernels for 35% -> 32%
where the time goes in v4:
time: 332 us; the launch traced here: 329 us
  waiting for transfers between devices  126 us (38%)
  Pallas kernels  106 us (32%)
  starting transfers between devices  37.2 us (11%)
  other arithmetic  23.4 us (7%)
  local copies, waits for them, and re-layouts  21.9 us (7%)
  between operations  14.6 us (4%)
    ppermute x30, waiting for transfers between devices, xor_swap(): return lax.ppermute(value, axis, [(i, i ^ step) for i in range(size)])  123 us
    ppermute x30, starting transfers between devices, xor_swap(): return lax.ppermute(value, axis, [(i, i ^ step) for i in range(size)])  35.8 us
    pallas_call x1, Pallas kernels, attend_backward(): pl.pallas_call(functools.partial(backward_kernel, block, ends.shape[0]),...  26.7 us
    pallas_call x1, Pallas kernels, attend_forward(): pl.pallas_call(functools.partial(forward_kernel, block, ends.shape[0]), i...  19.3 us
    pallas_call x1, Pallas kernels, feed(): pl.pallas_call(functools.partial(feed_kernel, layout), grid=(rows // TILE...  15.1 us
    pallas_call x1, Pallas kernels, feed_grads(): pl.pallas_call(functools.partial(feed_grads_kernel, layout), grid=(width...  10.8 us
    pallas_call x1, Pallas kernels, post(): pl.pallas_call(functools.partial(post_kernel, heads, block), grid_spec=pl...  10.3 us
    pallas_call x1, Pallas kernels, prep(): pl.pallas_call(functools.partial(prep_kernel, heads, block), grid_spec=pl...  7.94 us
  transfers between devices with their start and end apart: 36, of which 15 were waited for; matrix products, arithmetic and copies ran while one was open for 10% of the time, Pallas kernels for 32%

profile of v4, /device:TPU:0, one launch (start us, length us, event | category | flops | bytes accessed | tf_op | source)
XLA Modules:
  0.0 329.5 jit_solution(7215208707042160420)
XLA Ops:
  10.4 5.1 %collective-permute-start.2 = (bf16[32,1920]{1,0:T(8,128)(2,1)S(1)}, bf16[32,1920]{1,0:T(8,128)(2,1)S(1)}, u32[]{:S(2)}, u32[]{:S(2)}) collective-permute-start(bf16[32,1920]{1,0:T(8,128)(2,1)S(1)} %get-tuple-element.244), channel_id=1, source_target_pairs={{0,12},{4,8},{8,4},{12,0},{1,13},{5,9},{9,5},{13,1},{2,14},{6,10},... | collective-permute-start | bytes 368648 | tf_op jit(solution)/shard_map/ppermute | solution.py:40
  19.8 8.2 %collective-permute-done.1 = bf16[32,1920]{1,0:T(8,128)(2,1)S(1)} collective-permute-done((bf16[32,1920]{1,0:T(8,128)(2,1)S(1)}, bf16[32,1920]{1,0:T(8,128)(2,1)S(1)}, u32[]{:S(2)}, u32[]{:S(2)}) %collective-permute-start.1) | collective-permute-done | bytes 122912 | tf_op jit(solution)/shard_map/ppermute | solution.py:40
  32.1 22.0 %collective-permute-done.4 = bf16[256,1024]{1,0:T(8,128)(2,1)S(1)} collective-permute-done((bf16[256,1024]{1,0:T(8,128)(2,1)S(1)}, bf16[256,1024]{1,0:T(8,128)(2,1)S(1)}, u32[]{:S(2)}, u32[]{:S(2)}) %collective-permute-start.4) | collective-permute-done | bytes 524320 | tf_op jit(solution)/shard_map/ppermute | solution.py:40
  55.1 3.2 all-gather.5.cloned.1.call-done
  66.6 12.6 %collective-permute-done.5 = bf16[2,256,1024]{2,1,0:T(8,128)(2,1)} collective-permute-done((bf16[2,256,1024]{2,1,0:T(8,128)(2,1)}, bf16[2,256,1024]{2,1,0:T(8,128)(2,1)}, u32[]{:S(2)}, u32[]{:S(2)}) %collective-permute-start.5) | collective-permute-done | bytes 1048608 | tf_op jit(solution)/shard_map/ppermute | solution.py:40
  84.5 7.9 %shard_map.246 = (bf16[1024,1024]{1,0:T(8,128)(2,1)}, bf16[1024,1024]{1,0:T(8,128)(2,1)}, bf16[1536,128]{1,0:T(8,128)(2,1)}, bf16[1536,128]{1,0:T(8,128)(2,1)}, ...) custom-call(s32[1]{0:T(128)} %bitcast.z_ref, bf16[1024,1024]{1,0:T(8,128)(2,1)} %pad_maximum_fusion.x_ref, ...), custom_call_target="tpu_custom_call" | custom-call | flops 1610612736 | bytes 12582912 | tf_op jit(solution)/shard_map/pallas_call | solution.py:126
  97.8 7.0 %collective-permute-done.7.refs_2_ = bf16[1536,128]{1,0:T(8,128)(2,1)S(1)} collective-permute-done((bf16[1536,128]{1,0:T(8,128)(2,1)}, bf16[1536,128]{1,0:T(8,128)(2,1)S(1)}, u32[]{:S(2)}, u32[]{:S(2)}) %collective-permute-start.7) | collective-permute-done | bytes 393248 | tf_op jit(solution)/shard_map/ppermute | solution.py:40
  104.8 7.6 %collective-permute-done.8.refs_3_ = bf16[1536,128]{1,0:T(8,128)(2,1)} collective-permute-done((bf16[1536,128]{1,0:T(8,128)(2,1)}, bf16[1536,128]{1,0:T(8,128)(2,1)}, u32[]{:S(2)}, u32[]{:S(2)}) %collective-permute-start.8) | collective-permute-done | bytes 393248 | tf_op jit(solution)/shard_map/ppermute | solution.py:40
  115.2 19.3 %shard_map.247 = (bf16[512,128]{1,0:T(8,128)(2,1)}, bf16[512,128]{1,0:T(8,128)(2,1)}, bf16[512,128]{1,0:T(8,128)(2,1)}, bf16[512,128]{1,0:T(8,128)(2,1)}, f32[64,4096]{1,0:T(8,128)}, /*index=5*/f32[1,4096]{1,0:T(1,128)}) custom-call(s32[64]{0:T(128)} %fusion.24.source_ref, s32[64]{0:T(128)} %copy-done.25, s32[4]{0:T(128)} %bitcast.130, ...), custom_call_target="tpu_custom_call" | custom-call | flops 42949672960 | bytes 3145728 | tf_op jit(solution)/shard_map/pallas_call | solution.py:674
  134.5 4.5 %collective-permute-done.10 = bf16[2,256,1024]{2,1,0:T(8,128)(2,1)S(1)} collective-permute-done((bf16[2,256,1024]{2,1,0:T(8,128)(2,1)}, bf16[2,256,1024]{2,1,0:T(8,128)(2,1)S(1)}, u32[]{:S(2)}, u32[]{:S(2)}) %collective-permute-start.10) | collective-permute-done | bytes 1048608 | tf_op jit(solution)/shard_map/ppermute | solution.py:40
  142.5 4.4 %shard_map.249 = (bf16[512,128]{1,0:T(8,128)(2,1)}, bf16[512,128]{1,0:T(8,128)(2,1)}, bf16[512,128]{1,0:T(8,128)(2,1)}, bf16[512,128]{1,0:T(8,128)(2,1)}) custom-call(s32[1]{0:T(128)} %bitcast.z_ref, bf16[1024,1024]{1,0:T(8,128)(2,1)} %pad_maximum_fusion.1.dy_ref, bf16[256,1024]{1,0:T(8,128)(2,1)} %reshape.287.wo_ref), custom_call_target="tpu_custom_call" | custom-call | flops 536870912 | bytes 4194304 | tf_op jit(solution)/shard_map/pallas_call | solution.py:318
  148.7 15.1 %shard_map.248 = (bf16[1024,1024]{1,0:T(8,128)(2,1)}, bf16[1024,1024]{1,0:T(8,128)(2,1)}, f32[1024,1024]{1,0:T(8,128)}, f32[1024,1024]{1,0:T(8,128)}, f32[8,1024]{1,0:T(8,128)}, /*index=5*/f32[8,1024]{1,0:T(8,128)}) custom-call(bf16[1024,1024]{1,0:T(8,128)(2,1)} %pad_maximum_fusion.x_ref, bf16[1024,1024]{1,0:T(8,128)(2,1)} %get-tuple-element.125.n2_ref, ...), custom_call_target="tpu_custom_call" | custom-call | flops 8589934592 | bytes 25165824 | tf_op jit(solution)/shard_map/pallas_call | solution.py:205
  164.6 5.8 %shard_map.250 = (bf16[1024,256]{1,0:T(8,128)(2,1)}, bf16[512,512]{1,0:T(8,128)(2,1)}, bf16[512,512]{1,0:T(8,128)(2,1)}, bf16[512,512]{1,0:T(8,128)(2,1)}, bf16[512,512]{1,0:T(8,128)(2,1)}) custom-call(s32[1]{0:T(128)} %bitcast.z_ref, f32[1024,1024]{1,0:T(8,128)} %get-tuple-element.153.y_ref, bf16[256,1024]{1,0:T(8,128)(2,1)} %reshape.287.wo_ref, ...), custom_call_target="tpu_custom_call" | custom-call | flops 536870912 | bytes 8388608 | tf_op jit(solution)/shard_map/pallas_call | solution.py:367
  170.5 10.8 %shard_map.251 = bf16[8,288,1024]{2,1,0:T(8,128)(2,1)} custom-call(bf16[1024,1024]{1,0:T(8,128)(2,1)} %get-tuple-element.125.n2_ref, bf16[1024,1024]{1,0:T(8,128)(2,1)} %get-tuple-element.146.du_ref, bf16[1024,1024]{1,0:T(8,128)(2,1)} %get-tuple-element.147.h_ref, bf16[1024,1024]{1,0:T(8,128)(2,1)} %pad_maximum_fusion.1.dy_ref, ...), custom_call_target="tpu_custom_call" | custom-call | flops 4294967296 | bytes 14680064 | tf_op jit(solution)/shard_map/pallas_call | solution.py:262
  184.2 26.7 %shard_map.252 = (bf16[1536,128]{1,0:T(8,128)(2,1)}, bf16[1536,128]{1,0:T(8,128)(2,1)}, bf16[1536,128]{1,0:T(8,128)(2,1)}, bf16[1536,128]{1,0:T(8,128)(2,1)}) custom-call(s32[64]{0:T(128)} %fusion.24.source_ref, s32[64]{0:T(128)} %copy-done.25, s32[4]{0:T(128)} %bitcast.131, bf16[1536,128]{1,0:T(8,128)(2,1)} %get-tuple-element.131.refs_0_, ...), custom_call_target="tpu_custom_call" | custom-call | flops 42949672960 | bytes 6291456 | tf_op jit(solution)/shard_map/pallas_call | solution.py:702
  218.6 14.8 %collective-permute-done.23 = bf16[256,512]{1,0:T(8,128)(2,1)} collective-permute-done((bf16[256,512]{1,0:T(8,128)(2,1)}, bf16[256,512]{1,0:T(8,128)(2,1)}, u32[]{:S(2)}, u32[]{:S(2)}) %collective-permute-start.23) | collective-permute-done | bytes 262176 | tf_op jit(solution)/shard_map/ppermute | solution.py:40
  233.4 5.0 %collective-permute-done.22 = bf16[256,512]{1,0:T(8,128)(2,1)} collective-permute-done((bf16[256,512]{1,0:T(8,128)(2,1)}, bf16[256,512]{1,0:T(8,128)(2,1)}, u32[]{:S(2)}, u32[]{:S(2)}) %collective-permute-start.22) | collective-permute-done | bytes 262176 | tf_op jit(solution)/shard_map/ppermute | solution.py:40
  241.0 10.3 %shard_map.253 = (bf16[1024,768]{1,0:T(8,128)(2,1)}, f32[8,1024]{1,0:T(8,128)}, f32[8,768]{1,0:T(8,128)}, bf16[512,512]{1,0:T(8,128)(2,1)}, bf16[512,512]{1,0:T(...) custom-call(s32[1]{0:T(128)} %bitcast.z_ref, bf16[1024,1024]{1,0:T(8,128)(2,1)} %pad_maximum_fusion.x_ref, ...), custom_call_target="tpu_custom_call" | custom-call | flops 1610612736 | bytes 14680064 | tf_op jit(solution)/shard_map/pallas_call | solution.py:420
  255.8 5.9 %shard_map.254 = bf16[8,128,896]{2,1,0:T(8,128)(2,1)} custom-call(bf16[1024,1024]{1,0:T(8,128)(2,1)} %get-tuple-element.206.n1_ref, bf16[1024,768]{1,0:T(8,128)(2,1)} %get-tuple-element.207.da_ref, bf16[8,128,128]{2,1,0:T(8,128)(2,1)} %bitcast.119), custom_call_target="tpu_custom_call" | custom-call | flops 1610612736 | bytes 6291456 | tf_op jit(solution)/shard_map/pallas_call | solution.py:294
  261.8 6.3 %collective-permute-done.24 = bf16[512,512]{1,0:T(8,128)(2,1)} collective-permute-done((bf16[512,512]{1,0:T(8,128)(2,1)}, bf16[512,512]{1,0:T(8,128)(2,1)}, u32[]{:S(2)}, u32[]{:S(2)}) %collective-permute-start.24) | collective-permute-done | bytes 524320 | tf_op jit(solution)/shard_map/ppermute | solution.py:40
  275.7 11.8 %collective-permute-done.26 = bf16[512,512]{1,0:T(8,128)(2,1)S(1)} collective-permute-done((bf16[512,512]{1,0:T(8,128)(2,1)}, bf16[512,512]{1,0:T(8,128)(2,1)S(1)}, u32[]{:S(2)}, u32[]{:S(2)}) %collective-permute-start.26) | collective-permute-done | bytes 524320 | tf_op jit(solution)/shard_map/ppermute | solution.py:40
  292.6 9.6 %collective-permute-done.27 = bf16[256,512]{1,0:T(8,128)(2,1)S(1)} collective-permute-done((bf16[256,512]{1,0:T(8,128)(2,1)S(1)}, bf16[256,512]{1,0:T(8,128)(2,1)S(1)}, u32[]{:S(2)}, u32[]{:S(2)}) %collective-permute-start.27) | collective-permute-done | bytes 262176 | tf_op jit(solution)/shard_map/ppermute | solution.py:40
  304.6 4.3 %collective-permute-start.29 = (bf16[32,1920]{1,0:T(8,128)(2,1)S(1)}, bf16[32,1920]{1,0:T(8,128)(2,1)S(1)}, u32[]{:S(2)}, u32[]{:S(2)}) collective-permute-start(bf16[32,1920]{1,0:T(8,128)(2,1)S(1)} %get-tuple-element.237), channel_id=1, source_target_pairs={{0,8},{4,12},{8,0},{12,4},{1,9},{5,13},{9,1},{13,5},{2,10},{6,14},... | collective-permute-start | bytes 368648 | tf_op jit(solution)/shard_map/ppermute | solution.py:40
  310.4 7.9 %collective-permute-done.29 = bf16[32,1920]{1,0:T(8,128)(2,1)S(1)} collective-permute-done((bf16[32,1920]{1,0:T(8,128)(2,1)S(1)}, bf16[32,1920]{1,0:T(8,128)(2,1)S(1)}, u32[]{:S(2)}, u32[]{:S(2)}) %collective-permute-start.29) | collective-permute-done | bytes 122912 | tf_op jit(solution)/shard_map/ppermute | solution.py:40
  (260 shorter events, 78.7 us)
Async XLA Ops:
  7.3 51.1 %all-gather.5.cloned.1.call-start = ((), (), s32[]{:S(2)}) async-start(), calls=%async_computation.4 | async-start | bytes 2654208 | tf_op jit(solution)/shard_map/all_gather | solution.py:828
  29.1 119.6 %all-gather.7.cloned.1.call-start = ((), (), s32[]{:S(2)}) async-start(), calls=%async_computation.5 | async-start | bytes 4718592 | tf_op jit(solution)/shard_map/all_gather | solution.py:830
  29.6 24.5 %collective-permute-start.4 = (bf16[256,1024]{1,0:T(8,128)(2,1)S(1)}, bf16[256,1024]{1,0:T(8,128)(2,1)S(1)}, u32[]{:S(2)}, u32[]{:S(2)}) collective-permute-start(bf16[256,1024]{1,0:T(8,128)(2,1)S(1)} %copy-done), channel_id=1, source_target_pairs={{0,8},{4,12},{8,0},{12,4},{1,9},{5,13},{9,1},{13,5},{2,10},{6,14},... | collective-permute-start | bytes 1572872 | tf_op jit(solution)/shard_map/ppermute | solution.py:40
  31.8 221.5 %reduce-scatter.3.cloned.1.call-start = ((), (), s32[]{:S(2)}) async-start(), calls=%async_computation.2 | async-start | bytes 5308416 | tf_op jit(solution)/shard_map/reduce_scatter | solution.py:899
  55.1 24.1 %collective-permute-start.5 = (bf16[2,256,1024]{2,1,0:T(8,128)(2,1)}, bf16[2,256,1024]{2,1,0:T(8,128)(2,1)}, u32[]{:S(2)}, u32[]{:S(2)}) collective-permute-start(bf16[2,256,1024]{2,1,0:T(8,128)(2,1)} %pad_maximum_fusion.2), channel_id=1, source_target_pairs={{0,4},{4,0},{8,12},{12,8},{1,5},{5,1},{9,13},{13,9},{2,6},{6,2},{1... | collective-permute-start | bytes 3145736 | tf_op jit(solution)/shard_map/ppermute | solution.py:40
  82.6 29.8 %collective-permute-start.9 = (bf16[256,1024]{1,0:T(8,128)(2,1)S(1)}, bf16[256,1024]{1,0:T(8,128)(2,1)S(1)}, u32[]{:S(2)}, u32[]{:S(2)}) collective-permute-start(bf16[256,1024]{1,0:T(8,128)(2,1)S(1)} %copy-done.1), channel_id=1, source_target_pairs={{0,8},{4,12},{8,0},{12,4},{1,9},{5,13},{9,1},{13,5},{2,10},{6,14},... | collective-permute-start | bytes 1572872 | tf_op jit(solution)/shard_map/ppermute | solution.py:40
  94.1 18.2 %collective-permute-start.8 = (bf16[1536,128]{1,0:T(8,128)(2,1)}, bf16[1536,128]{1,0:T(8,128)(2,1)}, u32[]{:S(2)}, u32[]{:S(2)}) collective-permute-start(bf16[1536,128]{1,0:T(8,128)(2,1)} %get-tuple-element.129), channel_id=1, source_target_pairs={{0,3},{1,2},{2,1},{3,0},{4,7},{5,6},{6,5},{7,4},{8,11},{9,10},{10,... | collective-permute-start | bytes 1179656 | tf_op jit(solution)/shard_map/ppermute | solution.py:40
  113.5 25.6 %collective-permute-start.10 = (bf16[2,256,1024]{2,1,0:T(8,128)(2,1)}, bf16[2,256,1024]{2,1,0:T(8,128)(2,1)S(1)}, u32[]{:S(2)}, u32[]{:S(2)}) collective-permute-start(bf16[2,256,1024]{2,1,0:T(8,128)(2,1)} %pad_maximum_fusion.3), channel_id=1, source_target_pairs={{0,4},{4,0},{8,12},{12,8},{1,5},{5,1},{9,13},{13,9},{2,6},{6,2},{1... | collective-permute-start | bytes 3145736 | tf_op jit(solution)/shard_map/ppermute | solution.py:40
  139.0 24.8 %collective-permute-start.14 = (bf16[512,128]{1,0:T(8,128)(2,1)}, bf16[512,128]{1,0:T(8,128)(2,1)S(1)}, u32[]{:S(2)}, u32[]{:S(2)}) collective-permute-start(bf16[512,128]{1,0:T(8,128)(2,1)} %get-tuple-element.149), channel_id=1, source_target_pairs={{0,1},{1,0},{2,3},{3,2},{4,5},{5,4},{6,7},{7,6},{8,9},{9,8},{10,11... | collective-permute-start | bytes 393224 | tf_op jit(solution)/shard_map/ppermute | solution.py:40
  139.0 24.9 %collective-permute-start.15 = (bf16[512,128]{1,0:T(8,128)(2,1)}, bf16[512,128]{1,0:T(8,128)(2,1)S(1)}, u32[]{:S(2)}, u32[]{:S(2)}) collective-permute-start(bf16[512,128]{1,0:T(8,128)(2,1)} %get-tuple-element.150), channel_id=1, source_target_pairs={{0,2},{1,3},{2,0},{3,1},{4,6},{5,7},{6,4},{7,5},{8,10},{9,11},{10,... | collective-permute-start | bytes 393224 | tf_op jit(solution)/shard_map/ppermute | solution.py:40
  140.5 23.4 %collective-permute-start.16 = (bf16[512,128]{1,0:T(8,128)(2,1)}, bf16[512,128]{1,0:T(8,128)(2,1)S(1)}, u32[]{:S(2)}, u32[]{:S(2)}) collective-permute-start(bf16[512,128]{1,0:T(8,128)(2,1)} %get-tuple-element.151), channel_id=1, source_target_pairs={{0,3},{1,2},{2,1},{3,0},{4,7},{5,6},{6,5},{7,4},{8,11},{9,10},{10,... | collective-permute-start | bytes 393224 | tf_op jit(solution)/shard_map/ppermute | solution.py:40
  146.9 34.4 %collective-permute-start.11 = (bf16[512,128]{1,0:T(8,128)(2,1)}, bf16[512,128]{1,0:T(8,128)(2,1)S(1)}, u32[]{:S(2)}, u32[]{:S(2)}) collective-permute-start(bf16[512,128]{1,0:T(8,128)(2,1)} %get-tuple-element.143), channel_id=1, source_target_pairs={{0,1},{1,0},{2,3},{3,2},{4,5},{5,4},{6,7},{7,6},{8,9},{9,8},{10,11... | collective-permute-start | bytes 393224 | tf_op jit(solution)/shard_map/ppermute | solution.py:40
  147.2 34.1 %collective-permute-start.12 = (bf16[512,128]{1,0:T(8,128)(2,1)}, bf16[512,128]{1,0:T(8,128)(2,1)S(1)}, u32[]{:S(2)}, u32[]{:S(2)}) collective-permute-start(bf16[512,128]{1,0:T(8,128)(2,1)} %get-tuple-element.144), channel_id=1, source_target_pairs={{0,2},{1,3},{2,0},{3,1},{4,6},{5,7},{6,4},{7,5},{8,10},{9,11},{10,... | collective-permute-start | bytes 393224 | tf_op jit(solution)/shard_map/ppermute | solution.py:40
  163.8 17.5 %collective-permute-start.13 = (bf16[512,128]{1,0:T(8,128)(2,1)S(1)}, bf16[512,128]{1,0:T(8,128)(2,1)S(1)}, u32[]{:S(2)}, u32[]{:S(2)}) collective-permute-start(bf16[512,128]{1,0:T(8,128)(2,1)S(1)} %copy-done.33), channel_id=1, source_target_pairs={{0,3},{1,2},{2,1},{3,0},{4,7},{5,6},{6,5},{7,4},{8,11},{9,10},{10,... | collective-permute-start | bytes 393224 | tf_op jit(solution)/shard_map/ppermute | solution.py:40
  182.0 120.7 %reduce-scatter.5.cloned.1.call-start = ((), (), s32[]{:S(2)}) async-start(), calls=%async_computation.3 | async-start | bytes 2064384 | tf_op jit(solution)/shard_map/reduce_scatter | solution.py:945
  182.0 28.9 %collective-permute-start.17 = (bf16[512,512]{1,0:T(8,128)(2,1)}, bf16[512,512]{1,0:T(8,128)(2,1)S(1)}, u32[]{:S(2)}, u32[]{:S(2)}) collective-permute-start(bf16[512,512]{1,0:T(8,128)(2,1)} %get-tuple-element.173), channel_id=1, source_target_pairs={{0,4},{4,0},{8,12},{12,8},{1,5},{5,1},{9,13},{13,9},{2,6},{6,2},{1... | collective-permute-start | bytes 1572872 | tf_op jit(solution)/shard_map/ppermute | solution.py:40
  183.7 27.2 %collective-permute-start.18 = (bf16[512,512]{1,0:T(8,128)(2,1)S(1)}, bf16[512,512]{1,0:T(8,128)(2,1)S(1)}, u32[]{:S(2)}, u32[]{:S(2)}) collective-permute-start(bf16[512,512]{1,0:T(8,128)(2,1)S(1)} %copy-done.27), channel_id=1, source_target_pairs={{0,4},{4,0},{8,12},{12,8},{1,5},{5,1},{9,13},{13,9},{2,6},{6,2},{1... | collective-permute-start | bytes 1572872 | tf_op jit(solution)/shard_map/ppermute | solution.py:40
  211.8 21.6 %collective-permute-start.23 = (bf16[256,512]{1,0:T(8,128)(2,1)}, bf16[256,512]{1,0:T(8,128)(2,1)}, u32[]{:S(2)}, u32[]{:S(2)}) collective-permute-start(bf16[256,512]{1,0:T(8,128)(2,1)} %add_convert_fusion.2), channel_id=1, source_target_pairs={{0,8},{4,12},{8,0},{12,4},{1,9},{5,13},{9,1},{13,5},{2,10},{6,14},... | collective-permute-start | bytes 786440 | tf_op jit(solution)/shard_map/ppermute | solution.py:40
  213.5 24.8 %collective-permute-start.19 = (bf16[1536,128]{1,0:T(8,128)(2,1)}, bf16[1536,128]{1,0:T(8,128)(2,1)S(1)}, u32[]{:S(2)}, u32[]{:S(2)}) collective-permute-start(bf16[1536,128]{1,0:T(8,128)(2,1)} %get-tuple-element.176), channel_id=1, source_target_pairs={{0,1},{1,0},{2,3},{3,2},{4,5},{5,4},{6,7},{7,6},{8,9},{9,8},{10,11... | collective-permute-start | bytes 1179656 | tf_op jit(solution)/shard_map/ppermute | solution.py:40
  213.5 24.8 %collective-permute-start.20 = (bf16[1536,128]{1,0:T(8,128)(2,1)}, bf16[1536,128]{1,0:T(8,128)(2,1)S(1)}, u32[]{:S(2)}, u32[]{:S(2)}) collective-permute-start(bf16[1536,128]{1,0:T(8,128)(2,1)} %get-tuple-element.177), channel_id=1, source_target_pairs={{0,2},{1,3},{2,0},{3,1},{4,6},{5,7},{6,4},{7,5},{8,10},{9,11},{10,... | collective-permute-start | bytes 1179656 | tf_op jit(solution)/shard_map/ppermute | solution.py:40
  214.1 26.9 %collective-permute-start.21 = (bf16[1536,128]{1,0:T(8,128)(2,1)}, bf16[1536,128]{1,0:T(8,128)(2,1)}, u32[]{:S(2)}, u32[]{:S(2)}) collective-permute-start(bf16[1536,128]{1,0:T(8,128)(2,1)} %get-tuple-element.178), channel_id=1, source_target_pairs={{0,3},{1,2},{2,1},{3,0},{4,7},{5,6},{6,5},{7,4},{8,11},{9,10},{10,... | collective-permute-start | bytes 1179656 | tf_op jit(solution)/shard_map/ppermute | solution.py:40
  216.2 22.2 %collective-permute-start.22 = (bf16[256,512]{1,0:T(8,128)(2,1)}, bf16[256,512]{1,0:T(8,128)(2,1)}, u32[]{:S(2)}, u32[]{:S(2)}) collective-permute-start(bf16[256,512]{1,0:T(8,128)(2,1)} %add_convert_fusion.3), channel_id=1, source_target_pairs={{0,8},{4,12},{8,0},{12,4},{1,9},{5,13},{9,1},{13,5},{2,10},{6,14},... | collective-permute-start | bytes 786440 | tf_op jit(solution)/shard_map/ppermute | solution.py:40
  268.1 19.5 %collective-permute-start.26 = (bf16[512,512]{1,0:T(8,128)(2,1)}, bf16[512,512]{1,0:T(8,128)(2,1)S(1)}, u32[]{:S(2)}, u32[]{:S(2)}) collective-permute-start(bf16[512,512]{1,0:T(8,128)(2,1)} %get-tuple-element.203), channel_id=1, source_target_pairs={{0,4},{4,0},{8,12},{12,8},{1,5},{5,1},{9,13},{13,9},{2,6},{6,2},{1... | collective-permute-start | bytes 1572872 | tf_op jit(solution)/shard_map/ppermute | solution.py:40
  272.2 17.0 %collective-permute-start.25 = (bf16[256,512]{1,0:T(8,128)(2,1)S(1)}, bf16[256,512]{1,0:T(8,128)(2,1)S(1)}, u32[]{:S(2)}, u32[]{:S(2)}) collective-permute-start(bf16[256,512]{1,0:T(8,128)(2,1)S(1)} %add_convert_fusion.1), channel_id=1, source_target_pairs={{0,8},{4,12},{8,0},{12,4},{1,9},{5,13},{9,1},{13,5},{2,10},{6,14},... | collective-permute-start | bytes 786440 | tf_op jit(solution)/shard_map/ppermute | solution.py:40
  (48 other events, 412.4 us)
Sparse Core Ops, SparseCore 0:
  29.2 29.1 all-gather.4
  60.2 36.7 all-gather.6
  181.4 61.4 reduce-scatter.2
  261.9 38.7 reduce-scatter.4

commit v5 on v4

--- a/solution.py
+++ b/solution.py
@@ -328,27 +328,13 @@
     )(z, dy, wo)
 
 
-def split_parts(step, total, keep_refs, near_refs):
+def split_parts(step, total, refs):
     low = total.astype(BF16)
-    half = total.shape[1] // 2
-
-    @pl.when(step % 2 == 0)
-    def _():
-        for at, ref in enumerate(keep_refs):
-            ref[...] = low[:, at * half : (at + 1) * half]
-
-    @pl.when(step % 2 == 1)
-    def _():
-        for at, ref in enumerate(near_refs):
-            ref[...] = low[:, at * half : (at + 1) * half]
-
-
-def half_tile(width):
-    return pl.BlockSpec((TILE, width // 2), lambda i, z: (i // 2, 0))
-
-
-def half_parts(rows, width):
-    return jax.ShapeDtypeStruct((rows // 2, width // 2), BF16)
+    for at, ref in enumerate(refs):
+
+        @pl.when(step == at)
+        def _(ref=ref):
+            ref[...] = low
 
 
 def project_kernel(heads, block, z_ref, y_ref, wo_ref, *refs):
@@ -357,7 +343,7 @@
     for h in range(0, heads, 2):
         o_ref[:, h * HEAD : (h + 2) * HEAD] = jnp.concatenate(parts[h : h + 2], axis=1).astype(BF16)
     total = y_ref[...] + dot(o_ref[...], wo_ref[...])
-    split_parts(pl.program_id(0), total, refs[heads + 1 : heads + 3], refs[heads + 3 :])
+    split_parts(pl.program_id(0), total, refs[heads + 1 :])
 
 
 def project(z, parts, y, wo, block):
@@ -370,9 +356,9 @@
             num_scalar_prefetch=1,
             grid=(rows // TILE,),
             in_specs=[tile, pl.BlockSpec(wo.shape, whole_at)] + [piece(TILE // 2)] * heads,
-            out_specs=[pl.BlockSpec((TILE, heads * HEAD), row_at)] + [half_tile(width)] * 4,
+            out_specs=[pl.BlockSpec((TILE, heads * HEAD), row_at)] + [pl.BlockSpec((TILE, width), whole_at)] * GROUP_IN,
         ),
-        out_shape=[jax.ShapeDtypeStruct((rows, heads * HEAD), BF16)] + [half_parts(rows, width)] * 4,
+        out_shape=[jax.ShapeDtypeStruct((rows, heads * HEAD), BF16)] + [jax.ShapeDtypeStruct((TILE, width), BF16)] * GROUP_IN,
         **params(2 * rows * width * wo.shape[0], 8 * 2**20),
     )(z, y, wo, *parts)
 
@@ -396,7 +382,7 @@
     grad = da_ref[...]
     grad_norm = dot_nt(grad, w_ref[...])
     total = dx_ref[...] + grad_norm * norm_ref[0:1]
-    split_parts(pl.program_id(0), total, refs[heads + 3 : heads + 5], refs[heads + 5 :])
+    split_parts(pl.program_id(0), total, refs[heads + 3 :])
     gain = jnp.sum(grad_norm * normalized(x_ref), axis=0, keepdims=True)
     shift = jnp.sum(grad_norm, axis=0, keepdims=True)
     bias = jnp.sum(grad.astype(F32), axis=0, keepdims=True)
@@ -437,14 +423,14 @@
                 pl.BlockSpec((8, width), whole_at),
                 pl.BlockSpec((8, three), whole_at),
             ]
-            + [half_tile(width)] * 4,
+            + [pl.BlockSpec((TILE, width), whole_at)] * GROUP_IN,
         ),
         out_shape=[
             jax.ShapeDtypeStruct((rows, three), BF16),
             jax.ShapeDtypeStruct((8, width), F32),
             jax.ShapeDtypeStruct((8, three), F32),
         ]
-        + [half_parts(rows, width)] * 4,
+        + [jax.ShapeDtypeStruct((TILE, width), BF16)] * GROUP_IN,
         **params(2 * rows * width * three, 14 * 2**20),
     )(z, x, dx, norms, w, cos, sl, sr, *grads)
 
@@ -724,23 +710,8 @@
     )(source, packed, ends, *qkv, *do, o_t, lse)
 
 
-def join_in(value, far, near):
-    return jnp.concatenate([value, near[0], far, near[1]])
-
-
-def near_in(near):
-    return xor_swap(near, "in", GROUP_IN, 1)
-
-
-def far_in(keep, near):
-    size = keep.shape[0] // 2
-    return xor_swap((keep[size:].astype(F32) + near[size:].astype(F32)).astype(BF16), "in", GROUP_IN, 2)
-
-
-def total(keep, near, far):
-    size = far[0].shape[0]
-    parts = [k[:size].astype(F32) + n[:size].astype(F32) + f.astype(F32) for k, n, f in zip(keep, near, far)]
-    return jnp.concatenate(parts, axis=1)
+def total(*parts):
+    return sum((p.astype(F32) for p in parts[1:]), parts[0].astype(F32))
 
 
 def exchange_in(parts, t):
@@ -824,10 +795,10 @@
     out_rows = lax.ppermute(w_out, ALL_AXES, home).reshape(n_in * r_w, cols)
     first = jnp.concatenate([joined_cols[:, : 3 * cols + 128], out_rows], axis=1)
     first, to_send = lax.optimization_barrier((first, tokens))
-    x_far = xor_swap(to_send, "in", n_in, 2)
+    x_near = xor_swap(to_send, "in", n_in, 1)
+    x_far, x_near = lax.optimization_barrier((xor_swap(to_send, "in", n_in, 2), x_near))
     first, position = lax.optimization_barrier((lax.all_gather(first, G_AXES, axis=0, tiled=False), position))
     second = jnp.concatenate([joined_cols[:, 3 * cols + 128 :], w_fc2], axis=1)
-    second = lax.all_gather(second, G_AXES, axis=0, tiled=False)
 
     def natural(value):
         value = value.reshape(n_dp, n_out, n_in, r_w, -1)
@@ -839,9 +810,6 @@
 
     weight_qkv = natural(first[:, :, : 3 * cols])
     weight_out = first[:, :, 3 * cols + 128 :].reshape(cols, width)
-    if not layout.aligned:
-        in_rows = natural(second[:, :, :ff_in]).reshape(n_g, n_in * r_w, ff_in)
-        second = jnp.concatenate([in_rows, second[:, :, ff_in:]], axis=2)
     vec_all = first[:, :, 3 * cols : 3 * cols + 128].reshape(n_dp, n_out, n_in, r_w * per_row, lanes)
     vec_all = jnp.transpose(vec_all[:, :, :, : len(vectors)], (3, 0, 2, 1, 4)).astype(F32)
     spans = [vec_all[i, ..., :size] for i, size in enumerate(sizes)]
@@ -860,21 +828,25 @@
     sin_l = jnp.where(lane < half, sine, 0.0)
     sin_r = jnp.where((lane >= half) & (lane < ROT), sine, 0.0)
 
-    x_near = xor_swap(jnp.stack([tokens, x_far]), "in", n_in, 1)
-    x_near, weight_qkv, norms, bias_qkv, cos, sin_l, sin_r = lax.optimization_barrier(
-        (x_near, weight_qkv, norms, bias_qkv, cos, sin_l, sin_r)
+    x_both = xor_swap(x_far, "in", n_in, 1)
+    x_both, weight_qkv, norms, bias_qkv, cos, sin_l, sin_r = lax.optimization_barrier(
+        (x_both, weight_qkv, norms, bias_qkv, cos, sin_l, sin_r)
     )
-    x_all = join_in(tokens, x_far, x_near)
+    x_all = jnp.concatenate([tokens, x_near, x_far, x_both])
     x_all, to_send = lax.optimization_barrier((x_all, cotangent))
-    dy_far = xor_swap(to_send, "in", n_in, 2)
+    dy_near, dy_far = [xor_swap(to_send, "in", n_in, step) for step in (1, 2)]
 
     n1, n2, *qkv = prep(z_arr, x_all, norms, weight_qkv, bias_qkv[None], cos, sin_l, sin_r, block)
     qkv = exchange_out(qkv)
-    qkv, dy_far = lax.optimization_barrier((qkv, dy_far))
-    dy_near = xor_swap(jnp.stack([cotangent, dy_far]), "in", n_in, 1)
+    qkv, dy_far, dy_near, second = lax.optimization_barrier((qkv, dy_far, dy_near, second))
+    second = lax.all_gather(second, G_AXES, axis=0, tiled=False)
+    if not layout.aligned:
+        in_rows = natural(second[:, :, :ff_in]).reshape(n_g, n_in * r_w, ff_in)
+        second = jnp.concatenate([in_rows, second[:, :, ff_in:]], axis=2)
+    dy_both = xor_swap(dy_far, "in", n_in, 1)
     *o, o_t, lse = attend_forward(source, packed_of, ends, qkv, block)
-    o, dy_near = lax.optimization_barrier((o, dy_near))
-    dy_all = join_in(cotangent, dy_far, dy_near)
+    o, dy_both = lax.optimization_barrier((o, dy_both))
+    dy_all = jnp.concatenate([cotangent, dy_near, dy_far, dy_both])
     o = exchange_out(o)
     do = exchange_out(grad_att(z_arr, dy_all, weight_out, block))
 
@@ -897,26 +869,29 @@
 
     do, second_grads, y_parts = lax.optimization_barrier((do, second_grads, y_parts))
     second_grads = lax.psum_scatter(second_grads, G_AXES, scatter_dimension=0, tiled=False)
-    y_keep, y_near = y_parts[:2], [near_in(p) for p in y_parts[2:]]
+    y_hop = xor_swap(y_parts[3], "in", n_in, 1)
     own = tokens.astype(F32)
     parts = attend_backward(source, packed_of, ends, qkv, do, o_t, lse, block)
-    parts, y_near = lax.optimization_barrier((parts, y_near))
+    parts, y_hop, y_parts = lax.optimization_barrier((parts, y_hop, y_parts))
     parts = exchange_out(parts)
-    y_far = [far_in(k, n) for k, n in zip(y_keep, y_near)]
-    parts, y_far = lax.optimization_barrier((parts, y_far))
+    y_near = xor_swap(y_parts[1], "in", n_in, 1)
+    y_far = xor_swap(total(y_parts[2], y_hop).astype(BF16), "in", n_in, 2)
+    parts, y_far, y_near = lax.optimization_barrier((parts, y_far, y_near))
     da, sums_one, grad_b_qkv, *w_parts = post(
         z_arr, parts, x_all, dx_ff, norms, weight_qkv, cos, sin_l, sin_r, block
     )
     w_parts, da, second_grads = lax.optimization_barrier((w_parts, da, second_grads))
-    w_keep, w_near = w_parts[:2], [near_in(w_parts[2])]
-    w_near[0], w_next, tokens, y_far = lax.optimization_barrier((w_near[0], w_parts[3], tokens, y_far))
+    w_hop = xor_swap(w_parts[3], "in", n_in, 1)
+    w_hop, w_near, tokens, y_far, second_grads = lax.optimization_barrier(
+        (w_hop, w_parts[1], tokens, y_far, second_grads)
+    )
+    w_far = xor_swap(total(w_parts[2], w_hop).astype(BF16), "in", n_in, 2)
+    w_near = xor_swap(w_near, "in", n_in, 1)
     own = tokens.astype(F32)
-    mixed = (own + total(y_keep, y_near, y_far) + bias_out).astype(BF16)
-    w_near.append(near_in(w_next))
-    w_far = [far_in(w_keep[0], w_near[0])]
-    w_near[1], second_grads = lax.optimization_barrier((w_near[1], second_grads))
-    w_far.append(far_in(w_keep[1], w_near[1]))
-    w_sum = total(w_keep, w_near, w_far)
+    mixed = (own + total(y_parts[0], y_near, y_far) + bias_out).astype(BF16)
+    w_far, w_near, in_part = lax.optimization_barrier((w_far, w_near, second_grads[: n_in * r_w]))
+    in_part = exchange_in(in_part.reshape(n_in, r_w, ff_in), t)
+    w_sum = total(w_parts[0], w_near, w_far)
 
     def placed(vector, axis):
         spread = jnp.expand_dims(vector, axis)
@@ -944,9 +919,7 @@
         first_grads = jnp.concatenate([by_owner(dot_tn(n1, da).astype(BF16)), vec_grads], axis=2)
     first_grads = lax.psum_scatter(first_grads, G_AXES, scatter_dimension=0, tiled=False)
 
-    last = [first_grads.reshape(n_in, r_w, -1), second_grads[: n_in * r_w].reshape(n_in, r_w, ff_in)]
-    last = exchange_in(jnp.concatenate(last, axis=2), t)
-    qkv_part, in_part = last[:, :, : 3 * cols + 128], last[:, :, 3 * cols + 128 :]
+    qkv_part = exchange_in(first_grads.reshape(n_in, r_w, 3 * cols + 128), t)
     in_part = in_part.reshape(n_in, r_w, n_dp, n_out, r_ff)
     grad_w_in = jnp.transpose(in_part, (1, 2, 0, 3, 4)).reshape(r_w, ff).astype(F32)
     grad_w_fc2 = second_grads[n_in * r_w : n_in * r_w + r_ff].astype(F32)

time: 332 us -> 319 us (0.961)
  waiting for transfers between devices: 126 us -> 113 us
  other arithmetic: 23.4 us -> 15.3 us
  starting transfers between devices: 37.2 us -> 42.9 us
    ppermute x30 -> x33, waiting for transfers between devices: 123 us -> 108 us  [xor_swap(): return lax.ppermute(value, axis, [(i, i ^ step) for i in range(size)])]
    ppermute x30 -> x33, starting transfers between devices: 35.8 us -> 41.1 us  [xor_swap(): return lax.ppermute(value, axis, [(i, i ^ step) for i in range(size)])]
    unnamed x78 -> x86, local copies, waits for them, and re-layouts: 1.56 us -> 5.03 us
  transfers between devices with their start and end apart: 36 -> 39, of which waited for: 15 -> 16; matrix products, arithmetic and copies ran while one was open for 10% -> 8% of each run, Pallas kernels for 32% -> 33%
where the time goes in v5:
time: 319 us; the launch traced here: 318 us
  waiting for transfers between devices  113 us (35%)
  Pallas kernels  106 us (33%)
  starting transfers between devices  42.9 us (13%)
  local copies, waits for them, and re-layouts  25.1 us (8%)
  other arithmetic  15.3 us (5%)
  between operations  14.7 us (5%)
    ppermute x33, waiting for transfers between devices, xor_swap(): return lax.ppermute(value, axis, [(i, i ^ step) for i in range(size)])  108 us
    ppermute x33, starting transfers between devices, xor_swap(): return lax.ppermute(value, axis, [(i, i ^ step) for i in range(size)])  41.1 us
    pallas_call x1, Pallas kernels, attend_backward(): pl.pallas_call(functools.partial(backward_kernel, block, ends.shape[0]),...  26.8 us
    pallas_call x1, Pallas kernels, attend_forward(): pl.pallas_call(functools.partial(forward_kernel, block, ends.shape[0]), i...  19.3 us
    pallas_call x1, Pallas kernels, feed(): pl.pallas_call(functools.partial(feed_kernel, layout), grid=(rows // TILE...  15 us
    pallas_call x1, Pallas kernels, feed_grads(): pl.pallas_call(functools.partial(feed_grads_kernel, layout), grid=(width...  10.7 us
    pallas_call x1, Pallas kernels, post(): pl.pallas_call(functools.partial(post_kernel, heads, block), grid_spec=pl...  10.3 us
    pallas_call x1, Pallas kernels, prep(): pl.pallas_call(functools.partial(prep_kernel, heads, block), grid_spec=pl...  7.99 us
  transfers between devices with their start and end apart: 39, of which 16 were waited for; matrix products, arithmetic and copies ran while one was open for 8% of the time, Pallas kernels for 33%

profile of v5, /device:TPU:0, one launch (start us, length us, event | category | flops | bytes accessed | tf_op | source)
XLA Modules:
  0.0 317.6 jit_solution(8719408946201956221)
XLA Ops:
  10.4 5.1 %collective-permute-start.2 = (bf16[32,1920]{1,0:T(8,128)(2,1)S(1)}, bf16[32,1920]{1,0:T(8,128)(2,1)S(1)}, u32[]{:S(2)}, u32[]{:S(2)}) collective-permute-start(bf16[32,1920]{1,0:T(8,128)(2,1)S(1)} %get-tuple-element.246), channel_id=1, source_target_pairs={{0,12},{4,8},{8,4},{12,0},{1,13},{5,9},{9,5},{13,1},{2,14},{6,10},... | collective-permute-start | bytes 368648 | tf_op jit(solution)/shard_map/ppermute | solution.py:40
  16.9 2.9 collective-permute-done.2
  19.8 8.2 %collective-permute-done.1 = bf16[32,1920]{1,0:T(8,128)(2,1)S(1)} collective-permute-done((bf16[32,1920]{1,0:T(8,128)(2,1)S(1)}, bf16[32,1920]{1,0:T(8,128)(2,1)S(1)}, u32[]{:S(2)}, u32[]{:S(2)}) %collective-permute-start.1) | collective-permute-done | bytes 122912 | tf_op jit(solution)/shard_map/ppermute | solution.py:40
  31.2 20.8 %collective-permute-done.5 = bf16[256,1024]{1,0:T(8,128)(2,1)} collective-permute-done((bf16[256,1024]{1,0:T(8,128)(2,1)S(1)}, bf16[256,1024]{1,0:T(8,128)(2,1)}, u32[]{:S(2)}, u32[]{:S(2)}) %collective-permute-start.5) | collective-permute-done | bytes 524320 | tf_op jit(solution)/shard_map/ppermute | solution.py:40
  52.0 3.8 %collective-permute-done.4 = bf16[256,1024]{1,0:T(8,128)(2,1)S(1)} collective-permute-done((bf16[256,1024]{1,0:T(8,128)(2,1)S(1)}, bf16[256,1024]{1,0:T(8,128)(2,1)S(1)}, u32[]{:S(2)}, u32[]{:S(2)}) %collective-permute-start.4) | collective-permute-done | bytes 524320 | tf_op jit(solution)/shard_map/ppermute | solution.py:40
  63.5 3.1 fusion.11
  66.6 2.9 pad_maximum_fusion.x_ref
  74.1 8.0 %shard_map.246 = (bf16[1024,1024]{1,0:T(8,128)(2,1)}, bf16[1024,1024]{1,0:T(8,128)(2,1)}, bf16[1536,128]{1,0:T(8,128)(2,1)}, bf16[1536,128]{1,0:T(8,128)(2,1)}, ...) custom-call(s32[1]{0:T(128)} %bitcast.z_ref, bf16[1024,1024]{1,0:T(8,128)(2,1)} %pad_maximum_fusion.x_ref, ...), custom_call_target="tpu_custom_call" | custom-call | flops 1610612736 | bytes 12582912 | tf_op jit(solution)/shard_map/pallas_call | solution.py:126
  84.8 9.5 %collective-permute-done.8.refs_2_ = bf16[1536,128]{1,0:T(8,128)(2,1)S(1)} collective-permute-done((bf16[1536,128]{1,0:T(8,128)(2,1)}, bf16[1536,128]{1,0:T(8,128)(2,1)S(1)}, u32[]{:S(2)}, u32[]{:S(2)}) %collective-permute-start.8) | collective-permute-done | bytes 393248 | tf_op jit(solution)/shard_map/ppermute | solution.py:40
  94.3 7.6 %collective-permute-done.9.refs_3_ = bf16[1536,128]{1,0:T(8,128)(2,1)} collective-permute-done((bf16[1536,128]{1,0:T(8,128)(2,1)}, bf16[1536,128]{1,0:T(8,128)(2,1)}, u32[]{:S(2)}, u32[]{:S(2)}) %collective-permute-start.9) | collective-permute-done | bytes 393248 | tf_op jit(solution)/shard_map/ppermute | solution.py:40
  107.3 19.3 %shard_map.247 = (bf16[512,128]{1,0:T(8,128)(2,1)}, bf16[512,128]{1,0:T(8,128)(2,1)}, bf16[512,128]{1,0:T(8,128)(2,1)}, bf16[512,128]{1,0:T(8,128)(2,1)}, f32[64,4096]{1,0:T(8,128)}, /*index=5*/f32[1,4096]{1,0:T(1,128)}) custom-call(s32[64]{0:T(128)} %fusion.18.source_ref, s32[64]{0:T(128)} %copy-done.28, s32[4]{0:T(128)} %bitcast.126, ...), custom_call_target="tpu_custom_call" | custom-call | flops 42949672960 | bytes 3145728 | tf_op jit(solution)/shard_map/pallas_call | solution.py:660
  131.2 4.4 %shard_map.249 = (bf16[512,128]{1,0:T(8,128)(2,1)}, bf16[512,128]{1,0:T(8,128)(2,1)}, bf16[512,128]{1,0:T(8,128)(2,1)}, bf16[512,128]{1,0:T(8,128)(2,1)}) custom-call(s32[1]{0:T(128)} %bitcast.z_ref, bf16[1024,1024]{1,0:T(8,128)(2,1)} %copy-done.1, bf16[256,1024]{1,0:T(8,128)(2,1)} %reshape.284.wo_ref), custom_call_target="tpu_custom_call" | custom-call | flops 536870912 | bytes 4194304 | tf_op jit(solution)/shard_map/pallas_call | solution.py:318
  139.8 15.0 %shard_map.248 = (bf16[1024,1024]{1,0:T(8,128)(2,1)}, bf16[1024,1024]{1,0:T(8,128)(2,1)}, f32[1024,1024]{1,0:T(8,128)}, f32[1024,1024]{1,0:T(8,128)}, f32[8,1024]{1,0:T(8,128)}, /*index=5*/f32[8,1024]{1,0:T(8,128)}) custom-call(bf16[1024,1024]{1,0:T(8,128)(2,1)} %pad_maximum_fusion.x_ref, bf16[1024,1024]{1,0:T(8,128)(2,1)} %get-tuple-element.134.n2_ref, ...), custom_call_target="tpu_custom_call" | custom-call | flops 8589934592 | bytes 25165824 | tf_op jit(solution)/shard_map/pallas_call | solution.py:205
  155.7 5.9 %shard_map.250 = (bf16[1024,256]{1,0:T(8,128)(2,1)}, bf16[256,1024]{1,0:T(8,128)(2,1)}, bf16[256,1024]{1,0:T(8,128)(2,1)}, bf16[256,1024]{1,0:T(8,128)(2,1)}, bf16[256,1024]{1,0:T(8,128)(2,1)}) custom-call(s32[1]{0:T(128)} %bitcast.z_ref, f32[1024,1024]{1,0:T(8,128)} %get-tuple-element.164.y_ref, bf16[256,1024]{1,0:T(8,128)(2,1)} %reshape.284.wo_ref, ...), custom_call_target="tpu_custom_call" | custom-call | flops 536870912 | bytes 8388608 | tf_op jit(solution)/shard_map/pallas_call | solution.py:353
  161.5 10.7 %shard_map.251 = bf16[8,288,1024]{2,1,0:T(8,128)(2,1)} custom-call(bf16[1024,1024]{1,0:T(8,128)(2,1)} %get-tuple-element.134.n2_ref, bf16[1024,1024]{1,0:T(8,128)(2,1)} %get-tuple-element.157.du_ref, bf16[1024,1024]{1,0:T(8,128)(2,1)} %get-tuple-element.158.h_ref, bf16[1024,1024]{1,0:T(8,128)(2,1)} %copy-done.1, bf16[1024,256]{1,0:T(8,128)(2,1)} %get-tuple-element.169.o_ref), custom_call_target="tpu_custom_call" | custom-call | flops 4294967296 | bytes 14680064 | tf_op jit(solution)/shard_map/pallas_call | solution.py:262
  175.1 26.8 %shard_map.252 = (bf16[1536,128]{1,0:T(8,128)(2,1)}, bf16[1536,128]{1,0:T(8,128)(2,1)}, bf16[1536,128]{1,0:T(8,128)(2,1)}, bf16[1536,128]{1,0:T(8,128)(2,1)}) custom-call(s32[64]{0:T(128)} %fusion.18.source_ref, s32[64]{0:T(128)} %copy-done.28, s32[4]{0:T(128)} %bitcast.127, bf16[1536,128]{1,0:T(8,128)(2,1)} %get-tuple-element.142.refs_0_, ...), custom_call_target="tpu_custom_call" | custom-call | flops 42949672960 | bytes 6291456 | tf_op jit(solution)/shard_map/pallas_call | solution.py:688
  202.1 4.3 %collective-permute-start.23 = (bf16[256,1024]{1,0:T(8,128)(2,1)S(1)}, bf16[256,1024]{1,0:T(8,128)(2,1)S(1)}, u32[]{:S(2)}, u32[]{:S(2)}) collective-permute-start(bf16[256,1024]{1,0:T(8,128)(2,1)S(1)} %add_convert_fusion.1), channel_id=1, source_target_pairs={{0,8},{4,12},{8,0},{12,4},{1,9},{5,13},{9,1},{13,5},{2,10},{6,14},... | collective-permute-start | bytes 1572872 | tf_op jit(solution)/shard_map/ppermute | solution.py:40
  210.0 10.7 %collective-permute-done.21.refs_2_ = bf16[1536,128]{1,0:T(8,128)(2,1)S(1)} collective-permute-done((bf16[1536,128]{1,0:T(8,128)(2,1)}, bf16[1536,128]{1,0:T(8,128)(2,1)S(1)}, u32[]{:S(2)}, u32[]{:S(2)}) %collective-permute-start.21) | collective-permute-done | bytes 393248 | tf_op jit(solution)/shard_map/ppermute | solution.py:40
  220.7 12.7 %collective-permute-done.22.refs_3_ = bf16[1536,128]{1,0:T(8,128)(2,1)} collective-permute-done((bf16[1536,128]{1,0:T(8,128)(2,1)}, bf16[1536,128]{1,0:T(8,128)(2,1)}, u32[]{:S(2)}, u32[]{:S(2)}) %collective-permute-start.22) | collective-permute-done | bytes 393248 | tf_op jit(solution)/shard_map/ppermute | solution.py:40
  233.4 10.3 %shard_map.253 = (bf16[1024,768]{1,0:T(8,128)(2,1)}, f32[8,1024]{1,0:T(8,128)}, f32[8,768]{1,0:T(8,128)}, bf16[256,1024]{1,0:T(8,128)(2,1)}, bf16[256,1024]{1,0:...) custom-call(s32[1]{0:T(128)} %bitcast.z_ref, bf16[1024,1024]{1,0:T(8,128)(2,1)} %pad_maximum_fusion.x_ref, ...), custom_call_target="tpu_custom_call" | custom-call | flops 1610612736 | bytes 14680064 | tf_op jit(solution)/shard_map/pallas_call | solution.py:406
  248.3 5.9 %shard_map.254 = bf16[8,128,896]{2,1,0:T(8,128)(2,1)} custom-call(bf16[1024,1024]{1,0:T(8,128)(2,1)} %get-tuple-element.220.n1_ref, bf16[1024,768]{1,0:T(8,128)(2,1)} %get-tuple-element.221.da_ref, bf16[8,128,128]{2,1,0:T(8,128)(2,1)} %bitcast.112), custom_call_target="tpu_custom_call" | custom-call | flops 1610612736 | bytes 6291456 | tf_op jit(solution)/shard_map/pallas_call | solution.py:294
  254.2 6.1 %collective-permute-done.25 = bf16[256,1024]{1,0:T(8,128)(2,1)S(1)} collective-permute-done((bf16[256,1024]{1,0:T(8,128)(2,1)}, bf16[256,1024]{1,0:T(8,128)(2,1)S(1)}, u32[]{:S(2)}, u32[]{:S(2)}) %collective-permute-start.25) | collective-permute-done | bytes 524320 | tf_op jit(solution)/shard_map/ppermute | solution.py:40
  267.3 19.7 %collective-permute-done.26 = bf16[256,1024]{1,0:T(8,128)(2,1)S(1)} collective-permute-done((bf16[256,1024]{1,0:T(8,128)(2,1)S(1)}, bf16[256,1024]{1,0:T(8,128)(2,1)S(1)}, u32[]{:S(2)}, u32[]{:S(2)}) %collective-permute-start.26) | collective-permute-done | bytes 524320 | tf_op jit(solution)/shard_map/ppermute | solution.py:40
  288.0 4.8 %collective-permute-start.34 = (bf16[32,1024]{1,0:T(8,128)(2,1)S(1)}, bf16[32,1024]{1,0:T(8,128)(2,1)S(1)}, u32[]{:S(2)}, u32[]{:S(2)}) collective-permute-start(bf16[32,1024]{1,0:T(8,128)(2,1)S(1)} %get-tuple-element.254), channel_id=1, source_target_pairs={{0,12},{4,8},{8,4},{12,0},{1,13},{5,9},{9,5},{13,1},{2,14},{6,10},... | collective-permute-start | bytes 196616 | tf_op jit(solution)/shard_map/ppermute | solution.py:40
  (267 shorter events, 74.4 us)
Async XLA Ops:
  7.3 51.1 %all-gather.5.cloned.1.call-start = ((), (), s32[]{:S(2)}) async-start(), calls=%async_computation.4 | async-start | bytes 2654208 | tf_op jit(solution)/shard_map/all_gather | solution.py:800
  29.0 110.7 %all-gather.7.cloned.1.call-start = ((), (), s32[]{:S(2)}) async-start(), calls=%async_computation.5 | async-start | bytes 4718592 | tf_op jit(solution)/shard_map/all_gather | solution.py:842
  29.7 22.3 %collective-permute-start.5 = (bf16[256,1024]{1,0:T(8,128)(2,1)S(1)}, bf16[256,1024]{1,0:T(8,128)(2,1)}, u32[]{:S(2)}, u32[]{:S(2)}) collective-permute-start(bf16[256,1024]{1,0:T(8,128)(2,1)S(1)} %copy-done), channel_id=1, source_target_pairs={{0,4},{4,0},{8,12},{12,8},{1,5},{5,1},{9,13},{13,9},{2,6},{6,2},{1... | collective-permute-start | bytes 1572872 | tf_op jit(solution)/shard_map/ppermute | solution.py:40
  31.1 24.7 %collective-permute-start.4 = (bf16[256,1024]{1,0:T(8,128)(2,1)S(1)}, bf16[256,1024]{1,0:T(8,128)(2,1)S(1)}, u32[]{:S(2)}, u32[]{:S(2)}) collective-permute-start(bf16[256,1024]{1,0:T(8,128)(2,1)S(1)} %copy-done), channel_id=1, source_target_pairs={{0,8},{4,12},{8,0},{12,4},{1,9},{5,13},{9,1},{13,5},{2,10},{6,14},... | collective-permute-start | bytes 1572872 | tf_op jit(solution)/shard_map/ppermute | solution.py:40
  69.6 32.4 %collective-permute-start.11 = (bf16[256,1024]{1,0:T(8,128)(2,1)S(1)}, bf16[256,1024]{1,0:T(8,128)(2,1)S(1)}, u32[]{:S(2)}, u32[]{:S(2)}) collective-permute-start(bf16[256,1024]{1,0:T(8,128)(2,1)S(1)} %copy-done.2), channel_id=1, source_target_pairs={{0,4},{4,0},{8,12},{12,8},{1,5},{5,1},{9,13},{13,9},{2,6},{6,2},{1... | collective-permute-start | bytes 1572872 | tf_op jit(solution)/shard_map/ppermute | solution.py:40
  71.1 30.9 %collective-permute-start.10 = (bf16[256,1024]{1,0:T(8,128)(2,1)S(1)}, bf16[256,1024]{1,0:T(8,128)(2,1)}, u32[]{:S(2)}, u32[]{:S(2)}) collective-permute-start(bf16[256,1024]{1,0:T(8,128)(2,1)S(1)} %copy-done.2), channel_id=1, source_target_pairs={{0,8},{4,12},{8,0},{12,4},{1,9},{5,13},{9,1},{13,5},{2,10},{6,14},... | collective-permute-start | bytes 1572872 | tf_op jit(solution)/shard_map/ppermute | solution.py:40
  83.7 18.3 %collective-permute-start.9 = (bf16[1536,128]{1,0:T(8,128)(2,1)}, bf16[1536,128]{1,0:T(8,128)(2,1)}, u32[]{:S(2)}, u32[]{:S(2)}) collective-permute-start(bf16[1536,128]{1,0:T(8,128)(2,1)} %get-tuple-element.138), channel_id=1, source_target_pairs={{0,3},{1,2},{2,1},{3,0},{4,7},{5,6},{6,5},{7,4},{8,11},{9,10},{10,... | collective-permute-start | bytes 1179656 | tf_op jit(solution)/shard_map/ppermute | solution.py:40
  102.0 143.8 %reduce-scatter.3.cloned.1.call-start = ((), (), s32[]{:S(2)}) async-start(), calls=%async_computation.2 | async-start | bytes 5308416 | tf_op jit(solution)/shard_map/reduce_scatter | solution.py:871
  106.8 21.0 %collective-permute-start.12 = (bf16[256,1024]{1,0:T(8,128)(2,1)}, bf16[256,1024]{1,0:T(8,128)(2,1)S(1)}, u32[]{:S(2)}, u32[]{:S(2)}) collective-permute-start(bf16[256,1024]{1,0:T(8,128)(2,1)} %collective-permute-done.10), channel_id=1, source_target_pairs={{0,4},{4,0},{8,12},{12,8},{1,5},{5,1},{9,13},{13,9},{2,6},{6,2},{1... | collective-permute-start | bytes 1572872 | tf_op jit(solution)/shard_map/ppermute | solution.py:40
  127.8 27.0 %collective-permute-start.16 = (bf16[512,128]{1,0:T(8,128)(2,1)}, bf16[512,128]{1,0:T(8,128)(2,1)S(1)}, u32[]{:S(2)}, u32[]{:S(2)}) collective-permute-start(bf16[512,128]{1,0:T(8,128)(2,1)} %get-tuple-element.160), channel_id=1, source_target_pairs={{0,1},{1,0},{2,3},{3,2},{4,5},{5,4},{6,7},{7,6},{8,9},{9,8},{10,11... | collective-permute-start | bytes 393224 | tf_op jit(solution)/shard_map/ppermute | solution.py:40
  127.9 27.0 %collective-permute-start.17 = (bf16[512,128]{1,0:T(8,128)(2,1)}, bf16[512,128]{1,0:T(8,128)(2,1)S(1)}, u32[]{:S(2)}, u32[]{:S(2)}) collective-permute-start(bf16[512,128]{1,0:T(8,128)(2,1)} %get-tuple-element.161), channel_id=1, source_target_pairs={{0,2},{1,3},{2,0},{3,1},{4,6},{5,7},{6,4},{7,5},{8,10},{9,11},{10,... | collective-permute-start | bytes 393224 | tf_op jit(solution)/shard_map/ppermute | solution.py:40
  129.3 25.7 %collective-permute-start.18 = (bf16[512,128]{1,0:T(8,128)(2,1)}, bf16[512,128]{1,0:T(8,128)(2,1)S(1)}, u32[]{:S(2)}, u32[]{:S(2)}) collective-permute-start(bf16[512,128]{1,0:T(8,128)(2,1)} %get-tuple-element.162), channel_id=1, source_target_pairs={{0,3},{1,2},{2,1},{3,0},{4,7},{5,6},{6,5},{7,4},{8,11},{9,10},{10,... | collective-permute-start | bytes 393224 | tf_op jit(solution)/shard_map/ppermute | solution.py:40
  135.6 36.7 %collective-permute-start.13 = (bf16[512,128]{1,0:T(8,128)(2,1)}, bf16[512,128]{1,0:T(8,128)(2,1)S(1)}, u32[]{:S(2)}, u32[]{:S(2)}) collective-permute-start(bf16[512,128]{1,0:T(8,128)(2,1)} %get-tuple-element.154), channel_id=1, source_target_pairs={{0,1},{1,0},{2,3},{3,2},{4,5},{5,4},{6,7},{7,6},{8,9},{9,8},{10,11... | collective-permute-start | bytes 393224 | tf_op jit(solution)/shard_map/ppermute | solution.py:40
  135.9 36.4 %collective-permute-start.14 = (bf16[512,128]{1,0:T(8,128)(2,1)}, bf16[512,128]{1,0:T(8,128)(2,1)S(1)}, u32[]{:S(2)}, u32[]{:S(2)}) collective-permute-start(bf16[512,128]{1,0:T(8,128)(2,1)} %get-tuple-element.155), channel_id=1, source_target_pairs={{0,2},{1,3},{2,0},{3,1},{4,6},{5,7},{6,4},{7,5},{8,10},{9,11},{10,... | collective-permute-start | bytes 393224 | tf_op jit(solution)/shard_map/ppermute | solution.py:40
  154.9 17.4 %collective-permute-start.15 = (bf16[512,128]{1,0:T(8,128)(2,1)S(1)}, bf16[512,128]{1,0:T(8,128)(2,1)S(1)}, u32[]{:S(2)}, u32[]{:S(2)}) collective-permute-start(bf16[512,128]{1,0:T(8,128)(2,1)S(1)} %copy-done.36), channel_id=1, source_target_pairs={{0,3},{1,2},{2,1},{3,0},{4,7},{5,6},{6,5},{7,4},{8,11},{9,10},{10,... | collective-permute-start | bytes 393224 | tf_op jit(solution)/shard_map/ppermute | solution.py:40
  173.0 125.7 %reduce-scatter.5.cloned.1.call-start = ((), (), s32[]{:S(2)}) async-start(), calls=%async_computation.3 | async-start | bytes 2064384 | tf_op jit(solution)/shard_map/reduce_scatter | solution.py:920
  173.5 28.4 %collective-permute-start.19 = (bf16[256,1024]{1,0:T(8,128)(2,1)S(1)}, bf16[256,1024]{1,0:T(8,128)(2,1)S(1)}, u32[]{:S(2)}, u32[]{:S(2)}) collective-permute-start(bf16[256,1024]{1,0:T(8,128)(2,1)S(1)} %copy-done.30), channel_id=1, source_target_pairs={{0,4},{4,0},{8,12},{12,8},{1,5},{5,1},{9,13},{13,9},{2,6},{6,2},{1... | collective-permute-start | bytes 1572872 | tf_op jit(solution)/shard_map/ppermute | solution.py:40
  202.1 31.3 %collective-permute-start.23 = (bf16[256,1024]{1,0:T(8,128)(2,1)S(1)}, bf16[256,1024]{1,0:T(8,128)(2,1)S(1)}, u32[]{:S(2)}, u32[]{:S(2)}) collective-permute-start(bf16[256,1024]{1,0:T(8,128)(2,1)S(1)} %add_convert_fusion.1), channel_id=1, source_target_pairs={{0,8},{4,12},{8,0},{12,4},{1,9},{5,13},{9,1},{13,5},{2,10},{6,14},... | collective-permute-start | bytes 1572872 | tf_op jit(solution)/shard_map/ppermute | solution.py:40
  206.4 27.0 %collective-permute-start.24 = (bf16[256,1024]{1,0:T(8,128)(2,1)}, bf16[256,1024]{1,0:T(8,128)(2,1)S(1)}, u32[]{:S(2)}, u32[]{:S(2)}) collective-permute-start(bf16[256,1024]{1,0:T(8,128)(2,1)} %get-tuple-element.194), channel_id=1, source_target_pairs={{0,4},{4,0},{8,12},{12,8},{1,5},{5,1},{9,13},{13,9},{2,6},{6,2},{1... | collective-permute-start | bytes 1572872 | tf_op jit(solution)/shard_map/ppermute | solution.py:40
  207.0 13.8 %collective-permute-start.21 = (bf16[1536,128]{1,0:T(8,128)(2,1)}, bf16[1536,128]{1,0:T(8,128)(2,1)S(1)}, u32[]{:S(2)}, u32[]{:S(2)}) collective-permute-start(bf16[1536,128]{1,0:T(8,128)(2,1)} %get-tuple-element.190), channel_id=1, source_target_pairs={{0,2},{1,3},{2,0},{3,1},{4,6},{5,7},{6,4},{7,5},{8,10},{9,11},{10,... | collective-permute-start | bytes 1179656 | tf_op jit(solution)/shard_map/ppermute | solution.py:40
  208.8 24.6 %collective-permute-start.22 = (bf16[1536,128]{1,0:T(8,128)(2,1)}, bf16[1536,128]{1,0:T(8,128)(2,1)}, u32[]{:S(2)}, u32[]{:S(2)}) collective-permute-start(bf16[1536,128]{1,0:T(8,128)(2,1)} %get-tuple-element.191), channel_id=1, source_target_pairs={{0,3},{1,2},{2,1},{3,0},{4,7},{5,6},{6,5},{7,4},{8,11},{9,10},{10,... | collective-permute-start | bytes 1179656 | tf_op jit(solution)/shard_map/ppermute | solution.py:40
  245.7 14.6 %collective-permute-start.25 = (bf16[256,1024]{1,0:T(8,128)(2,1)}, bf16[256,1024]{1,0:T(8,128)(2,1)S(1)}, u32[]{:S(2)}, u32[]{:S(2)}) collective-permute-start(bf16[256,1024]{1,0:T(8,128)(2,1)} %get-tuple-element.205), channel_id=1, source_target_pairs={{0,4},{4,0},{8,12},{12,8},{1,5},{5,1},{9,13},{13,9},{2,6},{6,2},{1... | collective-permute-start | bytes 1572872 | tf_op jit(solution)/shard_map/ppermute | solution.py:40
  260.5 26.5 %collective-permute-start.26 = (bf16[256,1024]{1,0:T(8,128)(2,1)S(1)}, bf16[256,1024]{1,0:T(8,128)(2,1)S(1)}, u32[]{:S(2)}, u32[]{:S(2)}) collective-permute-start(bf16[256,1024]{1,0:T(8,128)(2,1)S(1)} %add_convert_fusion), channel_id=1, source_target_pairs={{0,8},{4,12},{8,0},{12,4},{1,9},{5,13},{9,1},{13,5},{2,10},{6,14},... | collective-permute-start | bytes 1572872 | tf_op jit(solution)/shard_map/ppermute | solution.py:40
  263.0 25.0 %collective-permute-start.27 = (bf16[256,1024]{1,0:T(8,128)(2,1)}, bf16[256,1024]{1,0:T(8,128)(2,1)S(1)}, u32[]{:S(2)}, u32[]{:S(2)}) collective-permute-start(bf16[256,1024]{1,0:T(8,128)(2,1)} %get-tuple-element.216), channel_id=1, source_target_pairs={{0,4},{4,0},{8,12},{12,8},{1,5},{5,1},{9,13},{13,9},{2,6},{6,2},{1... | collective-permute-start | bytes 1572872 | tf_op jit(solution)/shard_map/ppermute | solution.py:40
  (54 other events, 536.4 us)
Sparse Core Ops, SparseCore 0:
  29.2 29.1 all-gather.4
  102.1 37.6 all-gather.6
  172.5 64.0 reduce-scatter.2
  254.3 38.7 reduce-scatter.4

commit v6 on v5

--- a/solution.py
+++ b/solution.py
@@ -889,8 +889,7 @@
     w_near = xor_swap(w_near, "in", n_in, 1)
     own = tokens.astype(F32)
     mixed = (own + total(y_parts[0], y_near, y_far) + bias_out).astype(BF16)
-    w_far, w_near, in_part = lax.optimization_barrier((w_far, w_near, second_grads[: n_in * r_w]))
-    in_part = exchange_in(in_part.reshape(n_in, r_w, ff_in), t)
+    in_part = exchange_in(second_grads[: n_in * r_w].reshape(n_in, r_w, ff_in), t)
     w_sum = total(w_parts[0], w_near, w_far)
 
     def placed(vector, axis):

time: 319 us -> 319 us (level)
  Pallas kernels: 106 us -> 112 us
  starting transfers between devices: 42.9 us -> 38.7 us
    ppermute x33, starting transfers between devices: 41.1 us -> 37.1 us  [xor_swap(): return lax.ppermute(value, axis, [(i, i ^ step) for i in range(size)])]
    ppermute x33, waiting for transfers between devices: 108 us -> 104 us  [xor_swap(): return lax.ppermute(value, axis, [(i, i ^ step) for i in range(size)])]
    pallas_call x1, Pallas kernels: 19.3 us -> 22.7 us  [attend_forward(): pl.pallas_call(functools.partial(forward_kernel, block, ends.shape[0]), i...]
    reduce_scatter x1, waiting for transfers between devices: 0.02 us -> 3.38 us  [body(): lax.psum_scatter(first_grads, G_AXES, scatter_dimension=0, tiled=False)]
  transfers between devices with their start and end apart: 39 -> 39, of which waited for: 16 -> 14; matrix products, arithmetic and copies ran while one was open for 8% -> 9% of each run, Pallas kernels for 33% -> 35%
where the time goes in v6:
time: 319 us; the launch traced here: 318 us
  Pallas kernels  112 us (35%)
  waiting for transfers between devices  110 us (34%)
  starting transfers between devices  38.7 us (12%)
  local copies, waits for them, and re-layouts  25.7 us (8%)
  other arithmetic  17.3 us (5%)
  between operations  14.7 us (5%)
    ppermute x33, waiting for transfers between devices, xor_swap(): return lax.ppermute(value, axis, [(i, i ^ step) for i in range(size)])  104 us
    ppermute x33, starting transfers between devices, xor_swap(): return lax.ppermute(value, axis, [(i, i ^ step) for i in range(size)])  37.1 us
    pallas_call x1, Pallas kernels, attend_backward(): pl.pallas_call(functools.partial(backward_kernel, block, ends.shape[0]),...  28.7 us
    pallas_call x1, Pallas kernels, attend_forward(): pl.pallas_call(functools.partial(forward_kernel, block, ends.shape[0]), i...  22.7 us
    pallas_call x1, Pallas kernels, feed(): pl.pallas_call(functools.partial(feed_kernel, layout), grid=(rows // TILE...  15.2 us
    pallas_call x1, Pallas kernels, feed_grads(): pl.pallas_call(functools.partial(feed_grads_kernel, layout), grid=(width...  10.8 us
    pallas_call x1, Pallas kernels, post(): pl.pallas_call(functools.partial(post_kernel, heads, block), grid_spec=pl...  10.2 us
    pallas_call x1, Pallas kernels, prep(): pl.pallas_call(functools.partial(prep_kernel, heads, block), grid_spec=pl...  7.97 us
  transfers between devices with their start and end apart: 39, of which 14 were waited for; matrix products, arithmetic and copies ran while one was open for 9% of the time, Pallas kernels for 35%

profile of v6, /device:TPU:0, one launch (start us, length us, event | category | flops | bytes accessed | tf_op | source)
XLA Modules:
  0.0 318.3 jit_solution(2412483754539581258)
XLA Ops:
  10.4 5.1 %collective-permute-start.2 = (bf16[32,1920]{1,0:T(8,128)(2,1)S(1)}, bf16[32,1920]{1,0:T(8,128)(2,1)S(1)}, u32[]{:S(2)}, u32[]{:S(2)}) collective-permute-start(bf16[32,1920]{1,0:T(8,128)(2,1)S(1)} %get-tuple-element.240), channel_id=1, source_target_pairs={{0,12},{4,8},{8,4},{12,0},{1,13},{5,9},{9,5},{13,1},{2,14},{6,10},... | collective-permute-start | bytes 368648 | tf_op jit(solution)/shard_map/ppermute | solution.py:40
  19.8 8.2 %collective-permute-done.1 = bf16[32,1920]{1,0:T(8,128)(2,1)S(1)} collective-permute-done((bf16[32,1920]{1,0:T(8,128)(2,1)S(1)}, bf16[32,1920]{1,0:T(8,128)(2,1)S(1)}, u32[]{:S(2)}, u32[]{:S(2)}) %collective-permute-start.1) | collective-permute-done | bytes 122912 | tf_op jit(solution)/shard_map/ppermute | solution.py:40
  31.2 20.7 %collective-permute-done.5 = bf16[256,1024]{1,0:T(8,128)(2,1)S(1)} collective-permute-done((bf16[256,1024]{1,0:T(8,128)(2,1)S(1)}, bf16[256,1024]{1,0:T(8,128)(2,1)S(1)}, u32[]{:S(2)}, u32[]{:S(2)}) %collective-permute-start.5) | collective-permute-done | bytes 524320 | tf_op jit(solution)/shard_map/ppermute | solution.py:40
  51.9 3.9 %collective-permute-done.4 = bf16[256,1024]{1,0:T(8,128)(2,1)S(1)} collective-permute-done((bf16[256,1024]{1,0:T(8,128)(2,1)S(1)}, bf16[256,1024]{1,0:T(8,128)(2,1)S(1)}, u32[]{:S(2)}, u32[]{:S(2)}) %collective-permute-start.4) | collective-permute-done | bytes 524320 | tf_op jit(solution)/shard_map/ppermute | solution.py:40
  63.4 3.2 fusion.11
  74.0 8.0 %shard_map.246 = (bf16[1024,1024]{1,0:T(8,128)(2,1)}, bf16[1024,1024]{1,0:T(8,128)(2,1)}, bf16[1536,128]{1,0:T(8,128)(2,1)}, bf16[1536,128]{1,0:T(8,128)(2,1)}, ...) custom-call(s32[1]{0:T(128)} %bitcast.z_ref, bf16[1024,1024]{1,0:T(8,128)(2,1)} %pad_maximum_fusion.x_ref, ...), custom_call_target="tpu_custom_call" | custom-call | flops 1610612736 | bytes 12582912 | tf_op jit(solution)/shard_map/pallas_call | solution.py:126
  84.7 9.5 %collective-permute-done.8.refs_2_ = bf16[1536,128]{1,0:T(8,128)(2,1)S(1)} collective-permute-done((bf16[1536,128]{1,0:T(8,128)(2,1)}, bf16[1536,128]{1,0:T(8,128)(2,1)S(1)}, u32[]{:S(2)}, u32[]{:S(2)}) %collective-permute-start.8) | collective-permute-done | bytes 393248 | tf_op jit(solution)/shard_map/ppermute | solution.py:40
  94.2 7.6 %collective-permute-done.9.refs_3_ = bf16[1536,128]{1,0:T(8,128)(2,1)} collective-permute-done((bf16[1536,128]{1,0:T(8,128)(2,1)}, bf16[1536,128]{1,0:T(8,128)(2,1)}, u32[]{:S(2)}, u32[]{:S(2)}) %collective-permute-start.9) | collective-permute-done | bytes 393248 | tf_op jit(solution)/shard_map/ppermute | solution.py:40
  107.2 22.7 %shard_map.247 = (bf16[512,128]{1,0:T(8,128)(2,1)}, bf16[512,128]{1,0:T(8,128)(2,1)}, bf16[512,128]{1,0:T(8,128)(2,1)}, bf16[512,128]{1,0:T(8,128)(2,1)}, f32[64,4096]{1,0:T(8,128)}, /*index=5*/f32[1,4096]{1,0:T(1,128)}) custom-call(s32[64]{0:T(128)} %fusion.18.source_ref, s32[64]{0:T(128)} %copy-done.32, s32[4]{0:T(128)} %bitcast.126, ...), custom_call_target="tpu_custom_call" | custom-call | flops 42949672960 | bytes 3145728 | tf_op jit(solution)/shard_map/pallas_call | solution.py:660
  134.4 4.4 %shard_map.249 = (bf16[512,128]{1,0:T(8,128)(2,1)}, bf16[512,128]{1,0:T(8,128)(2,1)}, bf16[512,128]{1,0:T(8,128)(2,1)}, bf16[512,128]{1,0:T(8,128)(2,1)}) custom-call(s32[1]{0:T(128)} %bitcast.z_ref, bf16[1024,1024]{1,0:T(8,128)(2,1)} %copy-done.1, bf16[256,1024]{1,0:T(8,128)(2,1)} %reshape.284.wo_ref), custom_call_target="tpu_custom_call" | custom-call | flops 536870912 | bytes 4194304 | tf_op jit(solution)/shard_map/pallas_call | solution.py:318
  140.6 15.2 %shard_map.248 = (bf16[1024,1024]{1,0:T(8,128)(2,1)}, bf16[1024,1024]{1,0:T(8,128)(2,1)}, f32[1024,1024]{1,0:T(8,128)}, f32[1024,1024]{1,0:T(8,128)}, f32[8,1024]{1,0:T(8,128)}, /*index=5*/f32[8,1024]{1,0:T(8,128)}) custom-call(bf16[1024,1024]{1,0:T(8,128)(2,1)} %pad_maximum_fusion.x_ref, bf16[1024,1024]{1,0:T(8,128)(2,1)} %get-tuple-element.131.n2_ref, ...), custom_call_target="tpu_custom_call" | custom-call | flops 8589934592 | bytes 25165824 | tf_op jit(solution)/shard_map/pallas_call | solution.py:205
  156.7 5.9 %shard_map.250 = (bf16[1024,256]{1,0:T(8,128)(2,1)}, bf16[256,1024]{1,0:T(8,128)(2,1)}, bf16[256,1024]{1,0:T(8,128)(2,1)}, bf16[256,1024]{1,0:T(8,128)(2,1)}, bf16[256,1024]{1,0:T(8,128)(2,1)}) custom-call(s32[1]{0:T(128)} %bitcast.z_ref, f32[1024,1024]{1,0:T(8,128)} %get-tuple-element.161.y_ref, bf16[256,1024]{1,0:T(8,128)(2,1)} %reshape.284.wo_ref, ...), custom_call_target="tpu_custom_call" | custom-call | flops 536870912 | bytes 8388608 | tf_op jit(solution)/shard_map/pallas_call | solution.py:353
  162.5 10.8 %shard_map.251 = bf16[8,288,1024]{2,1,0:T(8,128)(2,1)} custom-call(bf16[1024,1024]{1,0:T(8,128)(2,1)} %get-tuple-element.131.n2_ref, bf16[1024,1024]{1,0:T(8,128)(2,1)} %get-tuple-element.154.du_ref, bf16[1024,1024]{1,0:T(8,128)(2,1)} %get-tuple-element.155.h_ref, bf16[1024,1024]{1,0:T(8,128)(2,1)} %copy-done.1, bf16[1024,256]{1,0:T(8,128)(2,1)} %get-tuple-element.166.o_ref), custom_call_target="tpu_custom_call" | custom-call | flops 4294967296 | bytes 14680064 | tf_op jit(solution)/shard_map/pallas_call | solution.py:262
  176.0 28.7 %shard_map.252 = (bf16[1536,128]{1,0:T(8,128)(2,1)}, bf16[1536,128]{1,0:T(8,128)(2,1)}, bf16[1536,128]{1,0:T(8,128)(2,1)}, bf16[1536,128]{1,0:T(8,128)(2,1)}) custom-call(s32[64]{0:T(128)} %fusion.18.source_ref, s32[64]{0:T(128)} %copy-done.32, s32[4]{0:T(128)} %bitcast.127, bf16[1536,128]{1,0:T(8,128)(2,1)} %get-tuple-element.139.refs_0_, ...), custom_call_target="tpu_custom_call" | custom-call | flops 42949672960 | bytes 6291456 | tf_op jit(solution)/shard_map/pallas_call | solution.py:688
  208.9 10.5 %collective-permute-done.21.refs_2_ = bf16[1536,128]{1,0:T(8,128)(2,1)S(1)} collective-permute-done((bf16[1536,128]{1,0:T(8,128)(2,1)}, bf16[1536,128]{1,0:T(8,128)(2,1)S(1)}, u32[]{:S(2)}, u32[]{:S(2)}) %collective-permute-start.21) | collective-permute-done | bytes 393248 | tf_op jit(solution)/shard_map/ppermute | solution.py:40
  219.4 14.4 %collective-permute-done.22.refs_3_ = bf16[1536,128]{1,0:T(8,128)(2,1)S(1)} collective-permute-done((bf16[1536,128]{1,0:T(8,128)(2,1)}, bf16[1536,128]{1,0:T(8,128)(2,1)S(1)}, u32[]{:S(2)}, u32[]{:S(2)}) %collective-permute-start.22) | collective-permute-done | bytes 393248 | tf_op jit(solution)/shard_map/ppermute | solution.py:40
  234.6 10.2 %shard_map.253 = (bf16[1024,768]{1,0:T(8,128)(2,1)}, f32[8,1024]{1,0:T(8,128)}, f32[8,768]{1,0:T(8,128)}, bf16[256,1024]{1,0:T(8,128)(2,1)}, bf16[256,1024]{1,0:...) custom-call(s32[1]{0:T(128)} %bitcast.z_ref, bf16[1024,1024]{1,0:T(8,128)(2,1)} %pad_maximum_fusion.x_ref, ...), custom_call_target="tpu_custom_call" | custom-call | flops 1610612736 | bytes 14680064 | tf_op jit(solution)/shard_map/pallas_call | solution.py:406
  249.4 5.9 %shard_map.254 = bf16[8,128,896]{2,1,0:T(8,128)(2,1)} custom-call(bf16[1024,1024]{1,0:T(8,128)(2,1)} %get-tuple-element.214.n1_ref, bf16[1024,768]{1,0:T(8,128)(2,1)} %get-tuple-element.215.da_ref, bf16[8,128,128]{2,1,0:T(8,128)(2,1)} %bitcast.112), custom_call_target="tpu_custom_call" | custom-call | flops 1610612736 | bytes 6291456 | tf_op jit(solution)/shard_map/pallas_call | solution.py:294
  255.4 5.8 %collective-permute-done.25 = bf16[256,1024]{1,0:T(8,128)(2,1)S(1)} collective-permute-done((bf16[256,1024]{1,0:T(8,128)(2,1)}, bf16[256,1024]{1,0:T(8,128)(2,1)S(1)}, u32[]{:S(2)}, u32[]{:S(2)}) %collective-permute-start.25) | collective-permute-done | bytes 524320 | tf_op jit(solution)/shard_map/ppermute | solution.py:40
  262.1 3.4 %collective-permute-start.34 = (bf16[32,1024]{1,0:T(8,128)(2,1)S(1)}, bf16[32,1024]{1,0:T(8,128)(2,1)S(1)}, u32[]{:S(2)}, u32[]{:S(2)}) collective-permute-start(bf16[32,1024]{1,0:T(8,128)(2,1)S(1)} %get-tuple-element.248), channel_id=1, source_target_pairs={{0,12},{4,8},{8,4},{12,0},{1,13},{5,9},{9,5},{13,1},{2,14},{6,10},... | collective-permute-start | bytes 196616 | tf_op jit(solution)/shard_map/ppermute | solution.py:40
  272.6 9.6 %collective-permute-done.32 = bf16[32,1024]{1,0:T(8,128)(2,1)S(1)} collective-permute-done((bf16[32,1024]{1,0:T(8,128)(2,1)S(1)}, bf16[32,1024]{1,0:T(8,128)(2,1)S(1)}, u32[]{:S(2)}, u32[]{:S(2)}) %collective-permute-start.32) | collective-permute-done | bytes 65568 | tf_op jit(solution)/shard_map/ppermute | solution.py:40
  284.4 9.7 %collective-permute-done.26 = bf16[256,1024]{1,0:T(8,128)(2,1)S(1)} collective-permute-done((bf16[256,1024]{1,0:T(8,128)(2,1)}, bf16[256,1024]{1,0:T(8,128)(2,1)S(1)}, u32[]{:S(2)}, u32[]{:S(2)}) %collective-permute-start.26) | collective-permute-done | bytes 524320 | tf_op jit(solution)/shard_map/ppermute | solution.py:40
  294.6 3.4 %reduce-scatter.5.cloned.1.call-done = bf16[1,128,896]{2,1,0:T(8,128)(2,1)} async-done(((bf16[8,128,896]{2,1,0:T(8,128)(2,1)}), bf16[1,128,896]{2,1,0:T(8,128)(2,1)}) %reduce-scatter.5.cloned.1.call-update) | async-done | bytes 229392 | tf_op jit(solution)/shard_map/reduce_scatter | solution.py:919
  298.9 4.7 %collective-permute-start.30 = (bf16[32,896]{1,0:T(8,128)(2,1)S(1)}, bf16[32,896]{1,0:T(8,128)(2,1)S(1)}, u32[]{:S(2)}, u32[]{:S(2)}) collective-permute-start(bf16[32,896]{1,0:T(8,128)(2,1)S(1)} %get-tuple-element.256), channel_id=1, source_target_pairs={{0,12},{4,8},{8,4},{12,0},{1,13},{5,9},{9,5},{13,1},{2,14},{6,10},... | collective-permute-start | bytes 172040 | tf_op jit(solution)/shard_map/ppermute | solution.py:40
  (275 shorter events, 72.4 us)
Async XLA Ops:
  7.3 51.1 %all-gather.5.cloned.1.call-start = ((), (), s32[]{:S(2)}) async-start(), calls=%async_computation.4 | async-start | bytes 2654208 | tf_op jit(solution)/shard_map/all_gather | solution.py:800
  29.0 111.6 %all-gather.7.cloned.1.call-start = ((), (), s32[]{:S(2)}) async-start(), calls=%async_computation.5 | async-start | bytes 4718592 | tf_op jit(solution)/shard_map/all_gather | solution.py:842
  29.7 22.2 %collective-permute-start.5 = (bf16[256,1024]{1,0:T(8,128)(2,1)S(1)}, bf16[256,1024]{1,0:T(8,128)(2,1)S(1)}, u32[]{:S(2)}, u32[]{:S(2)}) collective-permute-start(bf16[256,1024]{1,0:T(8,128)(2,1)S(1)} %copy-done), channel_id=1, source_target_pairs={{0,4},{4,0},{8,12},{12,8},{1,5},{5,1},{9,13},{13,9},{2,6},{6,2},{1... | collective-permute-start | bytes 1572872 | tf_op jit(solution)/shard_map/ppermute | solution.py:40
  31.1 24.7 %collective-permute-start.4 = (bf16[256,1024]{1,0:T(8,128)(2,1)S(1)}, bf16[256,1024]{1,0:T(8,128)(2,1)S(1)}, u32[]{:S(2)}, u32[]{:S(2)}) collective-permute-start(bf16[256,1024]{1,0:T(8,128)(2,1)S(1)} %copy-done), channel_id=1, source_target_pairs={{0,8},{4,12},{8,0},{12,4},{1,9},{5,13},{9,1},{13,5},{2,10},{6,14},... | collective-permute-start | bytes 1572872 | tf_op jit(solution)/shard_map/ppermute | solution.py:40
  69.5 32.3 %collective-permute-start.11 = (bf16[256,1024]{1,0:T(8,128)(2,1)S(1)}, bf16[256,1024]{1,0:T(8,128)(2,1)S(1)}, u32[]{:S(2)}, u32[]{:S(2)}) collective-permute-start(bf16[256,1024]{1,0:T(8,128)(2,1)S(1)} %copy-done.2), channel_id=1, source_target_pairs={{0,4},{4,0},{8,12},{12,8},{1,5},{5,1},{9,13},{13,9},{2,6},{6,2},{1... | collective-permute-start | bytes 1572872 | tf_op jit(solution)/shard_map/ppermute | solution.py:40
  71.0 30.9 %collective-permute-start.10 = (bf16[256,1024]{1,0:T(8,128)(2,1)S(1)}, bf16[256,1024]{1,0:T(8,128)(2,1)}, u32[]{:S(2)}, u32[]{:S(2)}) collective-permute-start(bf16[256,1024]{1,0:T(8,128)(2,1)S(1)} %copy-done.2), channel_id=1, source_target_pairs={{0,8},{4,12},{8,0},{12,4},{1,9},{5,13},{9,1},{13,5},{2,10},{6,14},... | collective-permute-start | bytes 1572872 | tf_op jit(solution)/shard_map/ppermute | solution.py:40
  83.5 18.3 %collective-permute-start.9 = (bf16[1536,128]{1,0:T(8,128)(2,1)}, bf16[1536,128]{1,0:T(8,128)(2,1)}, u32[]{:S(2)}, u32[]{:S(2)}) collective-permute-start(bf16[1536,128]{1,0:T(8,128)(2,1)} %get-tuple-element.135), channel_id=1, source_target_pairs={{0,3},{1,2},{2,1},{3,0},{4,7},{5,6},{6,5},{7,4},{8,11},{9,10},{10,... | collective-permute-start | bytes 1179656 | tf_op jit(solution)/shard_map/ppermute | solution.py:40
  101.9 145.1 %reduce-scatter.3.cloned.1.call-start = ((), (), s32[]{:S(2)}) async-start(), calls=%async_computation.2 | async-start | bytes 5308416 | tf_op jit(solution)/shard_map/reduce_scatter | solution.py:871
  106.7 24.4 %collective-permute-start.12 = (bf16[256,1024]{1,0:T(8,128)(2,1)}, bf16[256,1024]{1,0:T(8,128)(2,1)S(1)}, u32[]{:S(2)}, u32[]{:S(2)}) collective-permute-start(bf16[256,1024]{1,0:T(8,128)(2,1)} %collective-permute-done.10), channel_id=1, source_target_pairs={{0,4},{4,0},{8,12},{12,8},{1,5},{5,1},{9,13},{13,9},{2,6},{6,2},{1... | collective-permute-start | bytes 1572872 | tf_op jit(solution)/shard_map/ppermute | solution.py:40
  131.1 24.7 %collective-permute-start.16 = (bf16[512,128]{1,0:T(8,128)(2,1)}, bf16[512,128]{1,0:T(8,128)(2,1)S(1)}, u32[]{:S(2)}, u32[]{:S(2)}) collective-permute-start(bf16[512,128]{1,0:T(8,128)(2,1)} %get-tuple-element.157), channel_id=1, source_target_pairs={{0,1},{1,0},{2,3},{3,2},{4,5},{5,4},{6,7},{7,6},{8,9},{9,8},{10,11... | collective-permute-start | bytes 393224 | tf_op jit(solution)/shard_map/ppermute | solution.py:40
  131.2 24.8 %collective-permute-start.17 = (bf16[512,128]{1,0:T(8,128)(2,1)}, bf16[512,128]{1,0:T(8,128)(2,1)S(1)}, u32[]{:S(2)}, u32[]{:S(2)}) collective-permute-start(bf16[512,128]{1,0:T(8,128)(2,1)} %get-tuple-element.158), channel_id=1, source_target_pairs={{0,2},{1,3},{2,0},{3,1},{4,6},{5,7},{6,4},{7,5},{8,10},{9,11},{10,... | collective-permute-start | bytes 393224 | tf_op jit(solution)/shard_map/ppermute | solution.py:40
  132.6 23.4 %collective-permute-start.18 = (bf16[512,128]{1,0:T(8,128)(2,1)}, bf16[512,128]{1,0:T(8,128)(2,1)S(1)}, u32[]{:S(2)}, u32[]{:S(2)}) collective-permute-start(bf16[512,128]{1,0:T(8,128)(2,1)} %get-tuple-element.159), channel_id=1, source_target_pairs={{0,3},{1,2},{2,1},{3,0},{4,7},{5,6},{6,5},{7,4},{8,11},{9,10},{10,... | collective-permute-start | bytes 393224 | tf_op jit(solution)/shard_map/ppermute | solution.py:40
  138.8 34.5 %collective-permute-start.13 = (bf16[512,128]{1,0:T(8,128)(2,1)}, bf16[512,128]{1,0:T(8,128)(2,1)S(1)}, u32[]{:S(2)}, u32[]{:S(2)}) collective-permute-start(bf16[512,128]{1,0:T(8,128)(2,1)} %get-tuple-element.151), channel_id=1, source_target_pairs={{0,1},{1,0},{2,3},{3,2},{4,5},{5,4},{6,7},{7,6},{8,9},{9,8},{10,11... | collective-permute-start | bytes 393224 | tf_op jit(solution)/shard_map/ppermute | solution.py:40
  139.2 34.1 %collective-permute-start.14 = (bf16[512,128]{1,0:T(8,128)(2,1)}, bf16[512,128]{1,0:T(8,128)(2,1)S(1)}, u32[]{:S(2)}, u32[]{:S(2)}) collective-permute-start(bf16[512,128]{1,0:T(8,128)(2,1)} %get-tuple-element.152), channel_id=1, source_target_pairs={{0,2},{1,3},{2,0},{3,1},{4,6},{5,7},{6,4},{7,5},{8,10},{9,11},{10,... | collective-permute-start | bytes 393224 | tf_op jit(solution)/shard_map/ppermute | solution.py:40
  155.8 17.5 %collective-permute-start.15 = (bf16[512,128]{1,0:T(8,128)(2,1)S(1)}, bf16[512,128]{1,0:T(8,128)(2,1)S(1)}, u32[]{:S(2)}, u32[]{:S(2)}) collective-permute-start(bf16[512,128]{1,0:T(8,128)(2,1)S(1)} %copy-done.40), channel_id=1, source_target_pairs={{0,3},{1,2},{2,1},{3,0},{4,7},{5,6},{6,5},{7,4},{8,11},{9,10},{10,... | collective-permute-start | bytes 393224 | tf_op jit(solution)/shard_map/ppermute | solution.py:40
  174.1 123.8 %reduce-scatter.5.cloned.1.call-start = ((), (), s32[]{:S(2)}) async-start(), calls=%async_computation.3 | async-start | bytes 2064384 | tf_op jit(solution)/shard_map/reduce_scatter | solution.py:919
  174.5 30.1 %collective-permute-start.19 = (bf16[256,1024]{1,0:T(8,128)(2,1)S(1)}, bf16[256,1024]{1,0:T(8,128)(2,1)S(1)}, u32[]{:S(2)}, u32[]{:S(2)}) collective-permute-start(bf16[256,1024]{1,0:T(8,128)(2,1)S(1)} %copy-done.34), channel_id=1, source_target_pairs={{0,4},{4,0},{8,12},{12,8},{1,5},{5,1},{9,13},{13,9},{2,6},{6,2},{1... | collective-permute-start | bytes 1572872 | tf_op jit(solution)/shard_map/ppermute | solution.py:40
  204.8 29.1 %collective-permute-start.23 = (bf16[256,1024]{1,0:T(8,128)(2,1)S(1)}, bf16[256,1024]{1,0:T(8,128)(2,1)S(1)}, u32[]{:S(2)}, u32[]{:S(2)}) collective-permute-start(bf16[256,1024]{1,0:T(8,128)(2,1)S(1)} %add_convert_fusion.1), channel_id=1, source_target_pairs={{0,8},{4,12},{8,0},{12,4},{1,9},{5,13},{9,1},{13,5},{2,10},{6,14},... | collective-permute-start | bytes 1572872 | tf_op jit(solution)/shard_map/ppermute | solution.py:40
  205.5 28.4 %collective-permute-start.24 = (bf16[256,1024]{1,0:T(8,128)(2,1)}, bf16[256,1024]{1,0:T(8,128)(2,1)S(1)}, u32[]{:S(2)}, u32[]{:S(2)}) collective-permute-start(bf16[256,1024]{1,0:T(8,128)(2,1)} %get-tuple-element.191), channel_id=1, source_target_pairs={{0,4},{4,0},{8,12},{12,8},{1,5},{5,1},{9,13},{13,9},{2,6},{6,2},{1... | collective-permute-start | bytes 1572872 | tf_op jit(solution)/shard_map/ppermute | solution.py:40
  207.6 26.3 %collective-permute-start.22 = (bf16[1536,128]{1,0:T(8,128)(2,1)}, bf16[1536,128]{1,0:T(8,128)(2,1)S(1)}, u32[]{:S(2)}, u32[]{:S(2)}) collective-permute-start(bf16[1536,128]{1,0:T(8,128)(2,1)} %get-tuple-element.188), channel_id=1, source_target_pairs={{0,3},{1,2},{2,1},{3,0},{4,7},{5,6},{6,5},{7,4},{8,11},{9,10},{10,... | collective-permute-start | bytes 1179656 | tf_op jit(solution)/shard_map/ppermute | solution.py:40
  247.0 14.2 %collective-permute-start.25 = (bf16[256,1024]{1,0:T(8,128)(2,1)}, bf16[256,1024]{1,0:T(8,128)(2,1)S(1)}, u32[]{:S(2)}, u32[]{:S(2)}) collective-permute-start(bf16[256,1024]{1,0:T(8,128)(2,1)} %get-tuple-element.202), channel_id=1, source_target_pairs={{0,4},{4,0},{8,12},{12,8},{1,5},{5,1},{9,13},{13,9},{2,6},{6,2},{1... | collective-permute-start | bytes 1572872 | tf_op jit(solution)/shard_map/ppermute | solution.py:40
  265.5 16.7 %collective-permute-start.32 = (bf16[32,1024]{1,0:T(8,128)(2,1)S(1)}, bf16[32,1024]{1,0:T(8,128)(2,1)S(1)}, u32[]{:S(2)}, u32[]{:S(2)}) collective-permute-start(bf16[32,1024]{1,0:T(8,128)(2,1)S(1)} %get-tuple-element.250), channel_id=1, source_target_pairs={{0,4},{4,0},{8,12},{12,8},{1,5},{5,1},{9,13},{13,9},{2,6},{6,2},{1... | collective-permute-start | bytes 196616 | tf_op jit(solution)/shard_map/ppermute | solution.py:40
  266.5 27.5 %collective-permute-start.26 = (bf16[256,1024]{1,0:T(8,128)(2,1)}, bf16[256,1024]{1,0:T(8,128)(2,1)S(1)}, u32[]{:S(2)}, u32[]{:S(2)}) collective-permute-start(bf16[256,1024]{1,0:T(8,128)(2,1)} %get-tuple-element.211), channel_id=1, source_target_pairs={{0,4},{4,0},{8,12},{12,8},{1,5},{5,1},{9,13},{13,9},{2,6},{6,2},{1... | collective-permute-start | bytes 1572872 | tf_op jit(solution)/shard_map/ppermute | solution.py:40
  268.5 25.6 %collective-permute-start.27 = (bf16[256,1024]{1,0:T(8,128)(2,1)}, bf16[256,1024]{1,0:T(8,128)(2,1)S(1)}, u32[]{:S(2)}, u32[]{:S(2)}) collective-permute-start(bf16[256,1024]{1,0:T(8,128)(2,1)} %add_convert_fusion), channel_id=1, source_target_pairs={{0,8},{4,12},{8,0},{12,4},{1,9},{5,13},{9,1},{13,5},{2,10},{6,14},... | collective-permute-start | bytes 1572872 | tf_op jit(solution)/shard_map/ppermute | solution.py:40
  (58 other events, 550.1 us)
Sparse Core Ops, SparseCore 0:
  29.2 29.1 all-gather.4
  102.0 34.4 all-gather.6
  173.5 60.9 reduce-scatter.2
  255.4 42.4 reduce-scatter.4
